TPU v7x, 32 devices: a whole 2x2x4 slice. The times are simulated.
32 devices in a mesh: dp: 2 (over core), ctx: 4 (over y, x), ulysses: 4 (over z).
Axes of the slice: x: 2, y: 2, z: 4, core: 2. Of those that a mesh axis runs over, the one named last changes fastest.
Arguments:
- hidden_in: bfloat16 [2, 2048, 2048], P('dp', ('ctx', 'ulysses')), may hold values from -6 to 6
- cotangent: bfloat16 [2, 2048, 2048], P('dp', ('ctx', 'ulysses')), may hold values from -6 to 6
- log_decay: float32 [2, 8, 2048], P('dp', 'ulysses', 'ctx'), may hold values from -1 to 0, as said below
- w_query: bfloat16 [2048, 2048], P(('dp', 'ctx', 'ulysses')), may hold values from -0.125 to 0.125
- w_key: bfloat16 [2048, 2048], P(('dp', 'ctx', 'ulysses')), may hold values from -0.125 to 0.125
- w_value: bfloat16 [2048, 3456], P(('dp', 'ctx', 'ulysses')), may hold values from -0.125 to 0.125
- w_swish: bfloat16 [2048, 3456], P(('dp', 'ctx', 'ulysses')), may hold values from -0.125 to 0.125
- w_output: bfloat16 [3456, 2048], P(('dp', 'ctx', 'ulysses')), may hold values from -0.21875 to 0.21875
- w_gate: bfloat16 [2048, 3456], P(('dp', 'ctx', 'ulysses')), may hold values from -0.125 to 0.125
- w_up: bfloat16 [2048, 3456], P(('dp', 'ctx', 'ulysses')), may hold values from -0.125 to 0.125
- w_down: bfloat16 [3456, 2048], P(('dp', 'ctx', 'ulysses')), may hold values from -0.21875 to 0.21875
- gain_attn: bfloat16 [2048], P(('dp', 'ctx', 'ulysses')), may hold values from 0.5 to 1.5
- gain_ffn: bfloat16 [2048], P(('dp', 'ctx', 'ulysses')), may hold values from 0.5 to 1.5
Outputs:
- layer_out: float32 [2, 2048, 2048], P('dp', ('ctx', 'ulysses'))
- grad_input: float32 [2, 2048, 2048], P('dp', ('ctx', 'ulysses'))
- grad_query: float32 [2048, 2048], P(('dp', 'ctx', 'ulysses'))
- grad_key: float32 [2048, 2048], P(('dp', 'ctx', 'ulysses'))
- grad_value: float32 [2048, 3456], P(('dp', 'ctx', 'ulysses'))
- grad_swish: float32 [2048, 3456], P(('dp', 'ctx', 'ulysses'))
- grad_output: float32 [3456, 2048], P(('dp', 'ctx', 'ulysses'))
- grad_gate: float32 [2048, 3456], P(('dp', 'ctx', 'ulysses'))
- grad_up: float32 [2048, 3456], P(('dp', 'ctx', 'ulysses'))
- grad_down: float32 [3456, 2048], P(('dp', 'ctx', 'ulysses'))
- grad_gain_attn: float32 [2048], P(('dp', 'ctx', 'ulysses'))
- grad_gain_ffn: float32 [2048], P(('dp', 'ctx', 'ulysses'))
Inputs may be any that keep to these rules, and one draw needn't show every extreme that they name: log_decay is strictly negative.
All inputs are finite; a program needn't handle non-finite values.
Results may differ from a plain program's by a relative error of at most 0.015.
The roundings to bfloat16 on the way count: a program that leaves them out, or rounds other values in their place, can miss the bound.
Values may be sent and summed in bfloat16 or wider, within the bound.
A program may use at most 384 MiB of HBM per device.

v0:
```python
import math

import jax
import jax.numpy as jnp
from jax import lax
from jax.sharding import PartitionSpec as P

RETENTION_HEADS = 8
KEY_DIM = 256
VALUE_DIM = 432


EPSILON = 1e-06


def entering(value, axis, join, neutral, backward):
    count, mine = (lax.axis_size(axis), lax.axis_index(axis))
    pieces = jax.tree.map(lambda part: lax.all_gather(part, axis), value)
    if backward:
        pieces = jax.tree.map(lambda part: part[::-1], pieces)
        mine = count - 1 - mine
    subtotal = jax.tree.map(
        lambda part, zero: jnp.full_like(part, 0) + jnp.asarray(zero, part.dtype), value, neutral
    )

    def step(position, subtotal):
        longer = join(subtotal, jax.tree.map(lambda part: part[position], pieces))
        return jax.tree.map(lambda new, old: jnp.where(position < mine, new, old), longer, subtotal)

    return lax.fori_loop(0, count - 1, step, subtotal)


def normalize(values):
    inverse = lax.rsqrt(jnp.mean(values * values, axis=-1, keepdims=True) + EPSILON)
    return (values * inverse, inverse)


def norm_back(grad_normed, normed, inverse):
    return inverse * (grad_normed - normed * jnp.mean(grad_normed * normed, axis=-1, keepdims=True))


def swish_slope(values):
    sigma = jax.nn.sigmoid(values)
    return sigma * (1.0 + values * (1.0 - sigma))


def carry_forward(earlier, later):
    return (earlier[0] * later[0], later[0][:, None, None] * earlier[1] + later[1])


def carry_backward(earlier, later):
    return (earlier[0] * later[0], later[1] + later[0][:, None, None] * earlier[1])


def matmul(left, right):
    return jnp.dot(left, right, preferred_element_type=jnp.float32)


def local(
    hidden_in,
    cotangent,
    log_decay,
    w_query,
    w_key,
    w_value,
    w_swish,
    w_output,
    w_gate,
    w_up,
    w_down,
    gain_attn,
    gain_ffn,
):
    highest = lax.Precision.HIGHEST
    query_full, key_full, value_full, swish_full, output_full, gain_one = (
        lax.all_gather(w_query, ("dp", "ctx", "ulysses"), axis=0, tiled=True),
        lax.all_gather(w_key, ("dp", "ctx", "ulysses"), axis=0, tiled=True),
        lax.all_gather(w_value, ("dp", "ctx", "ulysses"), axis=0, tiled=True),
        lax.all_gather(w_swish, ("dp", "ctx", "ulysses"), axis=0, tiled=True),
        lax.all_gather(w_output, ("dp", "ctx", "ulysses"), axis=0, tiled=True),
        lax.all_gather(gain_attn, ("dp", "ctx", "ulysses"), axis=0, tiled=True),
    )
    inputs = hidden_in[0].astype(jnp.float32)
    tokens = inputs.shape[0]
    normed_one, inverse_one = normalize(inputs)
    scaled_one = (normed_one * gain_one.astype(jnp.float32)).astype(jnp.bfloat16)
    queries = (
        matmul(scaled_one, query_full)
        .astype(jnp.bfloat16)
        .reshape(tokens, RETENTION_HEADS, KEY_DIM)
    )
    keys_tok = (
        matmul(scaled_one, key_full).astype(jnp.bfloat16).reshape(tokens, RETENTION_HEADS, KEY_DIM)
    )
    values_tok = (
        matmul(scaled_one, value_full)
        .astype(jnp.bfloat16)
        .reshape(tokens, RETENTION_HEADS, VALUE_DIM)
    )
    swish_pre = matmul(scaled_one, swish_full)
    head_q, head_k, head_v = (
        lax.all_to_all(queries, "ulysses", split_axis=1, concat_axis=0, tiled=True),
        lax.all_to_all(keys_tok, "ulysses", split_axis=1, concat_axis=0, tiled=True),
        lax.all_to_all(values_tok, "ulysses", split_axis=1, concat_axis=0, tiled=True),
    )
    block = head_q.shape[0]
    scale = 1.0 / math.sqrt(KEY_DIM)
    cumulative = jnp.cumsum(log_decay[0], axis=1)
    later = lax.broadcasted_iota(jnp.int32, (block, block), 0) >= lax.broadcasted_iota(
        jnp.int32, (block, block), 1
    )
    gap = cumulative[:, :, None] - cumulative[:, None, :]
    mask = jnp.where(later[None], jnp.exp(jnp.minimum(gap, 0.0)), 0.0) * scale
    scores = jnp.einsum("thd,shd->hts", head_q, head_k, preferred_element_type=jnp.float32)
    weights = (scores * mask).astype(jnp.bfloat16)
    intra = jnp.einsum("hts,she->the", weights, head_v, preferred_element_type=jnp.float32)
    query_f = head_q.astype(jnp.float32)
    key_f = head_k.astype(jnp.float32)
    value_f = head_v.astype(jnp.float32)
    tail = jnp.exp(cumulative[:, -1:] - cumulative).T[:, :, None]
    reach = jnp.exp(cumulative).T[:, :, None]
    update = jnp.einsum("shd,she->hde", key_f * tail, value_f, precision=highest)
    block_decay = jnp.exp(cumulative[:, -1])
    identity = (jnp.ones_like(block_decay), jnp.zeros_like(update))
    _, state_in = entering((block_decay, update), "ctx", carry_forward, identity, False)
    retained = intra + scale * reach * jnp.einsum(
        "thd,hde->the", query_f, state_in, precision=highest
    )
    head_normed, head_inverse = normalize(retained)
    head_out = head_normed.astype(jnp.bfloat16)
    token_out = lax.all_to_all(
        head_out, "ulysses", split_axis=0, concat_axis=1, tiled=True
    ).reshape(tokens, RETENTION_HEADS * VALUE_DIM)
    token_out_f = token_out.astype(jnp.float32)
    swish_act = jax.nn.silu(swish_pre)
    gated = (swish_act * token_out_f).astype(jnp.bfloat16)
    residual = inputs + matmul(gated, output_full)
    gate_full, up_full, down_full, gain_two = (
        lax.all_gather(w_gate, ("dp", "ctx", "ulysses"), axis=0, tiled=True),
        lax.all_gather(w_up, ("dp", "ctx", "ulysses"), axis=0, tiled=True),
        lax.all_gather(w_down, ("dp", "ctx", "ulysses"), axis=0, tiled=True),
        lax.all_gather(gain_ffn, ("dp", "ctx", "ulysses"), axis=0, tiled=True),
    )
    normed_two, inverse_two = normalize(residual)
    scaled_two = (normed_two * gain_two.astype(jnp.float32)).astype(jnp.bfloat16)
    gate_pre = matmul(scaled_two, gate_full)
    up_pre = matmul(scaled_two, up_full)
    product = (jax.nn.silu(gate_pre) * up_pre).astype(jnp.bfloat16)
    layer_out = residual + matmul(product, down_full)
    grad_top = cotangent[0].astype(jnp.float32)
    grad_top_low = grad_top.astype(jnp.bfloat16)
    grad_product = matmul(grad_top_low, down_full.T)
    grad_down_term = matmul(product.T, grad_top_low)
    grad_gate_pre = (grad_product * up_pre * swish_slope(gate_pre)).astype(jnp.bfloat16)
    grad_up_pre = (grad_product * jax.nn.silu(gate_pre)).astype(jnp.bfloat16)
    grad_gate_term = matmul(scaled_two.T, grad_gate_pre)
    grad_up_term = matmul(scaled_two.T, grad_up_pre)
    grad_scaled_two = matmul(grad_gate_pre, gate_full.T) + matmul(grad_up_pre, up_full.T)
    grad_gain_two = jnp.sum(grad_scaled_two * normed_two, axis=0)
    grad_residual = grad_top + norm_back(
        grad_scaled_two * gain_two.astype(jnp.float32), normed_two, inverse_two
    )
    grad_gate, grad_up, grad_down, grad_gain_ffn = (
        lax.psum_scatter(grad_gate_term, ("dp", "ctx", "ulysses"), scatter_dimension=0, tiled=True),
        lax.psum_scatter(grad_up_term, ("dp", "ctx", "ulysses"), scatter_dimension=0, tiled=True),
        lax.psum_scatter(grad_down_term, ("dp", "ctx", "ulysses"), scatter_dimension=0, tiled=True),
        lax.psum_scatter(grad_gain_two, ("dp", "ctx", "ulysses"), scatter_dimension=0, tiled=True),
    )
    grad_y = grad_residual.astype(jnp.bfloat16)
    grad_output_term = matmul(gated.T, grad_y)
    grad_gated = matmul(grad_y, output_full.T)
    grad_swish_pre = (grad_gated * token_out_f * swish_slope(swish_pre)).astype(jnp.bfloat16)
    grad_token_out = (
        (grad_gated * swish_act).astype(jnp.bfloat16).reshape(tokens, RETENTION_HEADS, VALUE_DIM)
    )
    grad_swish_term = matmul(scaled_one.T, grad_swish_pre)
    grad_head_out = lax.all_to_all(
        grad_token_out, "ulysses", split_axis=1, concat_axis=0, tiled=True
    ).astype(jnp.float32)
    grad_retained = norm_back(grad_head_out, head_normed, head_inverse).astype(jnp.bfloat16)
    grad_retained_f = grad_retained.astype(jnp.float32)
    grad_weights = jnp.einsum(
        "the,she->hts", grad_retained, head_v, preferred_element_type=jnp.float32
    )
    grad_scores = (grad_weights * mask).astype(jnp.bfloat16)
    grad_state_in = scale * jnp.einsum(
        "thd,the->hde", query_f * reach, grad_retained_f, precision=highest
    )
    _, grad_update = entering((block_decay, grad_state_in), "ctx", carry_backward, identity, True)
    grad_head_q = jnp.einsum(
        "hts,shd->thd", grad_scores, head_k, preferred_element_type=jnp.float32
    ) + scale * reach * jnp.einsum("the,hde->thd", grad_retained_f, state_in, precision=highest)
    grad_head_k = jnp.einsum(
        "hts,thd->shd", grad_scores, head_q, preferred_element_type=jnp.float32
    ) + tail * jnp.einsum("she,hde->shd", value_f, grad_update, precision=highest)
    grad_head_v = jnp.einsum(
        "hts,the->she", weights, grad_retained, preferred_element_type=jnp.float32
    ) + tail * jnp.einsum("shd,hde->she", key_f, grad_update, precision=highest)
    grad_queries, grad_keys, grad_values = (
        lax.all_to_all(
            grad_head_q.astype(jnp.bfloat16), "ulysses", split_axis=0, concat_axis=1, tiled=True
        ),
        lax.all_to_all(
            grad_head_k.astype(jnp.bfloat16), "ulysses", split_axis=0, concat_axis=1, tiled=True
        ),
        lax.all_to_all(
            grad_head_v.astype(jnp.bfloat16), "ulysses", split_axis=0, concat_axis=1, tiled=True
        ),
    )
    grad_queries = grad_queries.reshape(tokens, RETENTION_HEADS * KEY_DIM)
    grad_keys = grad_keys.reshape(tokens, RETENTION_HEADS * KEY_DIM)
    grad_values = grad_values.reshape(tokens, RETENTION_HEADS * VALUE_DIM)
    grad_query_term = matmul(scaled_one.T, grad_queries)
    grad_key_term = matmul(scaled_one.T, grad_keys)
    grad_value_term = matmul(scaled_one.T, grad_values)
    grad_scaled_one = (
        matmul(grad_queries, query_full.T)
        + matmul(grad_keys, key_full.T)
        + matmul(grad_values, value_full.T)
        + matmul(grad_swish_pre, swish_full.T)
    )
    grad_gain_one = jnp.sum(grad_scaled_one * normed_one, axis=0)
    grad_input = grad_residual + norm_back(
        grad_scaled_one * gain_one.astype(jnp.float32), normed_one, inverse_one
    )
    grad_query, grad_key, grad_value, grad_swish, grad_output, grad_gain_attn = (
        lax.psum_scatter(
            grad_query_term, ("dp", "ctx", "ulysses"), scatter_dimension=0, tiled=True
        ),
        lax.psum_scatter(grad_key_term, ("dp", "ctx", "ulysses"), scatter_dimension=0, tiled=True),
        lax.psum_scatter(
            grad_value_term, ("dp", "ctx", "ulysses"), scatter_dimension=0, tiled=True
        ),
        lax.psum_scatter(
            grad_swish_term, ("dp", "ctx", "ulysses"), scatter_dimension=0, tiled=True
        ),
        lax.psum_scatter(
            grad_output_term, ("dp", "ctx", "ulysses"), scatter_dimension=0, tiled=True
        ),
        lax.psum_scatter(grad_gain_one, ("dp", "ctx", "ulysses"), scatter_dimension=0, tiled=True),
    )
    return (
        layer_out[None],
        grad_input[None],
        grad_query,
        grad_key,
        grad_value,
        grad_swish,
        grad_output,
        grad_gate,
        grad_up,
        grad_down,
        grad_gain_attn,
        grad_gain_ffn,
    )


def solution(mesh):
    placed = (
        P("dp", ("ctx", "ulysses"), None),
        P("dp", ("ctx", "ulysses"), None),
        P("dp", "ulysses", "ctx"),
        P(("dp", "ctx", "ulysses"), None),
        P(("dp", "ctx", "ulysses"), None),
        P(("dp", "ctx", "ulysses"), None),
        P(("dp", "ctx", "ulysses"), None),
        P(("dp", "ctx", "ulysses"), None),
        P(("dp", "ctx", "ulysses"), None),
        P(("dp", "ctx", "ulysses"), None),
        P(("dp", "ctx", "ulysses"), None),
        P(("dp", "ctx", "ulysses")),
        P(("dp", "ctx", "ulysses")),
    )
    return jax.shard_map(
        local,
        mesh=mesh,
        in_specs=placed,
        out_specs=(
            P("dp", ("ctx", "ulysses"), None),
            P("dp", ("ctx", "ulysses"), None),
            P(("dp", "ctx", "ulysses"), None),
            P(("dp", "ctx", "ulysses"), None),
            P(("dp", "ctx", "ulysses"), None),
            P(("dp", "ctx", "ulysses"), None),
            P(("dp", "ctx", "ulysses"), None),
            P(("dp", "ctx", "ulysses"), None),
            P(("dp", "ctx", "ulysses"), None),
            P(("dp", "ctx", "ulysses"), None),
            P(("dp", "ctx", "ulysses")),
            P(("dp", "ctx", "ulysses")),
        ),
        check_vma=False,
    )
```

profile of v0, /device:TPU:9, one launch (start us, length us, event | category | flops | bytes accessed | tf_op | source)
XLA Modules:
  0.0 3698.8 jit_solution(10345828626965850638)
XLA Ops:
  11.1 40.9 %all-reduce.10 = (bf16[2048]{0:T(1024)(128)(2,1)S(1)}, bf16[2048]{0:T(1024)(128)(2,1)S(1)}) all-reduce(bf16[2048]{0:T(1024)(128)(2,1)S(1)} %dynamic-update-slice, bf16[2048]{0:T(1024)(128)(2,1)S(1)} %dynamic-update-slice.2), channel_id=1, replica_groups=mesh['dp'=2,'ctx'=4,'ulysses'=4] {'dp','ctx','ulysses'}, use_global_device_ids=true, to_apply=%add | all-reduce | flops 4096 | bytes 16384
  53.2 37.2 %all-gather.22.cloned.1.call-done = bf16[2048,2048]{1,0:T(8,128)(2,1)} async-done(((bf16[64,2048]{1,0:T(8,128)(2,1)}), bf16[2048,2048]{1,0:T(8,128)(2,1)}) %all-gather.22.cloned.1.call-update) | async-done | bytes 8388624 | tf_op jit(solution)/shard_map/all_gather | solution.py:77
  99.6 102.6 %all-gather.18.cloned.1.call-done = bf16[2048,3456]{1,0:T(8,128)(2,1)} async-done(((bf16[64,3456]{1,0:T(8,128)(2,1)}), bf16[2048,3456]{1,0:T(8,128)(2,1)}) %all-gather.18.cloned.1.call-update) | async-done | bytes 14155792 | tf_op jit(solution)/shard_map/all_gather | solution.py:78
  216.8 21.6 all-to-all-done
  243.8 48.9 %all-gather.20.cloned.1.call-done = bf16[2048,2048]{1,0:T(8,128)(2,1)} async-done(((bf16[64,2048]{1,0:T(8,128)(2,1)}), bf16[2048,2048]{1,0:T(8,128)(2,1)}) %all-gather.20.cloned.1.call-update) | async-done | bytes 8388624 | tf_op jit(solution)/shard_map/all_gather | solution.py:76
  315.1 25.3 all-gather.28.cloned.1.call-done
  359.6 100.5 %all-gather.32.cloned.1.call-done = bf16[32,108,2048]{2,1,0:T(8,128)(2,1)} async-done(((bf16[1,108,2048]{2,1,0:T(8,128)(2,1)}), bf16[32,108,2048]{2,1,0:T(8,128)(2,1)}) %all-gather.32.cloned.1.call-update) | async-done | bytes 14155792 | tf_op jit(solution)/shard_map/all_gather | solution.py:80
  460.2 16.9 reshape.221
  477.1 89.4 %all-gather.34.cloned.1.call-done = bf16[32,108,2048]{2,1,0:T(8,128)(2,1)} async-done(((bf16[1,108,2048]{2,1,0:T(8,128)(2,1)}), bf16[32,108,2048]{2,1,0:T(8,128)(2,1)}) %all-gather.34.cloned.1.call-update) | async-done | bytes 14155792 | tf_op jit(solution)/shard_map/all_gather | solution.py:141
  566.4 16.9 reshape.223
  595.4 75.3 %all-gather.16.cloned.1.call-done = bf16[2048,3456]{1,0:T(8,128)(2,1)} async-done(((bf16[64,3456]{1,0:T(8,128)(2,1)}), bf16[2048,3456]{1,0:T(8,128)(2,1)}) %all-gather.16.cloned.1.call-update) | async-done | bytes 14155792 | tf_op jit(solution)/shard_map/all_gather | solution.py:79
  689.8 85.0 %all-gather.26.cloned.1.call-done = bf16[2048,3456]{1,0:T(8,128)(2,1)} async-done(((bf16[64,3456]{1,0:T(8,128)(2,1)}), bf16[2048,3456]{1,0:T(8,128)(2,1)}) %all-gather.26.cloned.1.call-update) | async-done | bytes 14155792 | tf_op jit(solution)/shard_map/all_gather | solution.py:140
  783.3 95.7 %all-gather.24.cloned.1.call-done = bf16[2048,3456]{1,0:T(8,128)(2,1)} async-done(((bf16[64,3456]{1,0:T(8,128)(2,1)}), bf16[2048,3456]{1,0:T(8,128)(2,1)}) %all-gather.24.cloned.1.call-update) | async-done | bytes 14155792 | tf_op jit(solution)/shard_map/all_gather | solution.py:139
  887.6 12.3 multiply_convert_fusion.4
  909.9 10.4 multiply_reduce_fusion.1
  920.7 12.4 multiply_convert_fusion.2
  935.3 25.0 all_to_all.117
  969.8 15.4 all_to_all.118
  995.3 11.4 fusion.65
  1008.0 11.2 fusion.79
  1020.4 11.5 fusion.78
  1053.5 30.5 all_to_all.119
  1098.9 54.9 %all_to_all.120 = bf16[512,2,432]{2,1,0:T(2,128)(2,1)S(1)} all-to-all(bf16[512,2,432]{2,1,0:T(2,128)(2,1)S(1)} %copy.151), channel_id=1, replica_groups=mesh['dp'=2,'ctx'=4,'ulysses'=4] {'ulysses'}, dimensions={0} | all-to-all | bytes 1769472 | tf_op jit(solution)/shard_map/all_to_all | solution.py:206
  1156.0 11.5 fusion.59
  1169.0 11.4 fusion.55
  1180.4 1004.9 %fusion = f32[112,2048]{1,0:T(8,128)} fusion(f32[3456,2048]{1,0:T(8,128)} %fusion.55), kind=kCustom, calls=%all-reduce-scatter | all-reduce-scatter fusion | flops 7340033 | bytes 29229056
  2190.3 12.4 fusion.49
  2202.7 992.2 %fusion.1 = f32[112,2048]{1,0:T(8,128)} fusion(f32[3456,2048]{1,0:T(8,128)} %fusion.49), kind=kCustom, calls=%all-reduce-scatter.1 | all-reduce-scatter fusion | flops 7340033 | bytes 29229056
  3216.1 38.4 %collective-permute-done.1 = f32[12,2048]{1,0:T(8,128)} collective-permute-done((f32[12,2048]{1,0:T(8,128)S(1)}, f32[12,2048]{1,0:T(8,128)}, u32[]{:S(2)}, u32[]{:S(2)}) %collective-permute-start.1) | collective-permute-done | bytes 98336
  3310.6 64.5 %all-reduce.9 = (f32[2048]{0:T(1024)S(1)}, f32[2048]{0:T(1024)S(1)}) all-reduce(f32[2048]{0:T(1024)S(1)} %get-tuple-element.265, f32[2048]{0:T(1024)S(1)} %copy-done.41), channel_id=13, replica_groups=mesh['dp'=2,'ctx'=4,'ulysses'=4] {'dp','ctx','ulysses'}, use_global_device_ids=true, to_apply=%region_21.22.clone | all-reduce | flops 4096 | bytes 32768
  3377.7 45.2 %reduce-scatter.13.cloned.1.call-done = f32[64,2048]{1,0:T(8,128)} async-done(((f32[2048,2048]{1,0:T(8,128)}), f32[64,2048]{1,0:T(8,128)}) %reduce-scatter.13.cloned.1.call-update) | async-done | bytes 524304 | tf_op jit(solution)/shard_map/reduce_scatter | solution.py:230
  3422.9 268.9 %reduce-scatter.15.cloned.1.call-done = f32[64,3456]{1,0:T(8,128)} async-done(((f32[2048,3456]{1,0:T(8,128)}), f32[64,3456]{1,0:T(8,128)}) %reduce-scatter.15.cloned.1.call-update) | async-done | bytes 884752 | tf_op jit(solution)/shard_map/reduce_scatter | solution.py:231
  (254 shorter events, 293.2 us)
Async XLA Ops:
  7.2 83.3 %copy-start = (bf16[1,128,2048]{2,1,0:T(8,128)(2,1)S(1)}, bf16[1,128,2048]{2,1,0:T(8,128)(2,1)}, u32[]{:S(2)}) copy-start(bf16[1,128,2048]{2,1,0:T(8,128)(2,1)} %param.17) | copy-start | bytes 1572868
  7.2 83.2 %all-gather.22.cloned.1.call-start = ((), (), s32[]{:S(2)}) async-start(), calls=%async_computation.17 | async-start | bytes 8650752 | tf_op jit(solution)/shard_map/all_gather | solution.py:77
  7.9 194.3 %all-gather.18.cloned.1.call-start = ((), (), s32[]{:S(2)}) async-start(), calls=%async_computation.15 | async-start | bytes 14598144 | tf_op jit(solution)/shard_map/all_gather | solution.py:78
  8.7 284.0 %all-gather.20.cloned.1.call-start = ((), (), s32[]{:S(2)}) async-start(), calls=%async_computation.16 | async-start | bytes 8650752 | tf_op jit(solution)/shard_map/all_gather | solution.py:76
  96.0 114.8 %all-to-all-start.2 = ((bf16[128,8,256]{2,0,1:T(8,128)(2,1)}), bf16[128,8,256]{2,0,1:T(8,128)(2,1)S(1)}, u32[]{:S(2)}, u32[]{:S(2)}) async-start(bf16[128,8,256]{2,0,1:T(8,128)(2,1)} %bitcast.242), calls=%async_computation.2 | async-start | bytes 1048576 | tf_op jit(solution)/shard_map/all_to_all | solution.py:103
  210.8 27.6 all-to-all-start
  215.4 125.1 %all-gather.28.cloned.1.call-start = ((), (), s32[]{:S(2)}) async-start(), calls=%async_computation.26 | async-start | bytes 4423680 | tf_op jit(solution)/shard_map/all_gather | solution.py:18
  216.7 23.7 copy-start.39
  216.7 96.6 %copy-start.13 = (bf16[128,4,2,256]{3,0,1,2:T(8,128)(2,1)}, bf16[128,4,2,256]{3,0,1,2:T(8,128)(2,1)S(1)}, u32[]{:S(2)}) copy-start(bf16[128,4,2,256]{3,0,1,2:T(8,128)(2,1)S(1)} %copy.127) | copy-start | bytes 1572868
  240.4 219.8 %all-gather.32.cloned.1.call-start = ((), (), s32[]{:S(2)}) async-start(), calls=%async_computation.28 | async-start | bytes 15138816 | tf_op jit(solution)/shard_map/all_gather | solution.py:80
  241.0 325.4 %all-gather.34.cloned.1.call-start = ((), (), s32[]{:S(2)}) async-start(), calls=%async_computation.29 | async-start | bytes 15138816 | tf_op jit(solution)/shard_map/all_gather | solution.py:141
  241.6 429.1 %all-gather.16.cloned.1.call-start = ((), (), s32[]{:S(2)}) async-start(), calls=%async_computation.14 | async-start | bytes 14598144 | tf_op jit(solution)/shard_map/all_gather | solution.py:79
  242.3 532.5 %all-gather.26.cloned.1.call-start = ((), (), s32[]{:S(2)}) async-start(), calls=%async_computation.19 | async-start | bytes 14598144 | tf_op jit(solution)/shard_map/all_gather | solution.py:140
  243.1 635.9 %all-gather.24.cloned.1.call-start = ((), (), s32[]{:S(2)}) async-start(), calls=%async_computation.18 | async-start | bytes 14598144 | tf_op jit(solution)/shard_map/all_gather | solution.py:139
  298.2 15.1 all-to-all-start.1
  355.1 228.3 %all-to-all-start.3 = ((bf16[512,2,432]{2,1,0:T(2,128)(2,1)}), bf16[512,2,432]{2,1,0:T(2,128)(2,1)}, u32[]{:S(2)}, u32[]{:S(2)}) async-start(bf16[512,2,432]{2,1,0:T(2,128)(2,1)} %copy.131), calls=%async_computation.3 | async-start | bytes 2097152 | tf_op jit(solution)/shard_map/all_to_all | solution.py:131
  359.6 676.1 %all-gather.30.cloned.1.call-start = ((), (), s32[]{:S(2)}) async-start(), calls=%async_computation.27 | async-start | bytes 4423680 | tf_op jit(solution)/shard_map/all_gather | solution.py:18
  899.9 10.0 copy-start.34
  920.7 12.5 copy-start.11
  964.0 2413.7 %reduce-scatter.11.cloned.1.call-start = ((), (), s32[]{:S(2)}) async-start(), calls=%async_computation.20 | async-start | bytes 17301504 | tf_op jit(solution)/shard_map/reduce_scatter | solution.py:227
  994.2 2383.5 %reduce-scatter.17.cloned.1.call-start = ((), (), s32[]{:S(2)}) async-start(), calls=%async_computation.23 | async-start | bytes 29196288 | tf_op jit(solution)/shard_map/reduce_scatter | solution.py:234
  1006.7 2370.9 %reduce-scatter.21.cloned.1.call-start = ((), (), s32[]{:S(2)}) async-start(), calls=%async_computation.25 | async-start | bytes 29196288 | tf_op jit(solution)/shard_map/reduce_scatter | solution.py:165
  1019.3 2358.4 %reduce-scatter.19.cloned.1.call-start = ((), (), s32[]{:S(2)}) async-start(), calls=%async_computation.24 | async-start | bytes 29196288 | tf_op jit(solution)/shard_map/reduce_scatter | solution.py:164
  1031.9 2391.0 %reduce-scatter.13.cloned.1.call-start = ((), (), s32[]{:S(2)}) async-start(), calls=%async_computation.21 | async-start | bytes 17301504 | tf_op jit(solution)/shard_map/reduce_scatter | solution.py:230
  1094.4 2597.4 %reduce-scatter.15.cloned.1.call-start = ((), (), s32[]{:S(2)}) async-start(), calls=%async_computation.22 | async-start | bytes 29196288 | tf_op jit(solution)/shard_map/reduce_scatter | solution.py:231
  1180.4 1009.9 %copy-start.19 = (bf16[128,3456]{1,0:T(8,128)(2,1)S(1)}, bf16[128,3456]{1,0:T(8,128)(2,1)}, u32[]{:S(2)}) copy-start(bf16[128,3456]{1,0:T(8,128)(2,1)} %get-tuple-element.295) | copy-start | bytes 2654212
  2185.3 1069.2 %collective-permute-start = (f32[112,2048]{1,0:T(8,128)}, f32[112,2048]{1,0:T(8,128)}, u32[]{:S(2)}, u32[]{:S(2)}) collective-permute-start(f32[112,2048]{1,0:T(8,128)} %fusion), channel_id=1, source_target_pairs={{0,1},{1,2},{2,3},{3,4},{4,5},{5,6},{6,7},{7,8},{8,9},{9,10},{10,1... | collective-permute-start | bytes 2752520
  2202.7 1005.0 %copy-start.3 = (f32[128,2048]{1,0:T(8,128)S(1)}, f32[128,2048]{1,0:T(8,128)}, u32[]{:S(2)}) copy-start(f32[128,2048]{1,0:T(8,128)} %copy-done.1) | copy-start | bytes 3145732
  3194.9 69.6 %collective-permute-start.2 = (f32[112,2048]{1,0:T(8,128)}, f32[112,2048]{1,0:T(8,128)}, u32[]{:S(2)}, u32[]{:S(2)}) collective-permute-start(f32[112,2048]{1,0:T(8,128)} %fusion.1), channel_id=1, source_target_pairs={{0,1},{1,2},{2,3},{3,4},{4,5},{5,6},{6,7},{7,8},{8,9},{9,10},{10,1... | collective-permute-start | bytes 2752520
  3203.5 50.9 %collective-permute-start.1 = (f32[12,2048]{1,0:T(8,128)S(1)}, f32[12,2048]{1,0:T(8,128)}, u32[]{:S(2)}, u32[]{:S(2)}) collective-permute-start(f32[12,2048]{1,0:T(8,128)S(1)} %slice.15), channel_id=1, source_target_pairs={{0,2},{1,3},{2,4},{3,5},{4,6},{5,7},{6,8},{7,9},{8,10},{9,11},{10,... | collective-permute-start | bytes 294920
  3205.4 59.1 %collective-permute-start.3 = (f32[12,2048]{1,0:T(8,128)}, f32[12,2048]{1,0:T(8,128)}, u32[]{:S(2)}, u32[]{:S(2)}) collective-permute-start(f32[12,2048]{1,0:T(8,128)} %slice.16), channel_id=1, source_target_pairs={{0,2},{1,3},{2,4},{3,5},{4,6},{5,7},{6,8},{7,9},{8,10},{9,11},{10,... | collective-permute-start | bytes 294920
  3216.1 48.5 %copy-start.26 = (f32[112,2048]{1,0:T(8,128)S(1)}, f32[112,2048]{1,0:T(8,128)}, u32[]{:S(2)}) copy-start(f32[112,2048]{1,0:T(8,128)} %fusion.1) | copy-start | bytes 2752516
  (36 other events, 146.9 us)
Sparse Core Ops, SparseCore 0:
  11.0 79.3 all-gather.21
  93.2 108.9 all-gather.17
  205.2 87.4 all-gather.19
  295.0 45.4 all-gather.27
  343.1 117.0 all-gather.31
  462.9 103.5 all-gather.33
  569.2 101.3 all-gather.15
  673.5 101.3 all-gather.25
  777.6 101.3 all-gather.23
  964.1 47.2 all-gather.29
  1014.2 616.6 reduce-scatter.10
  1637.8 414.8 reduce-scatter.16
  2059.7 410.3 reduce-scatter.20
  2476.9 414.2 reduce-scatter.18
  2893.9 528.9 reduce-scatter.12
  3429.8 262.0 reduce-scatter.14
where the time goes:
time: 3710 us; the launch traced here: 3700 us
  blocking collectives  2240 us (60%)
  waiting for transfers between devices  1040 us (28%)
  matrix products  244 us (7%)
  local copies, waits for them, and re-layouts  115 us (3%)
    unnamed x5, blocking collectives  2110 us
    reduce_scatter x1, waiting for transfers between devices, local(): lax.psum_scatter(grad_value_term, ('dp', 'ctx', 'ulysses'), scatter_dimen...  269 us
    dot_general x24, matrix products, matmul(): return jnp.dot(left, right, preferred_element_type=jnp.float32)  223 us
    all_gather x1, waiting for transfers between devices, local(): lax.all_gather(w_value, ('dp', 'ctx', 'ulysses'), axis=0, tiled=True)  103 us
    all_gather x1, waiting for transfers between devices, local(): lax.all_gather(w_output, ('dp', 'ctx', 'ulysses'), axis=0, tiled=True)  101 us
    all_gather x1, waiting for transfers between devices, local(): lax.all_gather(w_gate, ('dp', 'ctx', 'ulysses'), axis=0, tiled=True)  95.7 us
    all_gather x1, waiting for transfers between devices, local(): lax.all_gather(w_down, ('dp', 'ctx', 'ulysses'), axis=0, tiled=True)  89.4 us
    all_gather x1, waiting for transfers between devices, local(): lax.all_gather(w_up, ('dp', 'ctx', 'ulysses'), axis=0, tiled=True)  85 us
  transfers between devices with their start and end apart: 24, of which 15 were waited for; matrix products, arithmetic and copies ran while one was open for 62% of the time, Pallas kernels for 0%

commit v1 on v0

--- a/solution.py
+++ b/solution.py
@@ -52,11 +52,19 @@
     return (earlier[0] * later[0], later[1] + later[0][:, None, None] * earlier[1])
 
 
+def running_sum(values):
+    size = values.shape[-1]
+    upper = lax.broadcasted_iota(jnp.int32, (size, size), 0) <= lax.broadcasted_iota(
+        jnp.int32, (size, size), 1
+    )
+    return jnp.dot(values, upper.astype(jnp.float32), precision=lax.Precision.HIGHEST)
+
+
 def matmul(left, right):
     return jnp.dot(left, right, preferred_element_type=jnp.float32)
 
 
-def local(
+def local_any(
     hidden_in,
     cotangent,
     log_decay,
@@ -105,7 +113,7 @@
     )
     block = head_q.shape[0]
     scale = 1.0 / math.sqrt(KEY_DIM)
-    cumulative = jnp.cumsum(log_decay[0], axis=1)
+    cumulative = running_sum(log_decay[0])
     later = lax.broadcasted_iota(jnp.int32, (block, block), 0) >= lax.broadcasted_iota(
         jnp.int32, (block, block), 1
     )
@@ -255,7 +263,291 @@
     )
 
 
+HEAD_AXES = ("dp", "ulysses")
+FF_AXES = ("dp", "ctx")
+
+
+def dot_t(left, right):
+    return lax.dot_general(left, right, (((0,), (0,)), ((), ())), preferred_element_type=jnp.float32)
+
+
+def dot_nt(left, right):
+    return lax.dot_general(left, right, (((1,), (1,)), ((), ())), preferred_element_type=jnp.float32)
+
+
+def by_head(weight, width):
+    rows = weight.shape[0]
+    return (
+        weight.reshape(rows, 4, 2, width).transpose(2, 1, 0, 3).reshape(8, rows, width)
+    )
+
+
+def from_heads(parts, width):
+    rows = parts.shape[1]
+    return parts.reshape(2, 4, rows, width).transpose(2, 1, 0, 3).reshape(rows, 8 * width)
+
+
+def local(
+    hidden_in,
+    cotangent,
+    log_decay,
+    w_query,
+    w_key,
+    w_value,
+    w_swish,
+    w_output,
+    w_gate,
+    w_up,
+    w_down,
+    gain_attn,
+    gain_ffn,
+):
+    bf16, f32 = jnp.bfloat16, jnp.float32
+    everywhere = ("dp", "ctx", "ulysses")
+    dp, ctx, uly = (lax.axis_index(a) for a in everywhere)
+    tokens = hidden_in.shape[1]
+    width = hidden_in.shape[2]
+    rows = w_query.shape[0]
+    out_rows = w_output.shape[0]
+    key, val, ff = KEY_DIM, VALUE_DIM, w_gate.shape[1] // 8
+
+    packed = jnp.concatenate(
+        [by_head(w_query, key), by_head(w_key, key), by_head(w_value, val), by_head(w_swish, val)],
+        axis=2,
+    )
+    attn_cols = packed.shape[2]
+    packed = lax.all_to_all(packed, HEAD_AXES, split_axis=0, concat_axis=0, tiled=True)
+    packed = lax.all_gather(packed, "ctx", axis=0)
+    w_attn = (
+        packed.reshape(4, 2, 4, rows, attn_cols)
+        .transpose(1, 0, 2, 3, 4)
+        .reshape(32 * rows, attn_cols)
+    )
+    quarter = width // 4
+    pieces = []
+    for shift in range(4):
+        piece = lax.dynamic_slice_in_dim(w_output, (uly + shift) % 4 * quarter, quarter, axis=1)
+        perm = []
+        for d in range(2):
+            for c in range(4):
+                for u in range(4):
+                    h = d * 4 + c
+                    perm.append((d * 16 + c * 4 + u, (h % 2) * 16 + (u + shift) % 4 * 4 + h // 2))
+        pieces.append(lax.ppermute(piece, everywhere, perm))
+    mine = jnp.zeros((4, out_rows, quarter), bf16)
+    for shift in range(4):
+        mine = lax.dynamic_update_index_in_dim(mine, pieces[shift], (ctx - shift) % 4, 0)
+    w_out = (
+        lax.all_gather(mine, "ctx", axis=0).transpose(1, 2, 0, 3).reshape(4 * out_rows, width)
+    )
+    gate_up = jnp.concatenate(
+        [
+            w_gate.reshape(rows, 8, ff).transpose(1, 0, 2),
+            w_up.reshape(rows, 8, ff).transpose(1, 0, 2),
+        ],
+        axis=2,
+    )
+    gate_up = lax.all_to_all(gate_up, FF_AXES, split_axis=0, concat_axis=0, tiled=True)
+    gate_up = lax.all_gather(gate_up, "ulysses", axis=0)
+    w_gu = (
+        gate_up.reshape(4, 8, rows, 2 * ff).transpose(1, 0, 2, 3).reshape(32 * rows, 2 * ff)
+    )
+    w_dn = lax.all_gather(w_down, "ulysses", axis=0, tiled=True)
+
+    gain_one = lax.all_gather(gain_attn, everywhere, axis=0, tiled=True).astype(f32)
+    gain_two = lax.all_gather(gain_ffn, everywhere, axis=0, tiled=True).astype(f32)
+
+    top_all = lax.all_gather(cotangent[0], FF_AXES, axis=0, tiled=True)
+    hidden_all = lax.all_gather(hidden_in[0], HEAD_AXES, axis=0, tiled=True)
+    normed_all, _ = normalize(hidden_all.astype(f32))
+    scaled_one = (normed_all * gain_one).astype(bf16)
+    qkvs = matmul(scaled_one, w_attn)
+    block = 4 * tokens
+    q = qkvs[:, :key].astype(bf16).reshape(2, block, key)
+    k = qkvs[:, key : 2 * key].astype(bf16).reshape(2, block, key)
+    v = qkvs[:, 2 * key : 2 * key + val].astype(bf16).reshape(2, block, val)
+    swish_pre = qkvs[:, 2 * key + val :]
+
+    own = lax.dynamic_slice_in_dim(log_decay[0], dp, 1, axis=0)
+    other = lax.ppermute(
+        lax.dynamic_slice_in_dim(log_decay[0], 1 - dp, 1, axis=0), "dp", [(0, 1), (1, 0)]
+    )
+    decay = jnp.where(
+        dp == 0, jnp.concatenate([own, other]), jnp.concatenate([other, own])
+    )
+    scale = 1.0 / math.sqrt(KEY_DIM)
+    cumulative = running_sum(decay)
+    later = lax.broadcasted_iota(jnp.int32, (block, block), 0) >= lax.broadcasted_iota(
+        jnp.int32, (block, block), 1
+    )
+    gap = cumulative[:, :, None] - cumulative[:, None, :]
+    mask = jnp.where(later[None], jnp.exp(jnp.minimum(gap, 0.0)), 0.0) * scale
+    last = cumulative[:, -1:]
+    tail = jnp.exp(last - cumulative)[:, :, None]
+    reach = jnp.exp(cumulative)[:, :, None]
+
+    def bdot(pattern, a, b):
+        return jnp.einsum(pattern, a, b, preferred_element_type=f32)
+
+    weights = (bdot("btd,bsd->bts", q, k) * mask).astype(bf16)
+    k_tail = (k.astype(f32) * tail).astype(bf16)
+    update = bdot("bsd,bse->bde", k_tail, v)
+    lasts = lax.all_gather(last[:, 0], "ctx", axis=0)
+    spots = jnp.arange(4)
+    before = jnp.stack(
+        [
+            jnp.where(
+                j < ctx,
+                jnp.exp(jnp.sum(jnp.where(((spots > j) & (spots < ctx))[:, None], lasts, 0.0), 0)),
+                0.0,
+            )
+            for j in range(4)
+        ]
+    )
+    after = jnp.stack(
+        [
+            jnp.where(
+                j > ctx,
+                jnp.exp(jnp.sum(jnp.where(((spots < j) & (spots > ctx))[:, None], lasts, 0.0), 0)),
+                0.0,
+            )
+            for j in range(4)
+        ]
+    )
+    updates = lax.all_gather(update.astype(bf16), "ctx", axis=0).astype(f32)
+    state_in = jnp.sum(before[:, :, None, None] * updates, axis=0).astype(bf16)
+    retained = bdot("bts,bse->bte", weights, v) + scale * reach * bdot("btd,bde->bte", q, state_in)
+    head_normed, head_inverse = normalize(retained)
+    head_out = head_normed.astype(bf16).reshape(2 * block, val).astype(f32)
+    swish_act = jax.nn.silu(swish_pre)
+    gated = (swish_act * head_out).astype(bf16)
+    attn = lax.psum_scatter(
+        matmul(gated, w_out).astype(bf16), HEAD_AXES, scatter_dimension=0, tiled=True
+    )
+    inputs = hidden_in[0].astype(f32)
+    residual = inputs + attn.astype(f32)
+
+    normed_two, inverse_two = normalize(residual)
+    scaled_two = lax.all_gather(
+        (normed_two * gain_two).astype(bf16), FF_AXES, axis=0, tiled=True
+    )
+    gu = matmul(scaled_two, w_gu)
+    gate_pre, up_pre = gu[:, :ff], gu[:, ff:]
+    gate_act = jax.nn.silu(gate_pre)
+    product = (gate_act * up_pre).astype(bf16)
+    grad_product = dot_nt(top_all, w_dn)
+    grad_gu = jnp.concatenate(
+        [
+            (grad_product * up_pre * swish_slope(gate_pre)).astype(bf16),
+            (grad_product * gate_act).astype(bf16),
+        ],
+        axis=1,
+    )
+    gs2 = lax.psum_scatter(
+        dot_nt(grad_gu, w_gu).astype(bf16), FF_AXES, scatter_dimension=0, tiled=True
+    ).astype(f32)
+    out_part = lax.psum_scatter(
+        matmul(product, w_dn).astype(bf16), FF_AXES, scatter_dimension=0, tiled=True
+    )
+    layer_out = residual + out_part.astype(f32)
+    grad_top = cotangent[0].astype(f32)
+    gain_two_term = jnp.sum(gs2 * normed_two, axis=0)
+    grad_residual = grad_top + norm_back(gs2 * gain_two, normed_two, inverse_two)
+    grad_y = lax.all_gather(grad_residual.astype(bf16), HEAD_AXES, axis=0, tiled=True)
+
+    grad_down = lax.psum_scatter(
+        dot_t(product, top_all).astype(bf16).reshape(4, out_rows, width),
+        "ulysses",
+        scatter_dimension=0,
+        tiled=True,
+    )[0].astype(f32)
+    ggu = dot_t(scaled_two, grad_gu).astype(bf16).reshape(8, 4, rows, 2 * ff).transpose(1, 0, 2, 3)
+    ggu = lax.psum_scatter(ggu, "ulysses", scatter_dimension=0, tiled=True)[0]
+    ggu = lax.all_to_all(ggu, FF_AXES, split_axis=0, concat_axis=0, tiled=True).astype(f32)
+    grad_gate = ggu[:, :, :ff].transpose(1, 0, 2).reshape(rows, 8 * ff)
+    grad_up = ggu[:, :, ff:].transpose(1, 0, 2).reshape(rows, 8 * ff)
+
+    grad_gated = dot_nt(grad_y, w_out)
+    g_out = dot_t(gated, grad_y).astype(bf16)
+    grad_swish_pre = (grad_gated * head_out * swish_slope(swish_pre)).astype(bf16)
+    grad_head = (grad_gated * swish_act).astype(bf16).astype(f32).reshape(2, block, val)
+    grad_retained = norm_back(grad_head, head_normed, head_inverse).astype(bf16)
+    grad_scores = (bdot("bte,bse->bts", grad_retained, v) * mask).astype(bf16)
+    q_reach = (q.astype(f32) * (reach * scale)).astype(bf16)
+    grad_state = bdot("btd,bte->bde", q_reach, grad_retained)
+    grad_states = lax.all_gather(grad_state.astype(bf16), "ctx", axis=0).astype(f32)
+    grad_update = jnp.sum(after[:, :, None, None] * grad_states, axis=0).astype(bf16)
+    grad_q = bdot("bts,bsd->btd", grad_scores, k) + scale * reach * bdot(
+        "bte,bde->btd", grad_retained, state_in
+    )
+    grad_k = bdot("bts,btd->bsd", grad_scores, q) + tail * bdot("bse,bde->bsd", v, grad_update)
+    grad_v = bdot("bts,bte->bse", weights, grad_retained) + tail * bdot(
+        "bsd,bde->bse", k, grad_update
+    )
+    grad_cat = jnp.concatenate(
+        [
+            grad_q.astype(bf16).reshape(2 * block, key),
+            grad_k.astype(bf16).reshape(2 * block, key),
+            grad_v.astype(bf16).reshape(2 * block, val),
+            grad_swish_pre,
+        ],
+        axis=1,
+    )
+    gs1 = lax.psum_scatter(
+        dot_nt(grad_cat, w_attn).astype(bf16), HEAD_AXES, scatter_dimension=0, tiled=True
+    ).astype(f32)
+    normed_one, inverse_one = normalize(inputs)
+    gain_one_term = jnp.sum(gs1 * normed_one, axis=0)
+    grad_input = grad_residual + norm_back(gs1 * gain_one, normed_one, inverse_one)
+
+    gcat = dot_t(scaled_one, grad_cat).astype(bf16).reshape(2, 4, 4, rows, attn_cols)
+    gcat = lax.psum_scatter(
+        gcat.transpose(1, 0, 2, 3, 4), "ctx", scatter_dimension=0, tiled=True
+    )
+    gcat = lax.all_to_all(
+        gcat.reshape(8, rows, attn_cols), HEAD_AXES, split_axis=0, concat_axis=0, tiled=True
+    ).astype(f32)
+    grad_query = from_heads(gcat[:, :, :key], key)
+    grad_key = from_heads(gcat[:, :, key : 2 * key], key)
+    grad_value = from_heads(gcat[:, :, 2 * key : 2 * key + val], val)
+    grad_swish = from_heads(gcat[:, :, 2 * key + val :], val)
+
+    g_out = g_out.reshape(4, out_rows, 4, quarter).transpose(2, 0, 1, 3)
+    g_out = lax.psum_scatter(g_out, "ctx", scatter_dimension=0, tiled=True)[0]
+    grad_output = jnp.zeros((4, out_rows, quarter), bf16)
+    for shift in range(4):
+        piece = lax.dynamic_index_in_dim(g_out, (ctx - shift) % 4, 0, keepdims=False)
+        perm = []
+        for d in range(2):
+            for c in range(4):
+                for u in range(4):
+                    h = d * 4 + c
+                    perm.append(((h % 2) * 16 + (u + shift) % 4 * 4 + h // 2, d * 16 + c * 4 + u))
+        got = lax.ppermute(piece, everywhere, perm)
+        grad_output = lax.dynamic_update_index_in_dim(grad_output, got, (uly + shift) % 4, 0)
+    grad_output = grad_output.astype(f32).transpose(1, 0, 2).reshape(out_rows, width)
+
+    gain_terms = lax.psum_scatter(
+        jnp.stack([gain_one_term, gain_two_term]), everywhere, scatter_dimension=1, tiled=True
+    )
+    return (
+        layer_out[None],
+        grad_input[None],
+        grad_query,
+        grad_key,
+        grad_value,
+        grad_swish,
+        grad_output,
+        grad_gate,
+        grad_up,
+        grad_down,
+        gain_terms[0],
+        gain_terms[1],
+    )
+
+
 def solution(mesh):
+    planned = (mesh.shape["dp"], mesh.shape["ctx"], mesh.shape["ulysses"]) == (2, 4, 4)
     placed = (
         P("dp", ("ctx", "ulysses"), None),
         P("dp", ("ctx", "ulysses"), None),
@@ -272,7 +564,7 @@
         P(("dp", "ctx", "ulysses")),
     )
     return jax.shard_map(
-        local,
+        local if planned else local_any,
         mesh=mesh,
         in_specs=placed,
         out_specs=(

time: 3710 us -> 1350 us (0.36)
  blocking collectives: 2240 us -> 138 us
  waiting for transfers between devices: 1040 us -> 862 us
  matrix products: 244 us -> 104 us
    unnamed x5 -> x2, blocking collectives: 2110 us -> 50.8 us
    all_gather x10, waiting for transfers between devices: 660 us -> 144 us  [the longest x1 45.8 us: local(): lax.all_gather(grad_residual.astype(bf16), HEAD_AXES, axis=0, tiled=True)]
    unnamed x20 -> x21, waiting for transfers between devices: 44.3 us -> 356 us
    dot_general x24 -> x4, matrix products: 223 us -> 27.4 us  [matmul(): return jnp.dot(left, right, preferred_element_type=jnp.float32)]
    dot_general x12 -> x21, matrix products: 21 us -> 76.3 us  [the longest x4 32.3 us: dot_nt(): lax.dot_general(left, right, (((1,), (1,)), ((), ())), preferred_element_...]
    unnamed x107 -> x154, local copies, waits for them, and re-layouts: 72.5 us -> 26.5 us
    all_to_all x4 -> x2, blocking collectives: 126 us -> 86.7 us  [the longest x1 69.4 us: local(): lax.all_to_all(packed, HEAD_AXES, split_axis=0, concat_axis=0, tiled=True)]
    reduce_scatter x6 -> x5, waiting for transfers between devices: 314 us -> 348 us  [the longest x1 155 us: local(): lax.psum_scatter(matmul(gated, w_out).astype(bf16), HEAD_AXES, scatter_di...]
  transfers between devices with their start and end apart: 24 -> 29, of which waited for: 15 -> 16; matrix products, arithmetic and copies ran while one was open for 62% -> 16% of each run, Pallas kernels for 0% -> 0%
where the time goes in v1:
time: 1350 us; the launch traced here: 1330 us
  waiting for transfers between devices  862 us (64%)
  local copies, waits for them, and re-layouts  141 us (10%)
  blocking collectives  138 us (10%)
  matrix products  104 us (8%)
  starting transfers between devices  33.8 us (3%)
  other arithmetic  32 us (2%)
  between operations  18.9 us (1%)
    unnamed x21, waiting for transfers between devices  356 us
    reduce_scatter x1, waiting for transfers between devices, local(): lax.psum_scatter(matmul(gated, w_out).astype(bf16), HEAD_AXES, scatter_di...  155 us
    all_to_all x1, blocking collectives, local(): lax.all_to_all(packed, HEAD_AXES, split_axis=0, concat_axis=0, tiled=True)  69.4 us
    reduce_scatter x1, waiting for transfers between devices, local(): lax.psum_scatter(dot_t(product, top_all).astype(bf16).reshape(4, out_rows...  60.8 us
    unnamed x2, blocking collectives  50.8 us
    reduce_scatter x1, waiting for transfers between devices, local(): lax.psum_scatter(dot_nt(grad_gu, w_gu).astype(bf16), FF_AXES, scatter_dim...  50.7 us
    reduce_scatter x1, waiting for transfers between devices, local(): lax.psum_scatter(matmul(product, w_dn).astype(bf16), FF_AXES, scatter_dim...  47.3 us
    all_gather x1, waiting for transfers between devices, local(): lax.all_gather(grad_residual.astype(bf16), HEAD_AXES, axis=0, tiled=True)  45.8 us
  transfers between devices with their start and end apart: 29, of which 16 were waited for; matrix products, arithmetic and copies ran while one was open for 16% of the time, Pallas kernels for 0%

profile of v1, /device:TPU:9, one launch (start us, length us, event | category | flops | bytes accessed | tf_op | source)
XLA Modules:
  0.0 1328.7 jit_solution(12578751127250322115)
XLA Ops:
  15.6 69.4 %all_to_all.20 = bf16[8,64,1376]{2,1,0:T(8,128)(2,1)} all-to-all(bf16[8,64,1376]{2,1,0:T(8,128)(2,1)S(1)} %concatenate.18), channel_id=1, replica_groups=mesh['dp'=2,'ctx'=4,'ulysses'=4] {'dp','ulysses'}, dimensions={0} | all-to-all | bytes 2818048 | tf_op jit(solution)/shard_map/all_to_all | solution.py:319
  98.1 43.1 %all-reduce.6 = (bf16[2048]{0:T(1024)(128)(2,1)S(1)}, bf16[2048]{0:T(1024)(128)(2,1)S(1)}) all-reduce(bf16[2048]{0:T(1024)(128)(2,1)S(1)} %dynamic-update-slice, bf16[2048]{0:T(1024)(128)(2,1)S(1)} %dynamic-update-slice.2), channel_id=1, replica_groups=mesh['dp'=2,'ctx'=4,'ulysses'=4] {'dp','ctx','ulysses'}, use_global_device_ids=true, to_apply=%add | all-reduce | flops 4096 | bytes 16384
  164.8 8.5 fusion.83
  176.7 7.8 all-reduce.1
  185.3 10.5 all-gather.19.cloned.1.call-done
  203.5 27.2 %all-gather.29.cloned.1.call-done = bf16[8,256,432]{1,2,0:T(8,128)(2,1)} async-done(((bf16[2,256,432]{1,2,0:T(8,128)(2,1)}), bf16[8,256,432]{1,2,0:T(8,128)(2,1)}) %all-gather.29.cloned.1.call-update) | async-done | bytes 1769488 | tf_op jit(solution)/shard_map/all_gather | solution.py:417
  246.0 17.3 %all_to_all.21 = bf16[8,64,864]{2,1,0:T(8,128)(2,1)} all-to-all(bf16[8,64,864]{2,1,0:T(8,128)(2,1)S(1)} %copy.271), channel_id=1, replica_groups=mesh['dp'=2,'ctx'=4,'ulysses'=4] {'dp','ctx'}, dimensions={0} | all-to-all | bytes 1769472 | tf_op jit(solution)/shard_map/all_to_all | solution.py:350
  263.4 154.6 %reduce-scatter.11.cloned.1.call-done = bf16[128,2048]{1,0:T(8,128)(2,1)} async-done(((bf16[1024,2048]{1,0:T(8,128)(2,1)}), bf16[128,2048]{1,0:T(8,128)(2,1)}) %reduce-scatter.11.cloned.1.call-update) | async-done | bytes 524304 | tf_op jit(solution)/shard_map/reduce_scatter | solution.py:424
  429.4 31.1 %all-gather.21.cloned.1.call-done = bf16[1024,2048]{1,0:T(8,128)(2,1)} async-done(((bf16[128,2048]{1,0:T(8,128)(2,1)}), bf16[1024,2048]{1,0:T(8,128)(2,1)}) %all-gather.21.cloned.1.call-update) | async-done | bytes 4194320 | tf_op jit(solution)/shard_map/all_gather | solution.py:431
  460.4 9.0 fusion.84
  469.4 29.5 %all-gather.33.cloned.1.call-done = bf16[1,1024,2048]{2,1,0:T(8,128)(2,1)} async-done(((bf16[1,128,2048]{2,1,0:T(8,128)(2,1)}), bf16[1,1024,2048]{2,1,0:T(8,128)(2,1)}) %all-gather.33.cloned.1.call-update) | async-done | bytes 4194320 | tf_op jit(solution)/shard_map/all_gather | solution.py:360
  498.9 7.4 multiply_convert_fusion.5
  507.5 6.1 convolution_convert_fusion.4
  513.7 50.7 %reduce-scatter.15.cloned.1.call-done = bf16[128,2048]{1,0:T(8,128)(2,1)} async-done(((bf16[1024,2048]{1,0:T(8,128)(2,1)}), bf16[128,2048]{1,0:T(8,128)(2,1)}) %reduce-scatter.15.cloned.1.call-update) | async-done | bytes 524304 | tf_op jit(solution)/shard_map/reduce_scatter | solution.py:446
  569.4 45.8 %all-gather.23.cloned.1.call-done = bf16[1024,2048]{1,0:T(8,128)(2,1)} async-done(((bf16[128,2048]{1,0:T(8,128)(2,1)}), bf16[1024,2048]{1,0:T(8,128)(2,1)}) %all-gather.23.cloned.1.call-update) | async-done | bytes 4194320 | tf_op jit(solution)/shard_map/all_gather | solution.py:456
  615.2 7.2 fusion.41
  625.9 8.2 convolution_convert_fusion.5
  634.1 6.1 copy.299
  650.4 5.1 reshape.403
  675.6 9.3 convolution_convert_fusion
  684.9 8.4 copy.285
  699.3 11.6 convolution_convert_fusion.3
  712.5 5.6 convolution_convert_fusion.1
  719.3 56.6 %all-reduce.11.cloned.1.call-done = bf16[4,8,64,864]{3,2,0,1:T(8,128)(2,1)} async-done(((bf16[4,8,64,864]{3,2,0,1:T(8,128)(2,1)}), bf16[4,8,64,864]{3,2,0,1:T(8,128)(2,1)}) %all-reduce.11.cloned.1.call-update) | async-done | bytes 3538960
  783.8 163.1 %all-reduce.13.cloned.1.call-done = (bf16[4,2,4,64,1376]{4,3,2,0,1:T(8,128)(2,1)}, bf16[4,4,108,512]{3,1,2,0:T(4,128)(2,1)}) async-done(((bf16[4,2,4,64,1376]{4,3,2,0,1:T(8,128)(2,1)}, bf16[4,4,108,512]{3,1,2,0:T(4,128)(2,1)}), (bf16[4,2,4,64,1376]{4,3,2,0,1:T(8,128)(2,1)}, bf16[4,4,108,512]{3,1,2,0:T(4,128)(2,1)})) %all-reduce.13.cloned.1.call-update) | async-done | bytes 7405584
  951.1 5.6 all-to-all-start.2
  956.6 60.8 %reduce-scatter.19.cloned.1.call-done = bf16[1,108,2048]{2,1,0:T(8,128)(2,1)} async-done(((bf16[4,108,2048]{2,1,0:T(8,128)(2,1)}), bf16[1,108,2048]{2,1,0:T(8,128)(2,1)}) %reduce-scatter.19.cloned.1.call-update) | async-done | bytes 442384 | tf_op jit(solution)/shard_map/reduce_scatter | solution.py:458
  1044.8 9.8 collective-permute-done.5
  1062.3 5.1 dynamic_update_slice.33
  1083.4 34.0 %reduce-scatter.17.cloned.1.call-done = bf16[128,2048]{1,0:T(8,128)(2,1)} async-done(((bf16[1024,2048]{1,0:T(8,128)(2,1)}), bf16[128,2048]{1,0:T(8,128)(2,1)}) %reduce-scatter.17.cloned.1.call-update) | async-done | bytes 524304 | tf_op jit(solution)/shard_map/reduce_scatter | solution.py:496
  1124.0 47.3 %reduce-scatter.13.cloned.1.call-done = bf16[128,2048]{1,0:T(8,128)(2,1)} async-done(((bf16[1024,2048]{1,0:T(8,128)(2,1)}), bf16[128,2048]{1,0:T(8,128)(2,1)}) %reduce-scatter.13.cloned.1.call-update) | async-done | bytes 524304 | tf_op jit(solution)/shard_map/reduce_scatter | solution.py:449
  1174.8 134.4 %reduce-scatter.21.cloned.1.call-done = f32[64,2]{1,0:T(8,128)} async-done(((f32[2048,2]{1,0:T(8,128)}), f32[64,2]{1,0:T(8,128)}) %reduce-scatter.21.cloned.1.call-update) | async-done | bytes 528
  (339 shorter events, 213.8 us)
Async XLA Ops:
  8.0 149.7 %all-gather.25.cloned.1.call-start = ((), (), s32[]{:S(2)}) async-start(), calls=%async_computation.18 | async-start | bytes 4718592 | tf_op jit(solution)/shard_map/all_gather | solution.py:361
  8.8 152.1 %all-gather.27.cloned.1.call-start = ((), (), s32[]{:S(2)}) async-start(), calls=%async_computation.19 | async-start | bytes 7208960 | tf_op jit(solution)/shard_map/all_gather | solution.py:320
  85.0 110.8 %all-gather.19.cloned.1.call-start = ((), (), s32[]{:S(2)}) async-start(), calls=%async_computation.10 | async-start | bytes 2211840 | tf_op jit(solution)/shard_map/all_gather | solution.py:341
  85.1 56.0 %collective-permute-start = (f32[1,512]{1,0:T(1,128)S(1)}, f32[1,512]{1,0:T(1,128)S(1)}, u32[]{:S(2)}, u32[]{:S(2)}) collective-permute-start(f32[1,512]{1,0:T(1,128)S(1)} %get-tuple-element.56), channel_id=1, source_target_pairs={{0,16},{16,0},{1,17},{17,1},{2,18},{18,2},{3,19},{19,3},{4,20},{20... | collective-permute-start | bytes 6152 | tf_op jit(solution)/shard_map/ppermute | solution.py:372
  85.6 56.1 %collective-permute-start.4 = (bf16[108,512]{1,0:T(8,128)(2,1)S(1)}, bf16[108,512]{1,0:T(8,128)(2,1)S(1)}, u32[]{:S(2)}, u32[]{:S(2)}) collective-permute-start(bf16[108,512]{1,0:T(8,128)(2,1)S(1)} %get-tuple-element.47), channel_id=1, source_target_pairs={{0,12},{1,0},{2,4},{3,8},{4,28},{5,16},{6,20},{7,24},{8,13},{9,1},... | collective-permute-start | bytes 331784 | tf_op jit(solution)/shard_map/ppermute | solution.py:336
  88.4 53.5 %collective-permute-start.2 = (bf16[108,512]{1,0:T(8,128)(2,1)S(1)}, bf16[108,512]{1,0:T(8,128)(2,1)S(1)}, u32[]{:S(2)}, u32[]{:S(2)}) collective-permute-start(bf16[108,512]{1,0:T(8,128)(2,1)S(1)} %get-tuple-element.48), channel_id=1, source_target_pairs={{0,4},{1,8},{2,12},{3,0},{4,20},{5,24},{6,28},{7,16},{8,5},{9,9},{... | collective-permute-start | bytes 331784 | tf_op jit(solution)/shard_map/ppermute | solution.py:336
  93.0 49.1 %collective-permute-start.1 = (bf16[108,512]{1,0:T(8,128)(2,1)S(1)}, bf16[108,512]{1,0:T(8,128)(2,1)S(1)}, u32[]{:S(2)}, u32[]{:S(2)}) collective-permute-start(bf16[108,512]{1,0:T(8,128)(2,1)S(1)} %get-tuple-element.49), channel_id=1, source_target_pairs={{0,0},{1,4},{2,8},{3,12},{4,16},{5,20},{6,24},{7,28},{8,1},{9,5},{... | collective-permute-start | bytes 331784 | tf_op jit(solution)/shard_map/ppermute | solution.py:336
  97.2 45.0 %collective-permute-start.3 = (bf16[108,512]{1,0:T(8,128)(2,1)S(1)}, bf16[108,512]{1,0:T(8,128)(2,1)S(1)}, u32[]{:S(2)}, u32[]{:S(2)}) collective-permute-start(bf16[108,512]{1,0:T(8,128)(2,1)S(1)} %get-tuple-element.50), channel_id=1, source_target_pairs={{0,8},{1,12},{2,0},{3,4},{4,24},{5,28},{6,16},{7,20},{8,9},{9,13},... | collective-permute-start | bytes 331784 | tf_op jit(solution)/shard_map/ppermute | solution.py:336
  141.7 91.1 %copy-start.46 = (f32[2,512]{1,0:T(2,128)}, f32[2,512]{1,0:T(2,128)S(1)}, u32[]{:S(2)}) copy-start(f32[2,512]{1,0:T(2,128)S(1)} %get-tuple-element.54) | copy-start | bytes 12292
  157.2 73.5 %all-gather.29.cloned.1.call-start = ((), (), s32[]{:S(2)}) async-start(), calls=%async_computation.20 | async-start | bytes 2211840 | tf_op jit(solution)/shard_map/all_gather | solution.py:417
  175.0 243.0 %reduce-scatter.11.cloned.1.call-start = ((), (), s32[]{:S(2)}) async-start(), calls=%async_computation.11 | async-start | bytes 4718592 | tf_op jit(solution)/shard_map/reduce_scatter | solution.py:424
  242.1 180.3 %all-gather.37.cloned.1.call-start = ((), (), s32[]{:S(2)}) async-start(), calls=%async_computation.24 | async-start | bytes 2293760 | tf_op jit(solution)/shard_map/all_gather | solution.py:355
  242.7 182.4 %all-gather.31.cloned.1.call-start = ((), (), s32[]{:S(2)}) async-start(), calls=%async_computation.21 | async-start | bytes 4587520 | tf_op jit(solution)/shard_map/all_gather | solution.py:351
  245.8 172.2 %copy-start = (bf16[1,128,2048]{2,1,0:T(8,128)(2,1)S(1)}, bf16[1,128,2048]{2,1,0:T(8,128)(2,1)}, u32[]{:S(2)}) copy-start(bf16[1,128,2048]{2,1,0:T(8,128)(2,1)} %param.13) | copy-start | bytes 1572868
  263.3 197.1 %all-gather.21.cloned.1.call-start = ((), (), s32[]{:S(2)}) async-start(), calls=%async_computation.12 | async-start | bytes 4718592 | tf_op jit(solution)/shard_map/all_gather | solution.py:431
  419.3 147.3 %copy-start.48 = (f32[128]{0:T(128)}, f32[128]{0:T(128)S(1)}, u32[]{:S(2)}) copy-start(f32[128]{0:T(128)S(1)} %add_rsqrt_fusion.3) | copy-start | bytes 1540
  421.4 77.5 %all-gather.33.cloned.1.call-start = ((), (), s32[]{:S(2)}) async-start(), calls=%async_computation.22 | async-start | bytes 4718592 | tf_op jit(solution)/shard_map/all_gather | solution.py:360
  422.2 142.3 %reduce-scatter.15.cloned.1.call-start = ((), (), s32[]{:S(2)}) async-start(), calls=%async_computation.14 | async-start | bytes 4718592 | tf_op jit(solution)/shard_map/reduce_scatter | solution.py:446
  513.7 101.5 %all-gather.23.cloned.1.call-start = ((), (), s32[]{:S(2)}) async-start(), calls=%async_computation.15 | async-start | bytes 4718592 | tf_op jit(solution)/shard_map/all_gather | solution.py:456
  569.0 97.0 %all-gather.35.cloned.1.call-start = ((), (), s32[]{:S(2)}) async-start(), calls=%async_computation.23 | async-start | bytes 2211840 | tf_op jit(solution)/shard_map/all_gather | solution.py:478
  625.6 150.2 %all-reduce.11.cloned.1.call-start = ((), (), s32[]{:S(2)}) async-start(), calls=%async_computation.26 | async-start | bytes 7340032
  640.3 306.6 %all-reduce.13.cloned.1.call-start = ((), (), s32[]{:S(2)}) async-start(), calls=%async_computation.27 | async-start | bytes 15073280
  693.3 324.1 %reduce-scatter.19.cloned.1.call-start = ((), (), s32[]{:S(2)}) async-start(), calls=%async_computation.17 | async-start | bytes 2293760 | tf_op jit(solution)/shard_map/reduce_scatter | solution.py:458
  699.3 418.1 %reduce-scatter.17.cloned.1.call-start = ((), (), s32[]{:S(2)}) async-start(), calls=%async_computation.16 | async-start | bytes 4718592 | tf_op jit(solution)/shard_map/reduce_scatter | solution.py:496
  711.0 460.4 %reduce-scatter.13.cloned.1.call-start = ((), (), s32[]{:S(2)}) async-start(), calls=%async_computation.13 | async-start | bytes 4718592 | tf_op jit(solution)/shard_map/reduce_scatter | solution.py:449
  778.7 171.4 %all-to-all-start.3 = ((bf16[8,64,864]{2,1,0:T(8,128)(2,1)}), bf16[8,64,864]{2,1,0:T(8,128)(2,1)S(1)}, u32[]{:S(2)}, u32[]{:S(2)}) async-start(bf16[8,64,864]{2,1,0:T(8,128)(2,1)} %dynamic-slice_bitcast_fusion), calls=%async_computation.7 | async-start | bytes 1835008 | tf_op jit(solution)/shard_map/all_to_all | solution.py:466
  951.1 360.2 %all-to-all-start.2 = ((bf16[8,64,1376]{2,1,0:T(8,128)(2,1)}), bf16[8,64,1376]{2,1,0:T(8,128)(2,1)S(1)}, u32[]{:S(2)}, u32[]{:S(2)}) async-start(bf16[8,64,1376]{2,1,0:T(8,128)(2,1)} %bitcast.242), calls=%async_computation.6 | async-start | bytes 2883584 | tf_op jit(solution)/shard_map/all_to_all | solution.py:507
  956.6 352.5 %reduce-scatter.21.cloned.1.call-start = ((), (), s32[]{:S(2)}) async-start(), calls=%async_computation.25 | async-start | bytes 1081344
  1034.8 19.8 %collective-permute-start.5 = (bf16[108,512]{1,0:T(8,128)(2,1)S(1)}, bf16[108,512]{1,0:T(8,128)(2,1)S(1)}, u32[]{:S(2)}, u32[]{:S(2)}) collective-permute-start(bf16[108,512]{1,0:T(8,128)(2,1)S(1)} %bitcast.292), channel_id=1, source_target_pairs={{0,0},{4,1},{8,2},{12,3},{16,4},{20,5},{24,6},{28,7},{1,8},{5,9},{... | collective-permute-start | bytes 331784 | tf_op jit(solution)/shard_map/ppermute | solution.py:526
  1038.0 19.2 %collective-permute-start.6 = (bf16[108,512]{1,0:T(8,128)(2,1)S(1)}, bf16[108,512]{1,0:T(8,128)(2,1)S(1)}, u32[]{:S(2)}, u32[]{:S(2)}) collective-permute-start(bf16[108,512]{1,0:T(8,128)(2,1)S(1)} %bitcast.288), channel_id=1, source_target_pairs={{4,0},{8,1},{12,2},{0,3},{20,4},{24,5},{28,6},{16,7},{5,8},{9,9},{... | collective-permute-start | bytes 331784 | tf_op jit(solution)/shard_map/ppermute | solution.py:526
  1039.9 20.6 %collective-permute-start.7 = (bf16[108,512]{1,0:T(8,128)(2,1)S(1)}, bf16[108,512]{1,0:T(8,128)(2,1)S(1)}, u32[]{:S(2)}, u32[]{:S(2)}) collective-permute-start(bf16[108,512]{1,0:T(8,128)(2,1)S(1)} %bitcast.287), channel_id=1, source_target_pairs={{8,0},{12,1},{0,2},{4,3},{24,4},{28,5},{16,6},{20,7},{9,8},{13,9},... | collective-permute-start | bytes 331784 | tf_op jit(solution)/shard_map/ppermute | solution.py:526
  1041.9 19.4 %collective-permute-start.8 = (bf16[108,512]{1,0:T(8,128)(2,1)S(1)}, bf16[108,512]{1,0:T(8,128)(2,1)S(1)}, u32[]{:S(2)}, u32[]{:S(2)}) collective-permute-start(bf16[108,512]{1,0:T(8,128)(2,1)S(1)} %bitcast.286), channel_id=1, source_target_pairs={{12,0},{0,1},{4,2},{8,3},{28,4},{16,5},{20,6},{24,7},{13,8},{1,9},... | collective-permute-start | bytes 331784 | tf_op jit(solution)/shard_map/ppermute | solution.py:526
  (64 other events, 971.4 us)
Sparse Core Ops, SparseCore 0:
  10.5 74.3 all-gather.24
  86.7 73.9 all-gather.26
  163.2 32.5 all-gather.18
  198.0 32.5 all-gather.28
  242.2 175.7 reduce-scatter.10
  569.1 46.1 all-gather.22
  625.7 32.4 all-gather.34
Sparse Core Ops, SparseCore 1:
  244.2 69.8 all-gather.36
  315.5 100.2 all-gather.30
  421.5 38.9 all-gather.20
  462.4 36.5 all-gather.32
  513.8 50.7 reduce-scatter.14
  640.3 135.5 all-reduce.10
  779.8 167.0 all-reduce.12
  949.2 68.2 reduce-scatter.18
  1019.7 97.6 reduce-scatter.16
  1121.1 50.2 reduce-scatter.12
  1173.5 135.6 reduce-scatter.20

commit v2 on v0

v2 whole, which is shorter than its diff:
```python
import functools
import math

import jax
import jax.numpy as jnp
from jax import lax
from jax.experimental import pallas as pl
from jax.experimental.pallas import tpu as pltpu
from jax.sharding import PartitionSpec as P

RETENTION_HEADS = 8
KEY_DIM = 256
VALUE_DIM = 432


EPSILON = 1e-06
DP, CTX, ULY = "dp", "ctx", "ulysses"
EVERYWHERE = (DP, CTX, ULY)


def entering(value, axis, join, neutral, backward):
    count, mine = (lax.axis_size(axis), lax.axis_index(axis))
    pieces = jax.tree.map(lambda part: lax.all_gather(part, axis), value)
    if backward:
        pieces = jax.tree.map(lambda part: part[::-1], pieces)
        mine = count - 1 - mine
    subtotal = jax.tree.map(
        lambda part, zero: jnp.full_like(part, 0) + jnp.asarray(zero, part.dtype), value, neutral
    )

    def step(position, subtotal):
        longer = join(subtotal, jax.tree.map(lambda part: part[position], pieces))
        return jax.tree.map(lambda new, old: jnp.where(position < mine, new, old), longer, subtotal)

    return lax.fori_loop(0, count - 1, step, subtotal)


def normalize(values):
    inverse = lax.rsqrt(jnp.mean(values * values, axis=-1, keepdims=True) + EPSILON)
    return (values * inverse, inverse)


def norm_back(grad_normed, normed, inverse):
    return inverse * (grad_normed - normed * jnp.mean(grad_normed * normed, axis=-1, keepdims=True))


def swish_slope(values):
    sigma = jax.nn.sigmoid(values)
    return sigma * (1.0 + values * (1.0 - sigma))


def carry_forward(earlier, later):
    return (earlier[0] * later[0], later[0][:, None, None] * earlier[1] + later[1])


def carry_backward(earlier, later):
    return (earlier[0] * later[0], later[1] + later[0][:, None, None] * earlier[1])


def running_sum(values):
    size = values.shape[-1]
    upper = lax.broadcasted_iota(jnp.int32, (size, size), 0) <= lax.broadcasted_iota(
        jnp.int32, (size, size), 1
    )
    return jnp.dot(values, upper.astype(jnp.float32), precision=lax.Precision.HIGHEST)


def matmul(left, right):
    return jnp.dot(left, right, preferred_element_type=jnp.float32)


def local_any(
    hidden_in,
    cotangent,
    log_decay,
    w_query,
    w_key,
    w_value,
    w_swish,
    w_output,
    w_gate,
    w_up,
    w_down,
    gain_attn,
    gain_ffn,
):
    highest = lax.Precision.HIGHEST
    query_full, key_full, value_full, swish_full, output_full, gain_one = (
        lax.all_gather(w_query, EVERYWHERE, axis=0, tiled=True),
        lax.all_gather(w_key, EVERYWHERE, axis=0, tiled=True),
        lax.all_gather(w_value, EVERYWHERE, axis=0, tiled=True),
        lax.all_gather(w_swish, EVERYWHERE, axis=0, tiled=True),
        lax.all_gather(w_output, EVERYWHERE, axis=0, tiled=True),
        lax.all_gather(gain_attn, EVERYWHERE, axis=0, tiled=True),
    )
    inputs = hidden_in[0].astype(jnp.float32)
    tokens = inputs.shape[0]
    normed_one, inverse_one = normalize(inputs)
    scaled_one = (normed_one * gain_one.astype(jnp.float32)).astype(jnp.bfloat16)
    queries = (
        matmul(scaled_one, query_full)
        .astype(jnp.bfloat16)
        .reshape(tokens, RETENTION_HEADS, KEY_DIM)
    )
    keys_tok = (
        matmul(scaled_one, key_full).astype(jnp.bfloat16).reshape(tokens, RETENTION_HEADS, KEY_DIM)
    )
    values_tok = (
        matmul(scaled_one, value_full)
        .astype(jnp.bfloat16)
        .reshape(tokens, RETENTION_HEADS, VALUE_DIM)
    )
    swish_pre = matmul(scaled_one, swish_full)
    head_q, head_k, head_v = (
        lax.all_to_all(queries, ULY, split_axis=1, concat_axis=0, tiled=True),
        lax.all_to_all(keys_tok, ULY, split_axis=1, concat_axis=0, tiled=True),
        lax.all_to_all(values_tok, ULY, split_axis=1, concat_axis=0, tiled=True),
    )
    block = head_q.shape[0]
    scale = 1.0 / math.sqrt(KEY_DIM)
    cumulative = running_sum(log_decay[0])
    later = lax.broadcasted_iota(jnp.int32, (block, block), 0) >= lax.broadcasted_iota(
        jnp.int32, (block, block), 1
    )
    gap = cumulative[:, :, None] - cumulative[:, None, :]
    mask = jnp.where(later[None], jnp.exp(jnp.minimum(gap, 0.0)), 0.0) * scale
    scores = jnp.einsum("thd,shd->hts", head_q, head_k, preferred_element_type=jnp.float32)
    weights = (scores * mask).astype(jnp.bfloat16)
    intra = jnp.einsum("hts,she->the", weights, head_v, preferred_element_type=jnp.float32)
    query_f = head_q.astype(jnp.float32)
    key_f = head_k.astype(jnp.float32)
    value_f = head_v.astype(jnp.float32)
    tail = jnp.exp(cumulative[:, -1:] - cumulative).T[:, :, None]
    reach = jnp.exp(cumulative).T[:, :, None]
    update = jnp.einsum("shd,she->hde", key_f * tail, value_f, precision=highest)
    block_decay = jnp.exp(cumulative[:, -1])
    identity = (jnp.ones_like(block_decay), jnp.zeros_like(update))
    _, state_in = entering((block_decay, update), CTX, carry_forward, identity, False)
    retained = intra + scale * reach * jnp.einsum(
        "thd,hde->the", query_f, state_in, precision=highest
    )
    head_normed, head_inverse = normalize(retained)
    head_out = head_normed.astype(jnp.bfloat16)
    token_out = lax.all_to_all(
        head_out, ULY, split_axis=0, concat_axis=1, tiled=True
    ).reshape(tokens, RETENTION_HEADS * VALUE_DIM)
    token_out_f = token_out.astype(jnp.float32)
    swish_act = jax.nn.silu(swish_pre)
    gated = (swish_act * token_out_f).astype(jnp.bfloat16)
    residual = inputs + matmul(gated, output_full)
    gate_full, up_full, down_full, gain_two = (
        lax.all_gather(w_gate, EVERYWHERE, axis=0, tiled=True),
        lax.all_gather(w_up, EVERYWHERE, axis=0, tiled=True),
        lax.all_gather(w_down, EVERYWHERE, axis=0, tiled=True),
        lax.all_gather(gain_ffn, EVERYWHERE, axis=0, tiled=True),
    )
    normed_two, inverse_two = normalize(residual)
    scaled_two = (normed_two * gain_two.astype(jnp.float32)).astype(jnp.bfloat16)
    gate_pre = matmul(scaled_two, gate_full)
    up_pre = matmul(scaled_two, up_full)
    product = (jax.nn.silu(gate_pre) * up_pre).astype(jnp.bfloat16)
    layer_out = residual + matmul(product, down_full)
    grad_top = cotangent[0].astype(jnp.float32)
    grad_top_low = grad_top.astype(jnp.bfloat16)
    grad_product = matmul(grad_top_low, down_full.T)
    grad_down_term = matmul(product.T, grad_top_low)
    grad_gate_pre = (grad_product * up_pre * swish_slope(gate_pre)).astype(jnp.bfloat16)
    grad_up_pre = (grad_product * jax.nn.silu(gate_pre)).astype(jnp.bfloat16)
    grad_gate_term = matmul(scaled_two.T, grad_gate_pre)
    grad_up_term = matmul(scaled_two.T, grad_up_pre)
    grad_scaled_two = matmul(grad_gate_pre, gate_full.T) + matmul(grad_up_pre, up_full.T)
    grad_gain_two = jnp.sum(grad_scaled_two * normed_two, axis=0)
    grad_residual = grad_top + norm_back(
        grad_scaled_two * gain_two.astype(jnp.float32), normed_two, inverse_two
    )
    grad_gate, grad_up, grad_down, grad_gain_ffn = (
        lax.psum_scatter(grad_gate_term, EVERYWHERE, scatter_dimension=0, tiled=True),
        lax.psum_scatter(grad_up_term, EVERYWHERE, scatter_dimension=0, tiled=True),
        lax.psum_scatter(grad_down_term, EVERYWHERE, scatter_dimension=0, tiled=True),
        lax.psum_scatter(grad_gain_two, EVERYWHERE, scatter_dimension=0, tiled=True),
    )
    grad_y = grad_residual.astype(jnp.bfloat16)
    grad_output_term = matmul(gated.T, grad_y)
    grad_gated = matmul(grad_y, output_full.T)
    grad_swish_pre = (grad_gated * token_out_f * swish_slope(swish_pre)).astype(jnp.bfloat16)
    grad_token_out = (
        (grad_gated * swish_act).astype(jnp.bfloat16).reshape(tokens, RETENTION_HEADS, VALUE_DIM)
    )
    grad_swish_term = matmul(scaled_one.T, grad_swish_pre)
    grad_head_out = lax.all_to_all(
        grad_token_out, ULY, split_axis=1, concat_axis=0, tiled=True
    ).astype(jnp.float32)
    grad_retained = norm_back(grad_head_out, head_normed, head_inverse).astype(jnp.bfloat16)
    grad_retained_f = grad_retained.astype(jnp.float32)
    grad_weights = jnp.einsum(
        "the,she->hts", grad_retained, head_v, preferred_element_type=jnp.float32
    )
    grad_scores = (grad_weights * mask).astype(jnp.bfloat16)
    grad_state_in = scale * jnp.einsum(
        "thd,the->hde", query_f * reach, grad_retained_f, precision=highest
    )
    _, grad_update = entering((block_decay, grad_state_in), CTX, carry_backward, identity, True)
    grad_head_q = jnp.einsum(
        "hts,shd->thd", grad_scores, head_k, preferred_element_type=jnp.float32
    ) + scale * reach * jnp.einsum("the,hde->thd", grad_retained_f, state_in, precision=highest)
    grad_head_k = jnp.einsum(
        "hts,thd->shd", grad_scores, head_q, preferred_element_type=jnp.float32
    ) + tail * jnp.einsum("she,hde->shd", value_f, grad_update, precision=highest)
    grad_head_v = jnp.einsum(
        "hts,the->she", weights, grad_retained, preferred_element_type=jnp.float32
    ) + tail * jnp.einsum("shd,hde->she", key_f, grad_update, precision=highest)
    grad_queries, grad_keys, grad_values = (
        lax.all_to_all(
            grad_head_q.astype(jnp.bfloat16), ULY, split_axis=0, concat_axis=1, tiled=True
        ),
        lax.all_to_all(
            grad_head_k.astype(jnp.bfloat16), ULY, split_axis=0, concat_axis=1, tiled=True
        ),
        lax.all_to_all(
            grad_head_v.astype(jnp.bfloat16), ULY, split_axis=0, concat_axis=1, tiled=True
        ),
    )
    grad_queries = grad_queries.reshape(tokens, RETENTION_HEADS * KEY_DIM)
    grad_keys = grad_keys.reshape(tokens, RETENTION_HEADS * KEY_DIM)
    grad_values = grad_values.reshape(tokens, RETENTION_HEADS * VALUE_DIM)
    grad_query_term = matmul(scaled_one.T, grad_queries)
    grad_key_term = matmul(scaled_one.T, grad_keys)
    grad_value_term = matmul(scaled_one.T, grad_values)
    grad_scaled_one = (
        matmul(grad_queries, query_full.T)
        + matmul(grad_keys, key_full.T)
        + matmul(grad_values, value_full.T)
        + matmul(grad_swish_pre, swish_full.T)
    )
    grad_gain_one = jnp.sum(grad_scaled_one * normed_one, axis=0)
    grad_input = grad_residual + norm_back(
        grad_scaled_one * gain_one.astype(jnp.float32), normed_one, inverse_one
    )
    grad_query, grad_key, grad_value, grad_swish, grad_output, grad_gain_attn = (
        lax.psum_scatter(
            grad_query_term, EVERYWHERE, scatter_dimension=0, tiled=True
        ),
        lax.psum_scatter(grad_key_term, EVERYWHERE, scatter_dimension=0, tiled=True),
        lax.psum_scatter(
            grad_value_term, EVERYWHERE, scatter_dimension=0, tiled=True
        ),
        lax.psum_scatter(
            grad_swish_term, EVERYWHERE, scatter_dimension=0, tiled=True
        ),
        lax.psum_scatter(
            grad_output_term, EVERYWHERE, scatter_dimension=0, tiled=True
        ),
        lax.psum_scatter(grad_gain_one, EVERYWHERE, scatter_dimension=0, tiled=True),
    )
    return (
        layer_out[None],
        grad_input[None],
        grad_query,
        grad_key,
        grad_value,
        grad_swish,
        grad_output,
        grad_gate,
        grad_up,
        grad_down,
        grad_gain_attn,
        grad_gain_ffn,
    )


MESH = pl.DeviceIdType.MESH
BF16, F32 = jnp.bfloat16, jnp.float32
HBM, VMEM = pltpu.HBM, pltpu.VMEM
N_SEMS = 160


def dot_t(left, right):
    return lax.dot_general(left, right, (((0,), (0,)), ((), ())), preferred_element_type=F32)


def dot_nt(left, right):
    return lax.dot_general(left, right, (((1,), (1,)), ((), ())), preferred_element_type=F32)


def pair_dot(left_axis, right_axis, left, right):
    dims = (((left_axis,), (right_axis,)), ((0,), (0,)))
    return lax.dot_general(left, right, dims, preferred_element_type=F32)


class Place:
    def __init__(self, uly):
        self.dp, self.ctx, self.uly = lax.axis_index(DP), lax.axis_index(CTX), uly
        odd = lax.rem(self.ctx, 2)
        self.xn = self.ctx + 1 - 2 * odd
        self.yn = lax.rem(self.ctx + 2, 4)
        self.dg = self.yn + 1 - 2 * odd
        self.other = 1 - self.dp

    def at(self, dp=None, ctx=None, uly=None):
        return (
            self.dp if dp is None else dp,
            self.ctx if ctx is None else ctx,
            self.uly if uly is None else uly,
        )


class Mover:
    def __init__(self, place, names, send, recv):
        self.place, self.names, self.send_sems, self.recv_sems = place, names, send, recv
        self.sent = []

    def number(self, name):
        return self.names.setdefault(name, len(self.names))

    def remote(self, name, src, dst, device):
        k = self.number(name)
        return pltpu.make_async_remote_copy(
            src_ref=src,
            dst_ref=dst,
            send_sem=self.send_sems.at[k],
            recv_sem=self.recv_sems.at[k],
            device_id=device,
            device_id_type=MESH,
        )

    def send(self, name, src, dst, device):
        copy = self.remote(name, src, dst, device)
        copy.start()
        self.sent.append(copy)

    def arrive(self, name, dst):
        self.remote(name, dst, dst, self.place.at(dp=self.place.other)).wait_recv()

    def local(self, name, src, dst):
        copy = pltpu.make_async_copy(src, dst, self.send_sems.at[self.number(name)])
        copy.start()
        return copy

    def finish(self):
        for copy in self.sent:
            copy.wait_send()


def greet(devices):
    barrier = pltpu.get_barrier_semaphore()
    for device in devices:
        pl.semaphore_signal(barrier, inc=1, device_id=device, device_id_type=MESH)
    pl.semaphore_wait(barrier, len(devices))


def together(streams):
    streams = list(streams)
    while streams:
        left = []
        for stream in streams:
            if next(stream, 0) is None:
                left.append(stream)
        streams = left


def later(stream, stages):
    for _ in range(stages):
        yield
    yield from stream


def add_up(dst, sources, step=32):
    rows, columns = dst.shape
    by_rows = rows % step == 0
    step = step if by_rows else 256

    def body(i, carry):
        part = pl.ds(pl.multiple_of(i * step, step), step)
        at = (part, slice(None)) if by_rows else (slice(None), part)
        total = sources[0][at].astype(F32)
        for source in sources[1:]:
            total = total + source[at].astype(F32)
        dst[at] = total.astype(dst.dtype)
        return carry

    lax.fori_loop(0, (rows if by_rows else columns) // step, body, 0)


def line_gather(m, tag, own, out, pause=1):
    p = m.place
    u = p.uly
    copy = m.local(tag + "=", own, out.at[p.dp * 4 + u])
    if u < 3:
        m.send((tag, "r", u), own, out.at[p.dp * 4 + u], p.at(uly=u + 1))
    if u > 0:
        m.send((tag, "l", u), own, out.at[p.dp * 4 + u], p.at(uly=u - 1))
    m.send((tag, "c", u), own, out.at[p.dp * 4 + u], p.at(dp=p.other))
    for _ in range(pause):
        yield
    for d in range(1, 4):
        for way, b, onward in (("r", u - d, u + 1), ("l", u + d, u - 1)):
            if 0 <= b <= 3:
                block = out.at[p.dp * 4 + b]
                m.arrive((tag, way, b), block)
                if 0 <= onward <= 3:
                    m.send((tag, way, b), block, block, p.at(uly=onward))
                m.send((tag, "c", b), block, block, p.at(dp=p.other))
        yield
    for b in range(4):
        m.arrive((tag, "c", b), out.at[p.other * 4 + b])
    copy.wait()


def plane_gather(m, tag, own, out, slot, halves, pair=True):
    p = m.place

    def half(c, i):
        return slot(out, p.dp, c, halves[i])

    mine = slot(out, p.dp, p.ctx, None)
    copy = m.local(tag + "=", own, mine)
    m.send((tag, "x"), own, mine, p.at(ctx=p.xn))
    m.send((tag, "y"), own, mine, p.at(ctx=p.yn))
    if pair:
        m.send((tag, "c", 0), own, mine, p.at(dp=p.other))
    yield
    block = slot(out, p.dp, p.xn, None)
    m.arrive((tag, "x"), block)
    m.send((tag, "z", 0), half(p.xn, 0), half(p.xn, 0), p.at(ctx=p.yn))
    if pair:
        m.send((tag, "c", 1), block, block, p.at(dp=p.other))
    block = slot(out, p.dp, p.yn, None)
    m.arrive((tag, "y"), block)
    m.send((tag, "z", 1), half(p.yn, 1), half(p.yn, 1), p.at(ctx=p.xn))
    if pair:
        m.send((tag, "c", 2), block, block, p.at(dp=p.other))
    yield
    for i in range(2):
        block = half(p.dg, i)
        m.arrive((tag, "z", i), block)
        if pair:
            m.send((tag, "c", 3 + i), block, block, p.at(dp=p.other))
    yield
    if pair:
        for i, c in enumerate((p.ctx, p.xn, p.yn)):
            m.arrive((tag, "c", i), slot(out, p.other, c, None))
        for i in range(2):
            m.arrive((tag, "c", 3 + i), slot(out, p.other, p.dg, halves[i]))
    copy.wait()


def line_reduce(m, tag, part, out, sib, right, left, sums):
    p = m.place
    u = p.uly
    order = (3, 0, 2, 1) if u < 2 else (0, 3, 1, 2)
    for b in order if sib is not None else ():
        m.send((tag, "c", b), part.at[p.other * 4 + b], sib.at[b], p.at(dp=p.other))
    met = set()

    def meet(b):
        if sib is None:
            return [part.at[b]]
        if b not in met:
            met.add(b)
            m.arrive((tag, "c", b), sib.at[b])
        return [part.at[p.dp * 4 + b], sib.at[b]]

    for slot in range(3):
        for b in range(1, 4):
            if u < b and u + 3 - b == slot:
                terms = meet(b)
                if u > 0:
                    m.arrive((tag, "r", b), right.at[b])
                    terms.append(right.at[b])
                add_up(sums.at[b], terms)
                m.send((tag, "r", b), sums.at[b], right.at[b], p.at(uly=u + 1))
        for b in range(3):
            if u > b and 3 - u + b == slot:
                terms = meet(b)
                if u < 3:
                    m.arrive((tag, "l", b), left.at[b])
                    terms.append(left.at[b])
                add_up(sums.at[b], terms)
                m.send((tag, "l", b), sums.at[b], left.at[b], p.at(uly=u - 1))
        yield
    terms = meet(u)
    if u > 0:
        m.arrive((tag, "r", u), right.at[u])
        terms.append(right.at[u])
    if u < 3:
        m.arrive((tag, "l", u), left.at[u])
        terms.append(left.at[u])
    add_up(out, terms)


def plane_reduce(m, tag, part, out, sib, sums, got, got2):
    p = m.place
    rows = out.shape[0]
    halves = (pl.ds(0, rows // 2), pl.ds(rows // 2, rows // 2))
    order = (p.dg, p.xn, p.yn, p.ctx)
    for i, c in enumerate(order):
        m.send((tag, "c", i), part.at[p.other * 4 + c], sib.at[c], p.at(dp=p.other))
    yield
    for i, c in enumerate(order):
        m.arrive((tag, "c", i), sib.at[c])
        add_up(sums.at[c], [part.at[p.dp * 4 + c], sib.at[c]])
        if i == 0:
            m.send((tag, "x", 1), sums.at[c, halves[0]], got.at[1, halves[0]], p.at(ctx=p.xn))
            m.send((tag, "y", 1), sums.at[c, halves[1]], got.at[1, halves[1]], p.at(ctx=p.yn))
        if i == 1:
            m.send((tag, "x", 0), sums.at[c, halves[0]], got.at[0, halves[0]], p.at(ctx=p.xn))
        if i == 2:
            m.send((tag, "y", 0), sums.at[c, halves[1]], got.at[0, halves[1]], p.at(ctx=p.yn))
    yield
    m.arrive((tag, "x", 1), got.at[1, halves[0]])
    add_up(got.at[1, halves[0]], [sums.at[p.yn, halves[0]], got.at[1, halves[0]]])
    m.send((tag, "y2"), got.at[1, halves[0]], got2.at[halves[0]], p.at(ctx=p.yn))
    m.arrive((tag, "y", 1), got.at[1, halves[1]])
    add_up(got.at[1, halves[1]], [sums.at[p.xn, halves[1]], got.at[1, halves[1]]])
    m.send((tag, "x2"), got.at[1, halves[1]], got2.at[halves[1]], p.at(ctx=p.xn))
    yield
    m.arrive((tag, "x", 0), got.at[0, halves[0]])
    m.arrive((tag, "y", 0), got.at[0, halves[1]])
    yield
    m.arrive((tag, "y2"), got2.at[halves[0]])
    m.arrive((tag, "x2"), got2.at[halves[1]])
    add_up(out, [sums.at[p.ctx], got.at[0], got2])


def run_kernel(name, number, branches, partners, streams, outs, ins, scratch=(), vmem=48, time=40):
    def kernel(*refs):
        send, recv = refs[-2:]
        refs = refs[:-2]
        uly = lax.axis_index(ULY)
        names = {}
        greet(partners(Place(uly)) if partners else [])

        def body(u):
            m = Mover(Place(u), names, send, recv)
            together(streams(m, *refs))
            m.finish()

        if branches == 1:
            body(uly)
        else:
            for u in range(4):
                pl.when(uly == u)(functools.partial(body, u))
        assert len(names) <= N_SEMS

    return pl.pallas_call(
        kernel,
        out_shape=[jax.ShapeDtypeStruct(*o[:2]) for o in outs],
        in_specs=[pl.BlockSpec(memory_space=s) for _, s in ins],
        out_specs=[pl.BlockSpec(memory_space=o[2]) for o in outs],
        scratch_shapes=[
            *[pltpu.VMEM(shape, dtype) for shape, dtype in scratch],
            pltpu.SemaphoreType.DMA((N_SEMS,)),
            pltpu.SemaphoreType.DMA((N_SEMS,)),
        ],
        name=name,
        cost_estimate=pl.CostEstimate(
            flops=0, bytes_accessed=time * 3_700_000, transcendentals=0
        ),
        compiler_params=pltpu.CompilerParams(
            collective_id=number, has_side_effects=True, vmem_limit_bytes=vmem << 20
        ),
    )(*[a for a, _ in ins])


def everyone(p):
    me = p.dp * 16 + p.ctx * 4 + p.uly
    found = []
    for k in range(1, 32):
        there = lax.rem(me + k, 32)
        found.append((lax.div(there, 16), lax.rem(lax.div(there, 4), 4), lax.rem(there, 4)))
    return found


def line_partners(p):
    found = [p.at(dp=p.other)]
    for d in range(1, 4):
        there = lax.rem(p.uly + d, 4)
        found += [p.at(uly=there), p.at(dp=p.other, uly=there)]
    return found


def plane_partners(p):
    return [p.at(dp=p.other), p.at(ctx=p.xn), p.at(ctx=p.yn)]


def token_slot(out, dp, c, part):
    view = out.at[dp * 4 + c]
    return view if part is None else view.at[part]


def state_slot(out, dp, c, part):
    view = out.at[c]
    return view if part is None else view.at[part]


def pack(w_query, w_key, w_value, w_swish, w_output, w_gate, w_up, gains):
    rows, (out_rows, width) = w_query.shape[0], w_output.shape
    key, val, ff, quarter = KEY_DIM, VALUE_DIM, w_gate.shape[1] // 8, width // 4
    cols = 2 * key + 2 * val + 32

    def kernel(q, k, v, s, o, g, u, n, packed, outw, gu):
        for d in range(2):
            for z in range(4):
                h, i = 2 * z + d, 4 * d + z
                at = 0
                for ref, w in ((q, key), (k, key), (v, val), (s, val)):
                    packed[i, :, at : at + w] = ref[:, h * w : (h + 1) * w]
                    at += w
                packed[i, :, at : at + 32] = n[...]
        for i in range(8):
            gu[i, :, :ff] = g[:, i * ff : (i + 1) * ff]
            gu[i, :, ff:] = u[:, i * ff : (i + 1) * ff]
        for j in range(4):
            outw[j] = o[:, j * quarter : (j + 1) * quarter]

    return pl.pallas_call(
        kernel,
        out_shape=[
            jax.ShapeDtypeStruct((8, rows, cols), BF16),
            jax.ShapeDtypeStruct((4, out_rows, quarter), BF16),
            jax.ShapeDtypeStruct((8, rows, 2 * ff), BF16),
        ],
        name="pack",
        compiler_params=pltpu.CompilerParams(vmem_limit_bytes=32 << 20),
    )(w_query, w_key, w_value, w_swish, w_output, w_gate, w_up, gains)


def unpack(heads, outg, slices):
    rows, (_, out_rows, quarter) = heads.shape[1], outg.shape
    key, val, ff = KEY_DIM, VALUE_DIM, slices.shape[2] // 2

    def kernel(hs, og, sl, q, k, v, s, o, g, u):
        for d in range(2):
            for z in range(4):
                h, i = 2 * z + d, 4 * d + z
                at = 0
                for ref, w in ((q, key), (k, key), (v, val), (s, val)):
                    ref[:, h * w : (h + 1) * w] = hs[i, :, at : at + w].astype(F32)
                    at += w
        for i in range(8):
            g[:, i * ff : (i + 1) * ff] = sl[i, :, :ff].astype(F32)
            u[:, i * ff : (i + 1) * ff] = sl[i, :, ff:].astype(F32)
        for j in range(4):
            o[:, j * quarter : (j + 1) * quarter] = og[j].astype(F32)

    wide = jax.ShapeDtypeStruct((rows, 8 * key), F32)
    wider = jax.ShapeDtypeStruct((rows, 8 * val), F32)
    ffs = jax.ShapeDtypeStruct((rows, 8 * ff), F32)
    return pl.pallas_call(
        kernel,
        out_shape=[
            wide, wide, wider, wider,
            jax.ShapeDtypeStruct((out_rows, 4 * quarter), F32),
            ffs, ffs,
        ],
        name="unpack",
        compiler_params=pltpu.CompilerParams(vmem_limit_bytes=32 << 20),
    )(heads, outg, slices)


def start_exchange(hidden, decay, packed, outw, gu):
    tokens, width = hidden.shape
    rows, cols = packed.shape[1:]
    out_rows, quarter = outw.shape[1:]
    ff2 = gu.shape[2]

    def streams(m, hid_ref, dec_ref, pk_ref, ow_ref, gu_ref, hall, dall, wall, oall, gall):
        p = m.place
        u = p.uly

        def row(q, c, us):
            dp = p.dp if q == 0 else p.other
            return wall.at[dp * 16 + c * 4 + us]

        def attn():
            sources = sorted(
                ((q, us) for q in range(2) for us in range(4)), key=lambda s: (abs(s[1] - u), s[0])
            )
            copy = None
            for q, to in sources:
                dp = p.dp if q == 0 else p.other
                mine = row(0, p.ctx, u)
                src = pk_ref.at[dp * 4 + to]
                if (q, to) == (0, u):
                    copy = m.local("T", src, mine)
                else:
                    m.send(("t", q, u), src, mine, p.at(dp=dp, uly=to))
            yield
            relays = []
            for n, (q, us) in enumerate(sources):
                tile = row(q, p.ctx, us)
                if (q, us) == (0, u):
                    copy.wait()
                else:
                    m.arrive(("t", q, us), tile)
                m.send(("X", q, us), tile, tile, p.at(ctx=p.xn))
                m.send(("Y", q, us), tile, tile, p.at(ctx=p.yn))
                relays.append((q, us))
                if n >= 2:
                    yield
                    relay(*relays.pop(0))
            while relays:
                yield
                relay(*relays.pop(0))
            yield
            for q, us in sources:
                even = (q + us) % 2 == 0
                m.arrive(("Y" if even else "X", q, us), row(q, p.yn if even else p.xn, us))
                m.arrive(("Z", q, us), row(q, p.dg, us))

        def relay(q, us):
            if (q + us) % 2 == 0:
                tile = row(q, p.xn, us)
                m.arrive(("X", q, us), tile)
                m.send(("Z", q, us), tile, tile, p.at(ctx=p.yn))
            else:
                tile = row(q, p.yn, us)
                m.arrive(("Y", q, us), tile)
                m.send(("Z", q, us), tile, tile, p.at(ctx=p.xn))

        def out_proj():
            head_dp, head_u = lax.rem(p.ctx, 2), p.dp * 2 + lax.div(p.ctx, 2)
            source_dp, source_ctx = u // 2, 2 * (u % 2) + p.dp

            def column(part, c):
                return oall.at[part, :, pl.ds(pl.multiple_of(c * quarter, quarter), quarter)]

            own = [
                (head_dp == p.dp) & (p.ctx == j) & (head_u == u) for j in range(4)
            ]
            for j in range(4):
                there = oall.at[u, :, pl.ds(j * quarter, quarter)]
                here = pltpu.make_async_copy(
                    ow_ref.at[j], there, m.send_sems.at[m.number("O")]
                )

                @pl.when(own[j])
                def _(here=here):
                    here.start()
                    here.wait()

                other = pltpu.make_async_remote_copy(
                    src_ref=ow_ref.at[j],
                    dst_ref=there,
                    send_sem=m.send_sems.at[m.number(("S", j))],
                    recv_sem=m.recv_sems.at[m.number(("o", u))],
                    device_id=(head_dp, j, head_u),
                    device_id_type=MESH,
                )
                pl.when(jnp.logical_not(own[j]))(other.start)
            for _ in range(7):
                yield
            for us in range(4):
                mine = (source_dp == p.dp) & (source_ctx == p.ctx) & (us == u)

                @pl.when(jnp.logical_not(mine))
                def _(us=us):
                    m.arrive(("o", us), column(us, p.ctx))

            yield
            mine = column(pl.ds(0, 4), p.ctx)
            m.send("ox", mine, mine, p.at(ctx=p.xn))
            m.send("oy", mine, mine, p.at(ctx=p.yn))
            yield
            low, high = pl.ds(0, 2), pl.ds(2, 2)
            m.arrive("ox", column(pl.ds(0, 4), p.xn))
            m.send("o0", column(low, p.xn), column(low, p.xn), p.at(ctx=p.yn))
            m.arrive("oy", column(pl.ds(0, 4), p.yn))
            m.send("o1", column(high, p.yn), column(high, p.yn), p.at(ctx=p.xn))
            yield
            for j in range(4):
                other = pltpu.make_async_remote_copy(
                    src_ref=ow_ref.at[j],
                    dst_ref=ow_ref.at[j],
                    send_sem=m.send_sems.at[m.number(("S", j))],
                    recv_sem=m.recv_sems.at[m.number(("o", u))],
                    device_id=p.at(dp=p.other),
                    device_id_type=MESH,
                )
                pl.when(jnp.logical_not(own[j]))(other.wait_send)
            m.arrive("o0", column(low, p.dg))
            m.arrive("o1", column(high, p.dg))

        def feed():
            mine = gall.at[p.dp * 4 + p.ctx]
            copy = m.local("F", gu_ref.at[p.dp * 4 + p.ctx], mine)
            decays = m.local("D", dec_ref, dall.at[p.dp * 4 + p.ctx])
            spots = [(q, c, i) for i, c in enumerate((p.ctx, p.xn, p.yn, p.dg)) for q in range(2)][1:]
            for q, c, i in spots:
                dp = p.dp if q == 0 else p.other
                m.send(("d", q, i), dec_ref, dall.at[p.dp * 4 + p.ctx], p.at(dp=dp, ctx=c))
                m.send(("f", q, i), gu_ref.at[dp * 4 + c], mine, p.at(dp=dp, ctx=c))
            for _ in range(5):
                yield
            for q, c, i in spots:
                dp = p.dp if q == 0 else p.other
                m.arrive(("d", q, i), dall.at[dp * 4 + c])
                m.arrive(("f", q, i), gall.at[dp * 4 + c])
            copy.wait()
            decays.wait()

        return [
            attn(),
            later(line_gather(m, "h", hid_ref, hall, 6), 1),
            later(out_proj(), 1),
            later(feed(), 6),
        ]

    return run_kernel(
        "start",
        1,
        4,
        everyone,
        streams,
        [
            ((8, tokens, width), BF16, HBM),
            ((8, *decay.shape), F32, HBM),
            ((32, rows, cols), BF16, HBM),
            ((4, out_rows, 4 * quarter), BF16, HBM),
            ((8, rows, ff2), BF16, HBM),
        ],
        [(hidden, HBM), (decay, HBM), (packed, HBM), (outw, HBM), (gu, HBM)],
    )


def state_exchange(state, number):
    def streams(m, own, out):
        return [
            plane_gather(m, "s", own, out, state_slot, (pl.ds(0, 1), pl.ds(1, 1)), pair=False)
        ]

    [out] = run_kernel(
        "state",
        number,
        1,
        lambda p: [p.at(ctx=p.xn), p.at(ctx=p.yn)],
        streams,
        [((4, *state.shape), state.dtype, HBM)],
        [(state, HBM)],
    )
    return out


def reduce_line(part, cot, number):
    _, tokens, width = part.shape
    half = tokens // 2

    def streams(m, part_ref, cot_ref, out, cots, sib, right, left, sums):
        return [
            line_reduce(m, "s", part_ref, out, sib, right, left, sums),
            plane_gather(m, "C", cot_ref, cots, token_slot, (pl.ds(0, half), pl.ds(half, half))),
        ]

    return run_kernel(
        "reduce_line",
        number,
        4,
        lambda p: line_partners(p) + plane_partners(p)[1:],
        streams,
        [((tokens, width), F32, VMEM), ((8, tokens, width), BF16, HBM)],
        [(part, VMEM), (cot, HBM)],
        [((4, tokens, width), BF16)] * 4,
    )


def gather_plane(own, number):
    tokens, width = own.shape
    half = tokens // 2

    def streams(m, own_ref, out):
        return [
            plane_gather(
                m, "k", own_ref, out, token_slot, (pl.ds(0, half), pl.ds(half, half))
            )
        ]

    [out] = run_kernel(
        "gather_plane",
        number,
        1,
        plane_partners,
        streams,
        [((8, tokens, width), BF16, HBM)],
        [(own, VMEM)],
    )
    return out


def reduce_plane(part, number):
    _, tokens, width = part.shape

    def streams(m, part_ref, out, sib, sums, got, got2):
        return [plane_reduce(m, "s", part_ref, out, sib, sums, got, got2)]

    [out] = run_kernel(
        "reduce_plane",
        number,
        1,
        plane_partners,
        streams,
        [((tokens, width), F32, VMEM)],
        [(part, VMEM)],
        [
            ((4, tokens, width), BF16),
            ((4, tokens, width), BF16),
            ((2, tokens, width), BF16),
            ((tokens, width), BF16),
        ],
    )
    return out


def gather_line_reduce_plane(own, part, down, gates, number):
    _, tokens, width = part.shape
    shapes = [g.shape for g in (down, *gates)]

    def streams(m, own_ref, part_ref, d_ref, g_ref, h_ref, out, total, dout, gout, hout, *scratch):
        sib, sums, got, got2 = scratch[:4]
        more = scratch[4:]
        return [
            line_gather(m, "k", own_ref, out),
            plane_reduce(m, "s", part_ref, total, sib, sums, got, got2),
            *[
                line_reduce(m, i, ref, o, None, *more[3 * i : 3 * i + 3])
                for i, (ref, o) in enumerate(((d_ref, dout), (g_ref, gout), (h_ref, hout)))
            ],
        ]

    return run_kernel(
        "gather_line",
        number,
        4,
        lambda p: line_partners(p) + plane_partners(p)[1:],
        streams,
        [
            ((8, tokens, width), BF16, HBM),
            ((tokens, width), F32, VMEM),
            (shapes[0][1:], F32, VMEM),
            (shapes[1][1:], BF16, VMEM),
            (shapes[2][1:], BF16, VMEM),
        ],
        [(own, VMEM), (part, VMEM), (down, VMEM), (gates[0], VMEM), (gates[1], VMEM)],
        [
            ((4, tokens, width), BF16),
            ((4, tokens, width), BF16),
            ((2, tokens, width), BF16),
            ((tokens, width), BF16),
            *[(shape, BF16) for shape in shapes for _ in range(3)],
        ],
        vmem=56,
    )


def last_exchange(part, grads, gout, gffn, inputs, term):
    _, tokens, width = part.shape
    rows, cols = grads.shape[3:]
    out_rows = gout.shape[1]
    quarter = width // 4
    ff2 = gffn.shape[2]

    def streams(
        m, part_ref, g_ref, o_ref, f_ref, in_ref, t_ref, out, gall, oall, fall, gains,
        sib, right, left, sums, gotx, goty, gotx2, goty2, oxs, oys, ox2, oy2, away,
    ):
        p = m.place
        u = p.uly

        def attn():
            for i, (cx, cy) in ((1, (p.dg, p.dg)), (0, (p.xn, p.yn))):
                for t in range(4):
                    m.send(("gx", i, t), g_ref.at[0, cx, t], gotx.at[i, t], p.at(ctx=p.xn))
                    m.send(("gy", i, t), g_ref.at[1, cy, t], goty.at[i, t], p.at(ctx=p.yn))
            yield
            for t in range(4):
                m.arrive(("gx", 1, t), gotx.at[1, t])
                add_up(gotx.at[1, t], [g_ref.at[0, p.yn, t], gotx.at[1, t]])
                m.send(("gy2", t), gotx.at[1, t], goty2.at[t], p.at(ctx=p.yn))
                m.arrive(("gy", 1, t), goty.at[1, t])
                add_up(goty.at[1, t], [g_ref.at[1, p.xn, t], goty.at[1, t]])
                m.send(("gx2", t), goty.at[1, t], gotx2.at[t], p.at(ctx=p.xn))
            yield
            yield
            for t in range(4):
                for dp, got, got2, tags in (
                    (0, gotx, goty2, ("gx", "gy2")),
                    (1, goty, gotx2, ("gy", "gx2")),
                ):
                    m.arrive((tags[0], 0, t), got.at[0, t])
                    m.arrive((tags[1], t), got2.at[t])
                    add_up(got.at[0, t], [g_ref.at[dp, p.ctx, t], got.at[0, t], got2.at[t]])
                    there = gall.at[p.dp * 4 + u]
                    if t == u:

                        @pl.when(p.dp == dp)
                        def _(got=got, there=there):
                            here = pltpu.make_async_copy(
                                got.at[0, u], there, m.send_sems.at[m.number("G")]
                            )
                            here.start()
                            here.wait()

                        @pl.when(p.dp != dp)
                        def _(got=got, there=there, dp=dp):
                            m.remote(
                                ("gc", u), got.at[0, u], there, (dp, p.ctx, u)
                            ).start()
                    else:
                        k = m.number(("gs", dp, t))
                        copies = []
                        for q in range(2):
                            copies.append(
                                pltpu.make_async_remote_copy(
                                    src_ref=got.at[0, t],
                                    dst_ref=there,
                                    send_sem=m.send_sems.at[k],
                                    recv_sem=m.recv_sems.at[m.number(("g", q, u))],
                                    device_id=(dp, p.ctx, t),
                                    device_id_type=MESH,
                                )
                            )
                        pl.when(p.dp == dp)(copies[0].start)
                        pl.when(p.dp != dp)(copies[1].start)
                        m.sent.append(copies[0])
            for _ in range(6):
                yield
            m.remote(("gc", u), gotx.at[0, u], gotx.at[0, u], p.at(dp=p.other)).wait_send()
            m.arrive(("gc", u), gall.at[p.other * 4 + u])
            for us in range(4):
                if us != u:
                    m.arrive(("g", 0, us), gall.at[p.dp * 4 + us])
                    m.arrive(("g", 1, us), gall.at[p.other * 4 + us])

        def out_proj():
            def column(ref, part, c):
                return ref.at[part, :, pl.ds(pl.multiple_of(c * quarter, quarter), quarter)]

            low, high = pl.ds(0, 2), pl.ds(2, 2)
            for i, (cx, cy) in ((1, (p.dg, p.dg)), (0, (p.xn, p.yn))):
                m.send(("ox", i), column(o_ref, low, cx), oxs.at[i], p.at(ctx=p.xn))
                m.send(("oy", i), column(o_ref, high, cy), oys.at[i], p.at(ctx=p.yn))
            yield
            m.arrive(("ox", 1), oxs.at[1])
            for t in range(2):
                add_up(oxs.at[1, t], [column(o_ref, t, p.yn), oxs.at[1, t]])
            m.send("oy2", oxs.at[1], oy2, p.at(ctx=p.yn))
            m.arrive(("oy", 1), oys.at[1])
            for t in range(2):
                add_up(oys.at[1, t], [column(o_ref, 2 + t, p.xn), oys.at[1, t]])
            m.send("ox2", oys.at[1], ox2, p.at(ctx=p.xn))
            yield
            m.arrive(("ox", 0), oxs.at[0])
            m.arrive(("oy", 0), oys.at[0])
            m.arrive("oy2", oy2)
            m.arrive("ox2", ox2)
            home_dp, home_ctx = u // 2, 2 * (u % 2) + p.dp
            here_all = []
            for us in range(4):
                got, got2 = (oxs, oy2) if us < 2 else (oys, ox2)
                t = us % 2
                add_up(got.at[0, t], [column(o_ref, us, p.ctx), got.at[0, t], got2.at[t]])
                own = (home_dp == p.dp) & (home_ctx == p.ctx) & (us == u)
                there = oall.at[p.ctx]
                here = pltpu.make_async_copy(
                    got.at[0, t], there, m.send_sems.at[m.number("O")]
                )

                @pl.when(own)
                def _(here=here):
                    here.start()
                    here.wait()

                for j in range(4):
                    copy = pltpu.make_async_remote_copy(
                        src_ref=got.at[0, t],
                        dst_ref=there,
                        send_sem=m.send_sems.at[m.number(("os", us))],
                        recv_sem=m.recv_sems.at[m.number(("o", j))],
                        device_id=(home_dp, home_ctx, us),
                        device_id_type=MESH,
                    )
                    pl.when(jnp.logical_not(own) & (p.ctx == j))(copy.start)
                here_all.append((own, copy))
            yield
            head_dp, head_u = lax.rem(p.ctx, 2), p.dp * 2 + lax.div(p.ctx, 2)
            for j in range(4):
                mine = (head_dp == p.dp) & (p.ctx == j) & (head_u == u)

                @pl.when(jnp.logical_not(mine))
                def _(j=j):
                    m.arrive(("o", j), oall.at[j])

            for own, copy in here_all:
                pl.when(jnp.logical_not(own))(copy.wait_send)

        def feed():
            mine = fall.at[p.dp * 4 + p.ctx]
            copy = m.local("F", f_ref.at[p.dp * 4 + p.ctx], mine)
            spots = [(q, c, i) for i, c in enumerate((p.ctx, p.xn, p.yn, p.dg)) for q in range(2)][1:]
            for q, c, i in spots:
                dp = p.dp if q == 0 else p.other
                m.send(("f", q, i), f_ref.at[dp * 4 + c], mine, p.at(dp=dp, ctx=c))
            for _ in range(4):
                yield
            for q, c, i in spots:
                dp = p.dp if q == 0 else p.other
                m.arrive(("f", q, i), fall.at[dp * 4 + c])
            copy.wait()

        def tokens_stream():
            yield from line_reduce(m, "s", part_ref, out, sib, right, left, sums)

            def body(i, total):
                at = pl.ds(pl.multiple_of(i * 16, 16), 16)
                values = in_ref[at, :].astype(F32)
                normed, _ = normalize(values)
                return total + jnp.sum(out[at, :] * normed, axis=0, keepdims=True)

            total = lax.fori_loop(0, tokens // 16, body, jnp.zeros((1, width), F32))
            row = lax.broadcasted_iota(jnp.int32, (8, width), 0)
            gains[...] = jnp.where(
                row == 0,
                jnp.broadcast_to(total, (8, width)),
                jnp.where(row == 1, jnp.broadcast_to(t_ref[...], (8, width)), 0.0),
            )
            for i, device in enumerate((p.at(dp=p.other), p.at(ctx=p.xn), p.at(ctx=p.yn))):
                m.remote(("n", i), gains, away.at[i], device).start()
                yield
                m.remote(("n", i), gains, away.at[i], device).wait()
                gains[...] = gains[...] + away[i]
            copies = [
                m.remote(("N", u, other), gains, away.at[3 + u], p.at(uly=other))
                for other in range(4)
                if other != u
            ]
            for copy in copies:
                copy.start()
            yield
            mine = gains[...]
            for other in range(4):
                if other != u:
                    m.arrive(("N", other, u), away.at[3 + other])
                    mine = mine + away[3 + other]
            for copy in copies:
                copy.wait_send()
            gains[...] = mine

        return [
            tokens_stream(),
            attn(),
            later(out_proj(), 1),
            later(feed(), 5),
        ]

    return run_kernel(
        "last",
        2,
        4,
        everyone,
        streams,
        [
            ((tokens, width), F32, VMEM),
            ((8, rows, cols), BF16, HBM),
            ((4, out_rows, quarter), BF16, HBM),
            ((8, rows, ff2), BF16, HBM),
            ((8, width), F32, VMEM),
        ],
        [(part, VMEM), (grads, VMEM), (gout, VMEM), (gffn, HBM), (inputs, VMEM), (term, VMEM)],
        [
            *[((4, tokens, width), BF16)] * 4,
            *[((2, 4, rows, cols), BF16)] * 2,
            *[((4, rows, cols), BF16)] * 2,
            *[((2, 2, out_rows, quarter), BF16)] * 2,
            *[((2, out_rows, quarter), BF16)] * 2,
            ((7, 8, width), F32),
        ],
        vmem=56,
    )


def local(
    hidden_in,
    cotangent,
    log_decay,
    w_query,
    w_key,
    w_value,
    w_swish,
    w_output,
    w_gate,
    w_up,
    w_down,
    gain_attn,
    gain_ffn,
):
    bf16, f32 = BF16, F32
    dp, ctx = lax.axis_index(DP), lax.axis_index(CTX)
    tokens = hidden_in.shape[1]
    width = hidden_in.shape[2]
    rows = w_query.shape[0]
    out_rows = w_output.shape[0]
    key, val, ff = KEY_DIM, VALUE_DIM, w_gate.shape[1] // 8

    gains = jnp.pad(jnp.stack([gain_attn, gain_ffn], axis=1), ((0, 0), (0, 30)))
    packed, outw, gate_up = pack(w_query, w_key, w_value, w_swish, w_output, w_gate, w_up, gains)
    attn_cols = 2 * key + 2 * val
    hidden_all, decays, w_all, w_out, gate_up = start_exchange(
        hidden_in[0],
        log_decay[0],
        packed,
        outw,
        gate_up,
    )
    w_gu = lax.all_gather(gate_up, ULY, axis=0)
    w_gu = w_gu.transpose(1, 0, 2, 3).reshape(32 * rows, 2 * ff)
    w_down, gate_up = lax.optimization_barrier((w_down, gate_up))
    w_dn = lax.all_gather(w_down, ULY, axis=0, tiled=True)
    w_all = w_all.reshape(32 * rows, packed.shape[2])
    w_attn = w_all[:, :attn_cols]
    gain_one = w_all[:, attn_cols].astype(f32)
    gain_two = w_all[:, attn_cols + 1].astype(f32)
    w_out = w_out.reshape(4 * out_rows, width)

    normed_all, _ = normalize(hidden_all.reshape(8 * tokens, width).astype(f32))
    scaled_one = (normed_all * gain_one).astype(bf16)
    qkvs = matmul(scaled_one, w_attn)
    block = 4 * tokens
    q = qkvs[:, :key].astype(bf16).reshape(2, block, key)
    k = qkvs[:, key : 2 * key].astype(bf16).reshape(2, block, key)
    v = qkvs[:, 2 * key : 2 * key + val].astype(bf16).reshape(2, block, val)
    swish_pre = qkvs[:, 2 * key + val :]

    decays = lax.dynamic_index_in_dim(decays, dp, 1, keepdims=False).reshape(2, 4, block)
    decay = lax.dynamic_index_in_dim(decays, ctx, 1, keepdims=False)
    lasts = jnp.sum(decays, axis=2).T
    scale = 1.0 / math.sqrt(KEY_DIM)
    cumulative = running_sum(decay)
    later = lax.broadcasted_iota(jnp.int32, (block, block), 0) >= lax.broadcasted_iota(
        jnp.int32, (block, block), 1
    )
    gap = cumulative[:, :, None] - cumulative[:, None, :]
    mask = jnp.where(later[None], jnp.exp(jnp.minimum(gap, 0.0)), 0.0) * scale
    last = cumulative[:, -1:]
    tail = jnp.exp(last - cumulative)[:, :, None]
    reach = jnp.exp(cumulative)[:, :, None]

    weights = (pair_dot(2, 2, q, k) * mask).astype(bf16)
    k_tail = (k.astype(f32) * tail).astype(bf16)
    update = pair_dot(1, 1, k_tail, v)
    spots = jnp.arange(4)

    def between(j, near):
        inside = (spots > jnp.minimum(j, near)) & (spots < jnp.maximum(j, near))
        return jnp.exp(jnp.sum(jnp.where(inside[:, None], lasts, 0.0), 0))

    before = jnp.stack([jnp.where(j < ctx, between(j, ctx), 0.0) for j in range(4)])
    after = jnp.stack([jnp.where(j > ctx, between(j, ctx), 0.0) for j in range(4)])
    updates = state_exchange(update.astype(bf16), 3).astype(f32)
    state_in = jnp.sum(before[:, :, None, None] * updates, axis=0).astype(bf16)
    retained = pair_dot(2, 1, weights, v) + scale * reach * pair_dot(2, 1, q, state_in)
    head_normed, head_inverse = normalize(retained)
    head_out = head_normed.astype(bf16).reshape(2 * block, val).astype(f32)
    swish_act = jax.nn.silu(swish_pre)
    gated = (swish_act * head_out).astype(bf16)
    attn, top_all = reduce_line(
        matmul(gated, w_out).astype(bf16).reshape(8, tokens, width), cotangent[0], 4
    )
    top_all = top_all.reshape(8 * tokens, width)
    inputs = hidden_in[0].astype(f32)
    residual = inputs + attn

    normed_two, inverse_two = normalize(residual)
    scaled_two = gather_plane((normed_two * gain_two).astype(bf16), 5).reshape(8 * tokens, width)
    gu = matmul(scaled_two, w_gu)
    gate_pre, up_pre = gu[:, :ff], gu[:, ff:]
    gate_act = jax.nn.silu(gate_pre)
    product = (gate_act * up_pre).astype(bf16)
    grad_product = dot_nt(top_all, w_dn)
    grad_gu = jnp.concatenate(
        [
            (grad_product * up_pre * swish_slope(gate_pre)).astype(bf16),
            (grad_product * gate_act).astype(bf16),
        ],
        axis=1,
    )
    gs2 = reduce_plane(dot_nt(grad_gu, w_gu).astype(bf16).reshape(8, tokens, width), 6)
    grad_top = cotangent[0].astype(f32)
    gain_two_term = jnp.sum(gs2 * normed_two, axis=0, keepdims=True)
    grad_residual = grad_top + norm_back(gs2 * gain_two, normed_two, inverse_two)
    ggu = dot_t(scaled_two, grad_gu).astype(bf16).reshape(2, 4, 4, rows, 2 * ff)
    ggu = ggu.transpose(0, 2, 1, 3, 4).reshape(2, 4, 4 * rows, 2 * ff)
    grad_y, out_part, grad_down, ggu_0, ggu_1 = gather_line_reduce_plane(
        grad_residual.astype(bf16),
        matmul(product, w_dn).astype(bf16).reshape(8, tokens, width),
        dot_t(product, top_all).astype(bf16).reshape(4, out_rows, width),
        (ggu[0], ggu[1]),
        7,
    )
    ggu = jnp.concatenate([ggu_0, ggu_1]).reshape(8, rows, 2 * ff)
    layer_out = residual + out_part
    grad_y = grad_y.reshape(8 * tokens, width)

    grad_gated = dot_nt(grad_y, w_out)
    g_out = dot_t(gated, grad_y).astype(bf16)
    grad_swish_pre = (grad_gated * head_out * swish_slope(swish_pre)).astype(bf16)
    grad_head = (grad_gated * swish_act).astype(bf16).astype(f32).reshape(2, block, val)
    grad_retained = norm_back(grad_head, head_normed, head_inverse).astype(bf16)
    grad_scores = (pair_dot(2, 2, grad_retained, v) * mask).astype(bf16)
    q_reach = (q.astype(f32) * (reach * scale)).astype(bf16)
    grad_state = pair_dot(1, 1, q_reach, grad_retained)
    grad_states = state_exchange(grad_state.astype(bf16), 8).astype(f32)
    grad_update = jnp.sum(after[:, :, None, None] * grad_states, axis=0).astype(bf16)
    grad_q = pair_dot(2, 1, grad_scores, k) + scale * reach * pair_dot(2, 2, grad_retained, state_in
    )
    grad_k = pair_dot(1, 1, grad_scores, q) + tail * pair_dot(2, 2, v, grad_update)
    grad_v = pair_dot(1, 1, weights, grad_retained) + tail * pair_dot(2, 1, k, grad_update
    )
    grad_cat = jnp.concatenate(
        [
            grad_q.astype(bf16).reshape(2 * block, key),
            grad_k.astype(bf16).reshape(2 * block, key),
            grad_v.astype(bf16).reshape(2 * block, val),
            grad_swish_pre,
        ],
        axis=1,
    )
    gs1, gcat, g_out, ggu, gain_terms = last_exchange(
        dot_nt(grad_cat, w_attn).astype(bf16).reshape(8, tokens, width),
        dot_t(scaled_one, grad_cat).astype(bf16).reshape(2, 4, 4, rows, attn_cols),
        g_out.reshape(4, out_rows, width),
        ggu,
        hidden_in[0],
        gain_two_term,
    )
    normed_one, inverse_one = normalize(inputs)
    grad_input = grad_residual + norm_back(gs1 * gain_one, normed_one, inverse_one)

    grad_query, grad_key, grad_value, grad_swish, grad_output, grad_gate, grad_up = unpack(
        gcat, g_out, ggu
    )
    me = dp * 16 + ctx * 4 + lax.axis_index(ULY)
    gain_terms = lax.dynamic_slice_in_dim(gain_terms, me * rows, rows, axis=1)
    return (
        layer_out[None],
        grad_input[None],
        grad_query,
        grad_key,
        grad_value,
        grad_swish,
        grad_output,
        grad_gate,
        grad_up,
        grad_down,
        gain_terms[0],
        gain_terms[1],
    )


def solution(mesh):
    shape = mesh.shape
    planned = (shape[DP], shape[CTX], shape[ULY]) == (2, 4, 4)
    tokens = P(DP, (CTX, ULY), None)
    weight = P(EVERYWHERE, None)
    gain = P(EVERYWHERE)
    return jax.shard_map(
        local if planned else local_any,
        mesh=mesh,
        in_specs=(tokens, tokens, P(DP, ULY, CTX), *[weight] * 8, gain, gain),
        out_specs=(tokens, tokens, *[weight] * 8, gain, gain),
        check_vma=False,
    )
```

time: 3710 us -> 723 us (0.19)
  blocking collectives: 2240 us -> 0 us
  waiting for transfers between devices: 1040 us -> 0.73 us
  Pallas kernels: 0 us -> 514 us
  matrix products: 244 us -> 92.8 us
  local copies, waits for them, and re-layouts: 115 us -> 67.2 us
    unnamed x5 -> x0, blocking collectives: 2110 us -> none
    all_gather x10 -> x2, waiting for transfers between devices: 660 us -> 0.02 us  [the longest x1 0.02 us: local(): w_dn = lax.all_gather(w_down, ULY, axis=0, tiled=True)]
    pallas_call x0 -> x10, Pallas kernels: none -> 514 us  [the longest x8 510 us: run_kernel(): pl.pallas_call(kernel, out_shape=[jax.ShapeDtypeStruct(*o[:2]) for o in o...]
    reduce_scatter x6 -> x0, waiting for transfers between devices: 314 us -> none  [the longest x1 269 us: local(): lax.psum_scatter(grad_value_term, ('dp', 'ctx', 'ulysses'), scatter_dimen...]
    dot_general x24 -> x4, matrix products: 223 us -> 24.7 us  [matmul(): return jnp.dot(left, right, preferred_element_type=jnp.float32)]
    all_to_all x4 -> x0, blocking collectives: 126 us -> none  [the longest x1 54.9 us: local(): lax.all_to_all(grad_head_v.astype(jnp.bfloat16), 'ulysses', split_axis=0,...]
    unnamed x107 -> x108, local copies, waits for them, and re-layouts: 72.5 us -> 22.5 us
    dot_general x12 -> x21, matrix products: 21 us -> 68 us  [the longest x4 24.9 us: dot_nt(): lax.dot_general(left, right, (((1,), (1,)), ((), ())), preferred_element_...]
  transfers between devices with their start and end apart: 24 -> 2, of which waited for: 15 -> 0; matrix products, arithmetic and copies ran while one was open for 62% -> 7% of each run, Pallas kernels for 0% -> 19%
where the time goes in v2:
time: 723 us; the launch traced here: 714 us
  Pallas kernels  514 us (71%)
  matrix products  92.8 us (13%)
  local copies, waits for them, and re-layouts  67.2 us (9%)
  other arithmetic  24.4 us (3%)
  between operations  15.2 us (2%)
    pallas_call x8, Pallas kernels, run_kernel(): pl.pallas_call(kernel, out_shape=[jax.ShapeDtypeStruct(*o[:2]) for o in o...  510 us
    dot_general x4, matrix products, dot_nt(): lax.dot_general(left, right, (((1,), (1,)), ((), ())), preferred_element_...  24.9 us
    dot_general x4, matrix products, matmul(): return jnp.dot(left, right, preferred_element_type=jnp.float32)  24.7 us
    dot_general x4, matrix products, dot_t(): lax.dot_general(left, right, (((0,), (0,)), ((), ())), preferred_element_...  23.3 us
    unnamed x108, local copies, waits for them, and re-layouts  22.5 us
    dot_general x12, matrix products, pair_dot(): return lax.dot_general(left, right, dims, preferred_element_type=F32)  19.6 us
  transfers between devices with their start and end apart: 2, of which 0 were waited for; matrix products, arithmetic and copies ran while one was open for 7% of the time, Pallas kernels for 19%

profile of v2, /device:TPU:9, one launch (start us, length us, event | category | flops | bytes accessed | tf_op | source)
XLA Modules:
  0.0 714.1 jit_solution(15615048574945395534)
XLA Ops:
  15.8 91.2 %start.1 = (bf16[8,128,2048]{2,1,0:T(8,128)(2,1)}, f32[8,2,512]{2,1,0:T(2,128)S(1)}, bf16[32,64,1408]{2,1,0:T(8,128)(2,1)}, bf16[4,108,2048]{2,1,0:T(8,128)(2,1)S(1)}, bf16[8,64,864]{2,1,0:T(8,128)(2,1)}) custom-call(bf16[128,2048]{1,0:T(8,128)(2,1)S(1)} %bitcast.140, f32[2,512]{1,0:T(2,128)S(1)} %bitcast.145, ...), custom_call_target="tpu_custom_call" | custom-call | bytes 148000000 | tf_op jit(solution)/shard_map/start/pallas_call | solution.py:545
  107.8 3.1 multiply_reduce_fusion
  110.9 2.9 slice_convert_fusion
  115.3 3.2 fusion.1
  118.5 12.1 %fusion.59 = (bf16[1024,1376]{0,1:T(8,128)(2,1)S(1)}, f32[1024,1376]{0,1:T(8,128)}) fusion(bf16[1024,2048]{1,0:T(8,128)(2,1)S(1)} %fusion.1, bf16[2048,1408]{1,0:T(8,128)(2,1)} %bitcast.185), kind=kOutput, calls=%fused_computation.145 | convolution fusion | flops 5772771328 | bytes 18415616 | tf_op jit(solution)/shard_map/dot_general | solution.py:69
  141.5 19.4 %state.2 = bf16[4,2,256,432]{3,2,1,0:T(8,128)(2,1)S(1)} custom-call(bf16[2,256,432]{2,1,0:T(8,128)(2,1)S(1)} %copy.120.refs_0_), custom_call_target="tpu_custom_call" | custom-call | bytes 148000000 | tf_op jit(solution)/shard_map/state/pallas_call | solution.py:545
  170.6 4.4 convolution_convert_fusion.2
  175.0 89.1 %reduce_line.1 = (f32[128,2048]{1,0:T(8,128)S(1)}, bf16[8,128,2048]{2,1,0:T(8,128)(2,1)S(1)}) custom-call(bf16[8,128,2048]{2,1,0:T(8,128)(2,1)} %bitcast.168, bf16[128,2048]{1,0:T(8,128)(2,1)S(1)} %bitcast.141), custom_call_target="tpu_custom_call" | custom-call | bytes 148000000 | tf_op jit(solution)/shard_map/reduce_line/pallas_call | solution.py:545
  266.5 26.5 %gather_plane.1 = bf16[8,128,2048]{2,1,0:T(8,128)(2,1)S(1)} custom-call(bf16[128,2048]{1,0:T(8,128)(2,1)S(1)} %multiply_convert_fusion.10.refs_0_), custom_call_target="tpu_custom_call" | custom-call | bytes 148000000 | tf_op jit(solution)/shard_map/gather_plane/pallas_call | solution.py:545
  295.0 2.6 reshape.346
  297.7 2.5 copy.125
  301.0 4.0 fusion.60
  305.0 2.7 multiply_convert_fusion.6
  307.6 6.1 convolution_convert_fusion.4
  313.7 5.2 convolution_convert_fusion.3
  318.9 3.3 convolution_convert_fusion.6
  322.2 4.3 convolution_convert_fusion.1
  326.6 24.3 %reduce_plane.1 = f32[128,2048]{1,0:T(8,128)S(1)} custom-call(bf16[8,128,2048]{2,1,0:T(8,128)(2,1)S(1)} %bitcast.142), custom_call_target="tpu_custom_call" | custom-call | bytes 148000000 | tf_op jit(solution)/shard_map/reduce_plane/pallas_call | solution.py:545
  351.8 2.6 reshape.326.refs_2_
  354.4 6.0 copy.126
  366.9 113.8 %gather_line.1 = (bf16[8,128,2048]{2,1,0:T(8,128)(2,1)}, f32[128,2048]{1,0:T(8,128)}, f32[108,2048]{1,0:T(8,128)}, bf16[256,864]{1,0:T(8,128)(2,1)}, bf16[256,864]{1,0:T(8,128)(2,1)}) custom-call(bf16[128,2048]{1,0:T(8,128)(2,1)} %fusion.56.refs_0_, bf16[8,128,2048]{2,1,0:T(8,128)(2,1)} %bitcast.169, bf16[4,108,2048]{2,1,0:T(8,128)(2,1)} %reshape.326.refs_2_, ...), custom_call_target="tpu_custom_call" | custom-call | bytes 148000000 | tf_op jit(solution)/shard_map/gather_line/pallas_call | solution.py:545
  480.7 6.3 fusion.26
  487.0 3.3 convolution_convert_fusion.5
  499.7 2.9 fusion.15
  504.7 21.3 %state.3 = bf16[4,2,256,432]{3,2,1,0:T(8,128)(2,1)S(1)} custom-call(bf16[2,256,432]{2,1,0:T(8,128)(2,1)S(1)} %copy.137.refs_0_), custom_call_target="tpu_custom_call" | custom-call | bytes 148000000 | tf_op jit(solution)/shard_map/state/pallas_call | solution.py:545
  531.4 2.5 fusion.14
  538.6 10.7 %fusion.6 = bf16[1024,2048]{1,0:T(8,128)(2,1)} fusion(bf16[2048,1408]{1,0:T(8,128)(2,1)} %bitcast.186, bf16[1024,432]{0,1:T(8,128)(2,1)} %get-tuple-element.79, bf16[1024,432]{0,1:T(8,128)(2,1)S(1)} %bitcast.177, bf16[1024,256]{0,1:T(8,128)(2,1)} %copy.146, bf16[1024,256]{0,1:T(8,128)(2,1)S(1)} %copy-done.47), kind=kOutput, calls=%fused_computation.13 | convolution fusion | flops 5784731648 | bytes 12779520 | tf_op jit(solution)/shard_map/dot_general | solution.py:282
  549.3 10.6 %convolution_convert_fusion = bf16[2048,1376]{0,1:T(8,128)(2,1)} fusion(bf16[1024,2048]{1,0:T(8,128)(2,1)S(1)} %copy-done.34, bf16[1024,432]{0,1:T(8,128)(2,1)S(1)} %copy-done.51, bf16[1024,432]{0,1:T(8,128)(2,1)S(1)} %bitcast.178, bf16[1024,256]{0,1:T(8,128)(2,1)S(1)} %copy-done.48, bf16[1024,256]{0,1:T(8,128)(2,1)S(1)} %copy-done.47), kind=kOutput, calls=%fused_computation.4 | convolution fusion | flops 5785452544 | bytes 12648448 | tf_op jit(solution)/shard_map/dot_general | solution.py:278
  559.9 2.7 reshape.336.refs_2_
  562.6 8.4 %copy.143 = bf16[2048,1376]{1,0:T(8,128)(2,1)} copy(bf16[2048,1376]{0,1:T(8,128)(2,1)} %convolution_convert_fusion) | data formatting | bytes 11272192 | tf_op jit(solution)/shard_map/convert_element_type | solution.py:1328
  573.0 124.6 %last.1 = (f32[128,2048]{1,0:T(8,128)}, bf16[8,64,1376]{2,1,0:T(8,128)(2,1)}, bf16[4,108,512]{2,1,0:T(8,128)(2,1)}, bf16[8,64,864]{2,1,0:T(8,128)(2,1)}, f32[8,2048]{1,0:T(8,128)}) custom-call(bf16[8,128,2048]{2,1,0:T(8,128)(2,1)} %bitcast.170, bf16[2,4,4,64,1376]{4,3,2,1,0:T(8,128)(2,1)} %bitcast.148, bf16[4,108,2048]{2,1,0:T(8,128)(2,1)} %reshape.336.refs_2_, ...), custom_call_target="tpu_custom_call" | custom-call | bytes 148000000 | tf_op jit(solution)/shard_map/last/pallas_call | solution.py:545
  703.0 2.9 unpack.1
  (182 shorter events, 73.5 us)
Async XLA Ops:
  7.2 8.6 %copy-start = (bf16[1,128,2048]{2,1,0:T(8,128)(2,1)S(1)}, bf16[1,128,2048]{2,1,0:T(8,128)(2,1)}, u32[]{:S(2)}) copy-start(bf16[1,128,2048]{2,1,0:T(8,128)(2,1)} %param.13) | copy-start | bytes 1572868
  7.2 287.8 %all-gather.7.cloned.1.call-start = ((), (), s32[]{:S(2)}) async-start(), calls=%async_computation.1 | async-start | bytes 2293760 | tf_op jit(solution)/shard_map/all_gather | solution.py:1216
  107.0 190.6 %all-gather.5.cloned.1.call-start = ((), (), s32[]{:S(2)}) async-start(), calls=%async_computation | async-start | bytes 4587520 | tf_op jit(solution)/shard_map/all_gather | solution.py:1213
  118.5 12.1 %copy-start.33 = (bf16[1024,2048]{1,0:T(8,128)(2,1)}, bf16[1024,2048]{1,0:T(8,128)(2,1)S(1)}, u32[]{:S(2)}) copy-start(bf16[1024,2048]{1,0:T(8,128)(2,1)S(1)} %fusion.1) | copy-start | bytes 12582916
  130.7 34.1 %copy-start.20 = (bf16[1024,432]{0,1:T(8,128)(2,1)}, bf16[1024,432]{0,1:T(8,128)(2,1)S(1)}, u32[]{:S(2)}) copy-start(bf16[1024,432]{0,1:T(8,128)(2,1)S(1)} %slice.66) | copy-start | bytes 2654212
  138.4 2.9 copy-start.39
  141.5 24.0 %copy-start.25 = (bf16[1024,256]{1,0:T(8,128)(2,1)}, bf16[1024,256]{1,0:T(8,128)(2,1)S(1)}, u32[]{:S(2)}) copy-start(bf16[1024,256]{1,0:T(8,128)(2,1)S(1)} %copy.147) | copy-start | bytes 1572868
  160.9 3.0 copy-start.28
  168.4 2.2 copy-start.40
  170.6 4.4 copy-start.45
  170.6 4.4 copy-start.2
  297.7 3.3 copy-start.4
  301.0 4.0 copy-start.17
  301.0 4.0 copy-start.42
  366.9 113.8 %copy-start.23 = (f32[2,54,8,512]{3,2,0,1:T(8,128)S(1)}, f32[2,54,8,512]{3,2,0,1:T(8,128)}, u32[]{:S(2)}) copy-start(f32[2,54,8,512]{3,2,0,1:T(8,128)} %copy-done.22) | copy-start | bytes 5308420
  366.9 113.8 %copy-start.41 = (bf16[432,2048]{1,0:T(8,128)(2,1)S(1)}, bf16[432,2048]{1,0:T(8,128)(2,1)}, u32[]{:S(2)}) copy-start(bf16[432,2048]{1,0:T(8,128)(2,1)} %reshape.319) | copy-start | bytes 5308420
  480.7 6.3 copy-start.46
  480.7 6.3 copy-start.50
  487.0 3.3 copy-start.19
  491.8 2.8 copy-start.31
  531.3 2.5 copy-start.27
  531.3 2.5 copy-start.32
  535.2 3.4 copy-start.47
  538.6 10.7 %copy-start.34 = (bf16[1024,2048]{1,0:T(8,128)(2,1)S(1)}, bf16[1024,2048]{1,0:T(8,128)(2,1)}, u32[]{:S(2)}) copy-start(bf16[1024,2048]{1,0:T(8,128)(2,1)} %copy-done.33) | copy-start | bytes 12582916
  538.6 10.7 %copy-start.48 = (bf16[1024,256]{0,1:T(8,128)(2,1)S(1)}, bf16[1024,256]{0,1:T(8,128)(2,1)}, u32[]{:S(2)}) copy-start(bf16[1024,256]{0,1:T(8,128)(2,1)} %copy.146) | copy-start | bytes 1572868
  538.6 10.7 %copy-start.51 = (bf16[1024,432]{0,1:T(8,128)(2,1)S(1)}, bf16[1024,432]{0,1:T(8,128)(2,1)}, u32[]{:S(2)}) copy-start(bf16[1024,432]{0,1:T(8,128)(2,1)} %get-tuple-element.79) | copy-start | bytes 2654212
  562.6 8.4 %copy-start.49 = (bf16[256,864]{1,0:T(8,128)(2,1)S(1)}, bf16[256,864]{1,0:T(8,128)(2,1)}, u32[]{:S(2)}) copy-start(bf16[256,864]{1,0:T(8,128)(2,1)} %get-tuple-element.53) | copy-start | bytes 1327108
  573.0 124.6 %copy-start.1 = (bf16[1,128,2048]{2,1,0:T(8,128)(2,1)S(1)}, bf16[1,128,2048]{2,1,0:T(8,128)(2,1)}, u32[]{:S(2)}) copy-start(bf16[1,128,2048]{2,1,0:T(8,128)(2,1)} %param.13) | copy-start | bytes 1572868
  573.0 127.5 %copy-start.43 = (f32[128,2048]{1,0:T(8,128)S(1)}, f32[128,2048]{1,0:T(8,128)}, u32[]{:S(2)}) copy-start(f32[128,2048]{1,0:T(8,128)} %get-tuple-element.51) | copy-start | bytes 3145732
  697.6 2.9 copy-start.35
  700.5 2.5 copy-start.8
  702.4 3.5 copy-start.44
  (22 other events, 29.6 us)
Sparse Core Ops, SparseCore 0:
  107.2 49.0 all-gather.6
  157.8 98.5 all-gather.4

commit v3 on v2

--- a/solution.py
+++ b/solution.py
@@ -305,7 +305,8 @@
 
 
 class Mover:
-    def __init__(self, place, names, send, recv):
+    def __init__(self, place, names, send, recv, like=None):
+        self.like = like
         self.place, self.names, self.send_sems, self.recv_sems = place, names, send, recv
         self.sent = []
 
@@ -326,7 +327,7 @@
     def send(self, name, src, dst, device):
         copy = self.remote(name, src, dst, device)
         copy.start()
-        self.sent.append(copy)
+        self.sent.append(copy if self.like is None else name)
 
     def arrive(self, name, dst):
         self.remote(name, dst, dst, self.place.at(dp=self.place.other)).wait_recv()
@@ -338,6 +339,9 @@
 
     def finish(self):
         for copy in self.sent:
+            if self.like is not None:
+                ref = self.like()
+                copy = self.remote(copy, ref, ref, self.place.at(dp=self.place.other))
             copy.wait_send()
 
 
@@ -365,6 +369,10 @@
 
 
 def add_up(dst, sources, step=32):
+    if len(dst.shape) > 2:
+        for i in range(dst.shape[0]):
+            add_up(dst.at[i], [source.at[i] for source in sources], step)
+        return
     rows, columns = dst.shape
     by_rows = rows % step == 0
     step = step if by_rows else 256
@@ -444,39 +452,37 @@
     copy.wait()
 
 
-def line_reduce(m, tag, part, out, sib, right, left, sums):
+def line_reduce(m, tag, part, out, sib, right, left):
     p = m.place
     u = p.uly
     order = (3, 0, 2, 1) if u < 2 else (0, 3, 1, 2)
     for b in order if sib is not None else ():
-        m.send((tag, "c", b), part.at[p.other * 4 + b], sib.at[b], p.at(dp=p.other))
+        m.send((tag, "c", b), part(p.other * 4 + b), sib.at[b], p.at(dp=p.other))
     met = set()
 
     def meet(b):
         if sib is None:
-            return [part.at[b]]
+            return [part(b)]
         if b not in met:
             met.add(b)
             m.arrive((tag, "c", b), sib.at[b])
-        return [part.at[p.dp * 4 + b], sib.at[b]]
+        return [part(p.dp * 4 + b), sib.at[b]]
+
+    def onward(way, b, arrived, there):
+        terms = meet(b)
+        if arrived is not None:
+            m.arrive((tag, way, b), arrived)
+            terms.append(arrived)
+        if len(terms) > 1:
+            add_up(terms[-1], terms)
+        m.send((tag, way, b), terms[-1], (right if way == "r" else left).at[b], p.at(uly=there))
 
     for slot in range(3):
-        for b in range(1, 4):
+        for b in range(4):
             if u < b and u + 3 - b == slot:
-                terms = meet(b)
-                if u > 0:
-                    m.arrive((tag, "r", b), right.at[b])
-                    terms.append(right.at[b])
-                add_up(sums.at[b], terms)
-                m.send((tag, "r", b), sums.at[b], right.at[b], p.at(uly=u + 1))
-        for b in range(3):
+                onward("r", b, right.at[b] if u > 0 else None, u + 1)
             if u > b and 3 - u + b == slot:
-                terms = meet(b)
-                if u < 3:
-                    m.arrive((tag, "l", b), left.at[b])
-                    terms.append(left.at[b])
-                add_up(sums.at[b], terms)
-                m.send((tag, "l", b), sums.at[b], left.at[b], p.at(uly=u - 1))
+                onward("l", b, left.at[b] if u < 3 else None, u - 1)
         yield
     terms = meet(u)
     if u > 0:
@@ -658,19 +664,57 @@
     )(heads, outg, slices)
 
 
-def start_exchange(hidden, decay, packed, outw, gu):
+def line_spread(m, tag, own, out):
+    u = m.place.uly
+    copy = m.local((tag, 8), own, out.at[u])
+    if u < 3:
+        m.send((tag, "r", u), own, out.at[u], m.place.at(uly=u + 1))
+    if u > 0:
+        m.send((tag, "l", u), own, out.at[u], m.place.at(uly=u - 1))
+    copy.wait()
+    yield
+    for d in range(1, 4):
+        for way, b, onward in (("r", u - d, u + 1), ("l", u + d, u - 1)):
+            if 0 <= b <= 3:
+                m.arrive((tag, way, b), out.at[b])
+                if 0 <= onward <= 3:
+                    m.send((tag, way, b), out.at[b], out.at[b], m.place.at(uly=onward))
+        yield
+
+
+def block_factors(cum, ctx, s, backward):
+    count = cum.shape[1]
+    lasts = [cum[4 * s + j : 4 * s + j + 1, count - 1 : count] for j in range(4)]
+    found = []
+    for j in range(4):
+        total = jnp.zeros((1, 1), F32)
+        for i in range(4):
+            inside = ((i > ctx) & (i < j)) if backward else ((i > j) & (i < ctx))
+            total = total + jnp.where(inside, lasts[i], 0.0)
+        right = (j > ctx) if backward else (j < ctx)
+        found.append(jnp.where(right, jnp.exp(total), 0.0))
+    return found
+
+
+def forward(hidden, cot, decay, packed, outw, gu, w_down):
     tokens, width = hidden.shape
     rows, cols = packed.shape[1:]
     out_rows, quarter = outw.shape[1:]
     ff2 = gu.shape[2]
-
-    def streams(m, hid_ref, dec_ref, pk_ref, ow_ref, gu_ref, hall, dall, wall, oall, gall):
+    key, val = KEY_DIM, VALUE_DIM
+    block, both = 4 * tokens, 8 * tokens
+    half = block // 2
+    scale = 1.0 / math.sqrt(key)
+    at_s = 2 * key + val
+
+    def start_streams(m, hid_ref, dec_ref, pk_ref, ow_ref, gu_ref, hall, dall, wall, oall, gall):
         p = m.place
         u = p.uly
 
         def row(q, c, us):
             dp = p.dp if q == 0 else p.other
-            return wall.at[dp * 16 + c * 4 + us]
+            at = (dp * 16 + c * 4 + us) * rows
+            return wall.at[pl.ds(pl.multiple_of(at, rows), rows)]
 
         def attn():
             sources = sorted(
@@ -806,149 +850,426 @@
             later(feed(), 6),
         ]
 
+    def kernel(
+        hid_ref, cot_ref, dec_ref, pk_ref, ow_ref, gu_ref, wd_ref,
+        w_all, s1_all, w2d, q_ref, k_ref, v_ref, sw_ref, w_ref, mask_ref, st_ref, reach_ref, tail_ref, cum_ref,
+        gain_ref, hn_ref, hi_ref, ga_ref, res_ref, s2_all, top_all, gu_all, wd_all,
+        wall, s1, oall, dall, gall, dec8, cols8, upd, upds, ret, part, sib, right, left, s2, send, recv,
+    ):
+        uly = lax.axis_index(ULY)
+        names = {}
+        place = Place(uly)
+        greet(everyone(place))
+        common = Mover(place, names, send, recv)
+        ctx = place.ctx
+
+        def for_each(body):
+            for u in range(4):
+                pl.when(uly == u)(functools.partial(body, u))
+
+        spread = []
+        for u in range(4):
+            for tag, own, out in (("g", gall, gu_all), ("e", wd_ref, wd_all)):
+                m = Mover(Place(u), names, send, recv, lambda out=out: out.at[0])
+                spread.append((u, m, line_spread(m, tag, own, out)))
+
+        def spread_on(u):
+            for v, _, stream in spread:
+                if u == v:
+                    next(stream, 0)
+
+        def first(u):
+            m = Mover(Place(u), names, send, recv)
+            together(
+                start_streams(m, hid_ref, dec_ref, pk_ref, ow_ref, gu_ref, s1, dall, wall, oall, gall)
+            )
+            m.finish()
+            spread_on(u)
+
+        for_each(first)
+        keep = [common.local("w", wall, w_all)]
+
+        table = wall[:, cols - 128 : cols].astype(F32).T
+        first_gain = 128 - 32
+        gain_ref[...] = table[first_gain : first_gain + 8]
+
+        def norm_one(i, carry):
+            b, at = lax.div(i, 4), pl.ds(pl.multiple_of(lax.rem(i, 4) * 32, 32), 32)
+            normed, _ = normalize(s1[b, at, :].astype(F32))
+            s1[b, at, :] = (normed * gain_ref[0:1, :]).astype(BF16)
+            return carry
+
+        lax.fori_loop(0, 32, norm_one, 0)
+        keep.append(common.local("W", s1, s1_all))
+
+        for i in range(8):
+            dec8[i : i + 1, :] = dall[i, pl.ds(place.dp, 1), :]
+        upper = lax.broadcasted_iota(jnp.int32, (block, block), 0) <= lax.broadcasted_iota(
+            jnp.int32, (block, block), 1
+        )
+        cum_ref[...] = jnp.dot(
+            dec8[...], upper.astype(F32), precision=lax.Precision.HIGHEST, preferred_element_type=F32
+        )
+        for s in range(2):
+            dec8[s : s + 1, :] = cum_ref[pl.ds(4 * s + ctx, 1), :]
+        cols8[...] = dec8[...].T
+        for s in range(2):
+            column = cols8[:, s : s + 1]
+            reach_ref[s] = jnp.exp(column) * scale
+            tail_ref[s] = jnp.exp(dec8[s : s + 1, block - 1 : block] - column)
+
+        for s in range(2):
+            lhs = s1[4 * s : 4 * s + 4].reshape(block, width)
+            q_ref[s] = matmul(lhs, wall[:, :key]).astype(BF16)
+            k_ref[s] = matmul(lhs, wall[:, key : 2 * key]).astype(BF16)
+            rest = matmul(lhs, wall[:, 2 * key :])
+            v_ref[s] = rest[:, :val].astype(BF16)
+            sw_ref[pl.ds(s * block, block), :] = rest[:, val : 2 * val]
+        for s in range(2):
+            k_tail = (k_ref[s].astype(F32) * tail_ref[s]).astype(BF16)
+            upd[s] = dot_t(k_tail, v_ref[s]).astype(BF16)
+        states = plane_gather(
+            common, "t", upd, upds, state_slot, (pl.ds(0, 1), pl.ds(1, 1)), pair=False
+        )
+        next(states)
+
+        def intra(c, carry):
+            s, h = lax.div(c, 2), lax.rem(c, 2)
+            at = pl.ds(pl.multiple_of(h * half, half), half)
+            here = pl.ds(pl.multiple_of(c * half, half), half)
+            gap = cols8[at, :]
+            column = jnp.where(s == 0, gap[:, 0:1], gap[:, 1:2])
+            gap = column - dec8[pl.ds(s, 1), :]
+            t = lax.broadcasted_iota(jnp.int32, (half, block), 0) + h * half
+            later_on = t >= lax.broadcasted_iota(jnp.int32, (half, block), 1)
+            mask = jnp.where(later_on, jnp.exp(jnp.minimum(gap, 0.0)), 0.0) * scale
+            mask_ref[s, at, :] = mask
+            weights = (dot_nt(q_ref[s, at, :], k_ref[s]) * mask).astype(BF16)
+            w_ref[s, at, :] = weights
+            ret[here, :] = matmul(weights, v_ref[s])
+            return carry
+
+        lax.fori_loop(0, 2, intra, 0)
+        next(states)
+        for_each(spread_on)
+        lax.fori_loop(2, 4, intra, 0)
+        for i in range(4):
+            w2d[i * out_rows : (i + 1) * out_rows, :] = oall[i]
+        for _ in states:
+            pass
+        for s in range(2):
+            factors = block_factors(cum_ref, ctx, s, False)
+            total = factors[0] * upds[0, s].astype(F32)
+            for j in range(1, 4):
+                total = total + factors[j] * upds[j, s].astype(F32)
+            st_ref[s] = total.astype(BF16)
+
+        def outer(c, carry):
+            s, h = lax.div(c, 2), lax.rem(c, 2)
+            at = pl.ds(pl.multiple_of(h * half, half), half)
+            here = pl.ds(pl.multiple_of(c * half, half), half)
+            retained = ret[here, :] + reach_ref[s, at, :] * matmul(q_ref[s, at, :], st_ref[s])
+            normed, inverse = normalize(retained)
+            hn_ref[here, :] = normed
+            hi_ref[here, :] = inverse
+            pre = sw_ref[here, :]
+            gated = (pre * jax.nn.sigmoid(pre) * normed.astype(BF16).astype(F32)).astype(BF16)
+            ga_ref[here, :] = gated
+            for n in range(4):
+                cut = pl.ds(n * quarter, quarter)
+                value = matmul(gated, w2d[:, cut]).astype(BF16)
+                part[pl.ds(2 * c, 2), :, cut] = value.reshape(2, tokens, quarter)
+            return carry
+
+        lax.fori_loop(0, 4, outer, 0)
+
+        def reduce(u):
+            m = Mover(Place(u), names, send, recv)
+            low = tokens // 2
+            together(
+                [
+                    line_reduce(m, "s", lambda i: part.at[i], res_ref, sib, right, left),
+                    plane_gather(
+                        m, "C", cot_ref, top_all, token_slot, (pl.ds(0, low), pl.ds(low, low))
+                    ),
+                ]
+            )
+            m.finish()
+            spread_on(u)
+
+        for_each(reduce)
+
+        def norm_two(i, carry):
+            at = pl.ds(pl.multiple_of(i * 16, 16), 16)
+            residual = hid_ref[at, :].astype(F32) + res_ref[at, :]
+            res_ref[at, :] = residual
+            normed, _ = normalize(residual)
+            s2[at, :] = (normed * gain_ref[1:2, :]).astype(BF16)
+            return carry
+
+        lax.fori_loop(0, tokens // 16, norm_two, 0)
+        low = tokens // 2
+        for _ in plane_gather(
+            common, "k", s2, s2_all, token_slot, (pl.ds(0, low), pl.ds(low, low))
+        ):
+            pass
+
+        def last(u):
+            spread_on(u)
+            for v, m, _ in spread:
+                if u == v:
+                    m.finish()
+
+        for_each(last)
+        for copy in keep:
+            copy.wait()
+        common.finish()
+        assert len(names) <= N_SEMS
+
+    vmem, hbm = pl.BlockSpec(memory_space=VMEM), pl.BlockSpec(memory_space=HBM)
+    outs = [
+        ((width, cols), BF16, hbm),
+        ((8, tokens, width), BF16, hbm),
+        ((4 * out_rows, width), BF16, vmem),
+        ((2, block, key), BF16, vmem),
+        ((2, block, key), BF16, vmem),
+        ((2, block, val), BF16, vmem),
+        ((both, val), F32, vmem),
+        ((2, block, block), BF16, vmem),
+        ((2, block, block), F32, vmem),
+        ((2, key, val), BF16, vmem),
+        ((2, block, 1), F32, vmem),
+        ((2, block, 1), F32, vmem),
+        ((8, block), F32, vmem),
+        ((8, width), F32, vmem),
+        ((both, val), F32, vmem),
+        ((both, 1), F32, vmem),
+        ((both, val), BF16, vmem),
+        ((tokens, width), F32, vmem),
+        ((8, tokens, width), BF16, hbm),
+        ((8, tokens, width), BF16, hbm),
+        ((4, 8, rows, ff2), BF16, hbm),
+        ((4, out_rows, width), BF16, hbm),
+    ]
+    return pl.pallas_call(
+        kernel,
+        out_shape=[jax.ShapeDtypeStruct(shape, kind) for shape, kind, _ in outs],
+        in_specs=[vmem, hbm, vmem, hbm, hbm, hbm, hbm],
+        out_specs=[spec for _, _, spec in outs],
+        scratch_shapes=[
+            pltpu.VMEM((width, cols), BF16),
+            pltpu.VMEM((8, tokens, width), BF16),
+            pltpu.VMEM((4, out_rows, width), BF16),
+            pltpu.VMEM((8, 2, block), F32),
+            pltpu.VMEM((8, rows, ff2), BF16),
+            pltpu.VMEM((8, block), F32),
+            pltpu.VMEM((block, 8), F32),
+            pltpu.VMEM((2, key, val), BF16),
+            pltpu.VMEM((4, 2, key, val), BF16),
+            pltpu.VMEM((both, val), F32),
+            pltpu.VMEM((8, tokens, width), BF16),
+            pltpu.VMEM((4, tokens, width), BF16),
+            pltpu.VMEM((4, tokens, width), BF16),
+            pltpu.VMEM((4, tokens, width), BF16),
+            pltpu.VMEM((tokens, width), BF16),
+            pltpu.SemaphoreType.DMA((N_SEMS,)),
+            pltpu.SemaphoreType.DMA((N_SEMS,)),
+        ],
+        name="forward",
+        compiler_params=pltpu.CompilerParams(
+            collective_id=1, has_side_effects=True, vmem_limit_bytes=62 << 20
+        ),
+    )(hidden, cot, decay, packed, outw, gu, w_down)
+
+
+def reduce_plane(part, down, number):
+    _, tokens, width = part.shape
+
+    def streams(m, part_ref, down_ref, out, dout, sib, sums, got, got2, right, left):
+        return [
+            plane_reduce(m, "s", part_ref, out, sib, sums, got, got2),
+            line_reduce(m, "d", lambda b: down_ref.at[b], dout, None, right, left),
+        ]
+
     return run_kernel(
-        "start",
-        1,
-        4,
-        everyone,
-        streams,
-        [
-            ((8, tokens, width), BF16, HBM),
-            ((8, *decay.shape), F32, HBM),
-            ((32, rows, cols), BF16, HBM),
-            ((4, out_rows, 4 * quarter), BF16, HBM),
-            ((8, rows, ff2), BF16, HBM),
-        ],
-        [(hidden, HBM), (decay, HBM), (packed, HBM), (outw, HBM), (gu, HBM)],
-    )
-
-
-def state_exchange(state, number):
-    def streams(m, own, out):
-        return [
-            plane_gather(m, "s", own, out, state_slot, (pl.ds(0, 1), pl.ds(1, 1)), pair=False)
-        ]
-
-    [out] = run_kernel(
-        "state",
-        number,
-        1,
-        lambda p: [p.at(ctx=p.xn), p.at(ctx=p.yn)],
-        streams,
-        [((4, *state.shape), state.dtype, HBM)],
-        [(state, HBM)],
-    )
-    return out
-
-
-def reduce_line(part, cot, number):
-    _, tokens, width = part.shape
-    half = tokens // 2
-
-    def streams(m, part_ref, cot_ref, out, cots, sib, right, left, sums):
-        return [
-            line_reduce(m, "s", part_ref, out, sib, right, left, sums),
-            plane_gather(m, "C", cot_ref, cots, token_slot, (pl.ds(0, half), pl.ds(half, half))),
-        ]
-
-    return run_kernel(
-        "reduce_line",
+        "reduce_plane",
         number,
         4,
         lambda p: line_partners(p) + plane_partners(p)[1:],
         streams,
-        [((tokens, width), F32, VMEM), ((8, tokens, width), BF16, HBM)],
-        [(part, VMEM), (cot, HBM)],
-        [((4, tokens, width), BF16)] * 4,
-    )
-
-
-def gather_plane(own, number):
-    tokens, width = own.shape
-    half = tokens // 2
-
-    def streams(m, own_ref, out):
-        return [
-            plane_gather(
-                m, "k", own_ref, out, token_slot, (pl.ds(0, half), pl.ds(half, half))
-            )
-        ]
-
-    [out] = run_kernel(
-        "gather_plane",
-        number,
-        1,
-        plane_partners,
-        streams,
-        [((8, tokens, width), BF16, HBM)],
-        [(own, VMEM)],
-    )
-    return out
-
-
-def reduce_plane(part, number):
-    _, tokens, width = part.shape
-
-    def streams(m, part_ref, out, sib, sums, got, got2):
-        return [plane_reduce(m, "s", part_ref, out, sib, sums, got, got2)]
-
-    [out] = run_kernel(
-        "reduce_plane",
-        number,
-        1,
-        plane_partners,
-        streams,
-        [((tokens, width), F32, VMEM)],
-        [(part, VMEM)],
+        [((tokens, width), F32, VMEM), (down.shape[1:], F32, VMEM)],
+        [(part, VMEM), (down, VMEM)],
         [
             ((4, tokens, width), BF16),
             ((4, tokens, width), BF16),
             ((2, tokens, width), BF16),
             ((tokens, width), BF16),
+            (down.shape, BF16),
+            (down.shape, BF16),
         ],
     )
-    return out
-
-
-def gather_line_reduce_plane(own, part, down, gates, number):
-    _, tokens, width = part.shape
-    shapes = [g.shape for g in (down, *gates)]
-
-    def streams(m, own_ref, part_ref, d_ref, g_ref, h_ref, out, total, dout, gout, hout, *scratch):
-        sib, sums, got, got2 = scratch[:4]
-        more = scratch[4:]
-        return [
-            line_gather(m, "k", own_ref, out),
-            plane_reduce(m, "s", part_ref, total, sib, sums, got, got2),
-            *[
-                line_reduce(m, i, ref, o, None, *more[3 * i : 3 * i + 3])
-                for i, (ref, o) in enumerate(((d_ref, dout), (g_ref, gout), (h_ref, hout)))
-            ],
+
+
+def attention_back(
+    own, lo, ggu, w_out, gated, normed, inverse, swish, q, k, v, weights, mask, state_in, reach, tail, cum
+):
+    tokens, width = own.shape
+    both, val = gated.shape
+    block, key = q.shape[1:]
+    rows, cols = ggu.shape[3:]
+    piece = w_out.shape[0] // 4
+    half = block // 2
+    at_v, at_s = 2 * key, 2 * key + val
+
+    def kernel(
+        own_ref, lo_ref, g_ref, wo_ref, ga_ref, hn_ref, hi_ref, sw_ref, q_ref, k_ref, v_ref, w_ref, mask_ref, st_ref,
+        reach_ref, tail_ref, cum_ref, cat_ref, total, gout, gsum,
+        gy, gr, gs, gq, gk, gv, gst, gsts, sib, sums, got, got2, right, left, send, recv,
+    ):
+        uly = lax.axis_index(ULY)
+        names = {}
+        place = Place(uly)
+        greet(line_partners(place) + plane_partners(place)[1:])
+        common = Mover(place, names, send, recv)
+        movers = [Mover(Place(u), names, send, recv, lambda: right.at[0]) for u in range(4)]
+        ways = [
+            line_reduce(movers[u], "f", lambda b: g_ref.at[:, :, b], gsum, None, right, left)
+            for u in range(4)
         ]
 
-    return run_kernel(
-        "gather_line",
-        number,
-        4,
-        lambda p: line_partners(p) + plane_partners(p)[1:],
-        streams,
-        [
-            ((8, tokens, width), BF16, HBM),
-            ((tokens, width), F32, VMEM),
-            (shapes[0][1:], F32, VMEM),
-            (shapes[1][1:], BF16, VMEM),
-            (shapes[2][1:], BF16, VMEM),
+        def for_each(body):
+            for u in range(4):
+                pl.when(uly == u)(functools.partial(body, u))
+
+        def first(u):
+            def slot_zero():
+                next(ways[u])
+                yield
+
+            m = Mover(Place(u), names, send, recv)
+            together(
+                [
+                    plane_reduce(m, "s", lo_ref, total, sib, sums, got, got2),
+                    line_gather(m, "k", own_ref, gy),
+                    slot_zero(),
+                ]
+            )
+            m.finish()
+
+        for_each(first)
+
+        def chunk(c):
+            return pl.ds(pl.multiple_of(c * half, half), half)
+
+        def gradients(c, carry):
+            at = chunk(c)
+            grad = gy[pl.ds(2 * c, 2)].reshape(half, width)
+            gg = dot_nt(grad, wo_ref[...])
+            pre = sw_ref[at, :]
+            sigma = jax.nn.sigmoid(pre)
+            head = hn_ref[at, :]
+            low = head.astype(BF16).astype(F32)
+            cat_ref[at, at_s : at_s + val] = (
+                gg * low * (sigma * (1.0 + pre * (1.0 - sigma)))
+            ).astype(BF16)
+            gh = (gg * (pre * sigma)).astype(BF16).astype(F32)
+            mean = jnp.mean(gh * head, axis=-1, keepdims=True)
+            grad_retained = (hi_ref[at, :] * (gh - head * mean)).astype(BF16)
+            gr[at, :] = grad_retained
+            s = lax.div(c, 2)
+            part = pl.ds(pl.multiple_of(lax.rem(c, 2) * half, half), half)
+            gs[at, :] = (dot_nt(grad_retained, v_ref[s]) * mask_ref[s, part, :]).astype(BF16)
+            return carry
+
+        lax.fori_loop(0, both // half, gradients, 0)
+        for s in range(2):
+            at = pl.ds(s * block, block)
+            reached = (q_ref[s].astype(F32) * reach_ref[s]).astype(BF16)
+            gst[s] = dot_t(reached, gr[at, :]).astype(BF16)
+        states = plane_gather(
+            common, "t", gst, gsts, state_slot, (pl.ds(0, 1), pl.ds(1, 1)), pair=False
+        )
+        next(states)
+        for_each(lambda u: next(ways[u]))
+
+        for s in range(2):
+            at = pl.ds(s * block, block)
+            gq[at, :] = jnp.dot(gs[at, :], k_ref[s], preferred_element_type=F32)
+            gk[at, :] = dot_t(gs[at, :], q_ref[s])
+        next(states)
+        for s in range(2):
+            at = pl.ds(s * block, block)
+            gv[at, :] = dot_t(w_ref[s], gr[at, :])
+
+        def out_grad(n, carry):
+            at = pl.ds(pl.multiple_of(n * 512, 512), 512)
+            grad = gy[:, :, at].reshape(both, 512)
+            value = dot_t(ga_ref[...], grad).astype(BF16)
+            for i in range(4):
+                gout[i, :, at] = value[i * piece : (i + 1) * piece]
+            return carry
+
+        lax.fori_loop(0, width // 512, out_grad, 0)
+        for _ in states:
+            pass
+        for_each(lambda u: next(ways[u]))
+        for s in range(2):
+            at = pl.ds(s * block, block)
+            factors = block_factors(cum_ref, place.ctx, s, True)
+            update = factors[0] * gsts[0, s].astype(F32)
+            for j in range(1, 4):
+                update = update + factors[j] * gsts[j, s].astype(F32)
+            update = update.astype(BF16)
+            grad = gr[at, :]
+            cat_ref[at, :key] = (gq[at, :] + reach_ref[s] * dot_nt(grad, st_ref[s])).astype(BF16)
+            cat_ref[at, key:at_v] = (gk[at, :] + tail_ref[s] * dot_nt(v_ref[s], update)).astype(BF16)
+            cat_ref[at, at_v:at_s] = (
+                gv[at, :] + tail_ref[s] * jnp.dot(k_ref[s], update, preferred_element_type=F32)
+            ).astype(BF16)
+
+        def last(u):
+            for _ in ways[u]:
+                pass
+            movers[u].finish()
+
+        for_each(last)
+        common.finish()
+        assert len(names) <= N_SEMS
+
+    vmem = pl.BlockSpec(memory_space=VMEM)
+    return pl.pallas_call(
+        kernel,
+        out_shape=[
+            jax.ShapeDtypeStruct((both, 2 * key + 2 * val), BF16),
+            jax.ShapeDtypeStruct((tokens, width), F32),
+            jax.ShapeDtypeStruct((4, piece, width), BF16),
+            jax.ShapeDtypeStruct((2, 4, rows, cols), BF16),
         ],
-        [(own, VMEM), (part, VMEM), (down, VMEM), (gates[0], VMEM), (gates[1], VMEM)],
-        [
-            ((4, tokens, width), BF16),
-            ((4, tokens, width), BF16),
-            ((2, tokens, width), BF16),
-            ((tokens, width), BF16),
-            *[(shape, BF16) for shape in shapes for _ in range(3)],
+        in_specs=[vmem] * 17,
+        out_specs=[vmem] * 4,
+        scratch_shapes=[
+            pltpu.VMEM((8, tokens, width), BF16),
+            pltpu.VMEM((both, val), BF16),
+            pltpu.VMEM((both, block), BF16),
+            pltpu.VMEM((both, key), F32),
+            pltpu.VMEM((both, key), F32),
+            pltpu.VMEM((both, val), F32),
+            pltpu.VMEM((2, key, val), BF16),
+            pltpu.VMEM((4, 2, key, val), BF16),
+            pltpu.VMEM((4, tokens, width), BF16),
+            pltpu.VMEM((4, tokens, width), BF16),
+            pltpu.VMEM((2, tokens, width), BF16),
+            pltpu.VMEM((tokens, width), BF16),
+            pltpu.VMEM((4, 2, 4, rows, cols), BF16),
+            pltpu.VMEM((4, 2, 4, rows, cols), BF16),
+            pltpu.SemaphoreType.DMA((N_SEMS,)),
+            pltpu.SemaphoreType.DMA((N_SEMS,)),
         ],
-        vmem=56,
-    )
+        name="attention_back",
+        compiler_params=pltpu.CompilerParams(
+            collective_id=7, has_side_effects=True, vmem_limit_bytes=62 << 20
+        ),
+    )(own, lo, ggu, w_out, gated, normed, inverse, swish, q, k, v, weights, mask, state_in, reach, tail, cum)
 
 
 def last_exchange(part, grads, gout, gffn, inputs, term):
@@ -960,7 +1281,7 @@
 
     def streams(
         m, part_ref, g_ref, o_ref, f_ref, in_ref, t_ref, out, gall, oall, fall, gains,
-        sib, right, left, sums, gotx, goty, gotx2, goty2, oxs, oys, ox2, oy2, away,
+        sib, right, left, gotx, goty, gotx2, goty2, oxs, oys, ox2, oy2, away,
     ):
         p = m.place
         u = p.uly
@@ -1107,7 +1428,7 @@
             copy.wait()
 
         def tokens_stream():
-            yield from line_reduce(m, "s", part_ref, out, sib, right, left, sums)
+            yield from line_reduce(m, "s", lambda i: part_ref.at[i], out, sib, right, left)
 
             def body(i, total):
                 at = pl.ds(pl.multiple_of(i * 16, 16), 16)
@@ -1166,7 +1487,7 @@
         ],
         [(part, VMEM), (grads, VMEM), (gout, VMEM), (gffn, HBM), (inputs, VMEM), (term, VMEM)],
         [
-            *[((4, tokens, width), BF16)] * 4,
+            *[((4, tokens, width), BF16)] * 3,
             *[((2, 4, rows, cols), BF16)] * 2,
             *[((4, rows, cols), BF16)] * 2,
             *[((2, 2, out_rows, quarter), BF16)] * 2,
@@ -1203,73 +1524,20 @@
     gains = jnp.pad(jnp.stack([gain_attn, gain_ffn], axis=1), ((0, 0), (0, 30)))
     packed, outw, gate_up = pack(w_query, w_key, w_value, w_swish, w_output, w_gate, w_up, gains)
     attn_cols = 2 * key + 2 * val
-    hidden_all, decays, w_all, w_out, gate_up = start_exchange(
-        hidden_in[0],
-        log_decay[0],
-        packed,
-        outw,
-        gate_up,
-    )
-    w_gu = lax.all_gather(gate_up, ULY, axis=0)
+    block = 4 * tokens
+    (
+        w_all, scaled_one, w_out, q, k, v, swish_pre, weights, mask, state_in, reach, tail, cum,
+        gains, head_normed, head_inverse, gated, residual, scaled_two, top_all, w_gu, w_dn,
+    ) = forward(hidden_in[0], cotangent[0], log_decay[0], packed, outw, gate_up, w_down)
+    w_attn = w_all[:, :attn_cols]
+    gain_one, gain_two = gains[0], gains[1]
+    scaled_one = scaled_one.reshape(8 * tokens, width)
+    scaled_two = scaled_two.reshape(8 * tokens, width)
+    top_all = top_all.reshape(8 * tokens, width)
     w_gu = w_gu.transpose(1, 0, 2, 3).reshape(32 * rows, 2 * ff)
-    w_down, gate_up = lax.optimization_barrier((w_down, gate_up))
-    w_dn = lax.all_gather(w_down, ULY, axis=0, tiled=True)
-    w_all = w_all.reshape(32 * rows, packed.shape[2])
-    w_attn = w_all[:, :attn_cols]
-    gain_one = w_all[:, attn_cols].astype(f32)
-    gain_two = w_all[:, attn_cols + 1].astype(f32)
-    w_out = w_out.reshape(4 * out_rows, width)
-
-    normed_all, _ = normalize(hidden_all.reshape(8 * tokens, width).astype(f32))
-    scaled_one = (normed_all * gain_one).astype(bf16)
-    qkvs = matmul(scaled_one, w_attn)
-    block = 4 * tokens
-    q = qkvs[:, :key].astype(bf16).reshape(2, block, key)
-    k = qkvs[:, key : 2 * key].astype(bf16).reshape(2, block, key)
-    v = qkvs[:, 2 * key : 2 * key + val].astype(bf16).reshape(2, block, val)
-    swish_pre = qkvs[:, 2 * key + val :]
-
-    decays = lax.dynamic_index_in_dim(decays, dp, 1, keepdims=False).reshape(2, 4, block)
-    decay = lax.dynamic_index_in_dim(decays, ctx, 1, keepdims=False)
-    lasts = jnp.sum(decays, axis=2).T
-    scale = 1.0 / math.sqrt(KEY_DIM)
-    cumulative = running_sum(decay)
-    later = lax.broadcasted_iota(jnp.int32, (block, block), 0) >= lax.broadcasted_iota(
-        jnp.int32, (block, block), 1
-    )
-    gap = cumulative[:, :, None] - cumulative[:, None, :]
-    mask = jnp.where(later[None], jnp.exp(jnp.minimum(gap, 0.0)), 0.0) * scale
-    last = cumulative[:, -1:]
-    tail = jnp.exp(last - cumulative)[:, :, None]
-    reach = jnp.exp(cumulative)[:, :, None]
-
-    weights = (pair_dot(2, 2, q, k) * mask).astype(bf16)
-    k_tail = (k.astype(f32) * tail).astype(bf16)
-    update = pair_dot(1, 1, k_tail, v)
-    spots = jnp.arange(4)
-
-    def between(j, near):
-        inside = (spots > jnp.minimum(j, near)) & (spots < jnp.maximum(j, near))
-        return jnp.exp(jnp.sum(jnp.where(inside[:, None], lasts, 0.0), 0))
-
-    before = jnp.stack([jnp.where(j < ctx, between(j, ctx), 0.0) for j in range(4)])
-    after = jnp.stack([jnp.where(j > ctx, between(j, ctx), 0.0) for j in range(4)])
-    updates = state_exchange(update.astype(bf16), 3).astype(f32)
-    state_in = jnp.sum(before[:, :, None, None] * updates, axis=0).astype(bf16)
-    retained = pair_dot(2, 1, weights, v) + scale * reach * pair_dot(2, 1, q, state_in)
-    head_normed, head_inverse = normalize(retained)
-    head_out = head_normed.astype(bf16).reshape(2 * block, val).astype(f32)
-    swish_act = jax.nn.silu(swish_pre)
-    gated = (swish_act * head_out).astype(bf16)
-    attn, top_all = reduce_line(
-        matmul(gated, w_out).astype(bf16).reshape(8, tokens, width), cotangent[0], 4
-    )
-    top_all = top_all.reshape(8 * tokens, width)
+    w_dn = w_dn.reshape(4 * out_rows, width)
     inputs = hidden_in[0].astype(f32)
-    residual = inputs + attn
-
     normed_two, inverse_two = normalize(residual)
-    scaled_two = gather_plane((normed_two * gain_two).astype(bf16), 5).reshape(8 * tokens, width)
     gu = matmul(scaled_two, w_gu)
     gate_pre, up_pre = gu[:, :ff], gu[:, ff:]
     gate_act = jax.nn.silu(gate_pre)
@@ -1282,52 +1550,39 @@
         ],
         axis=1,
     )
-    gs2 = reduce_plane(dot_nt(grad_gu, w_gu).astype(bf16).reshape(8, tokens, width), 6)
+    gs2, grad_down = reduce_plane(
+        dot_nt(grad_gu, w_gu).astype(bf16).reshape(8, tokens, width),
+        dot_t(product, top_all).astype(bf16).reshape(4, out_rows, width),
+        6,
+    )
     grad_top = cotangent[0].astype(f32)
     gain_two_term = jnp.sum(gs2 * normed_two, axis=0, keepdims=True)
     grad_residual = grad_top + norm_back(gs2 * gain_two, normed_two, inverse_two)
-    ggu = dot_t(scaled_two, grad_gu).astype(bf16).reshape(2, 4, 4, rows, 2 * ff)
-    ggu = ggu.transpose(0, 2, 1, 3, 4).reshape(2, 4, 4 * rows, 2 * ff)
-    grad_y, out_part, grad_down, ggu_0, ggu_1 = gather_line_reduce_plane(
+    grad_cat, out_part, g_out, ggu = attention_back(
         grad_residual.astype(bf16),
         matmul(product, w_dn).astype(bf16).reshape(8, tokens, width),
-        dot_t(product, top_all).astype(bf16).reshape(4, out_rows, width),
-        (ggu[0], ggu[1]),
-        7,
-    )
-    ggu = jnp.concatenate([ggu_0, ggu_1]).reshape(8, rows, 2 * ff)
+        dot_t(scaled_two, grad_gu).astype(bf16).reshape(2, 4, 4, rows, 2 * ff),
+        w_out,
+        gated,
+        head_normed,
+        head_inverse,
+        swish_pre,
+        q,
+        k,
+        v,
+        weights,
+        mask,
+        state_in,
+        reach,
+        tail,
+        cum,
+    )
     layer_out = residual + out_part
-    grad_y = grad_y.reshape(8 * tokens, width)
-
-    grad_gated = dot_nt(grad_y, w_out)
-    g_out = dot_t(gated, grad_y).astype(bf16)
-    grad_swish_pre = (grad_gated * head_out * swish_slope(swish_pre)).astype(bf16)
-    grad_head = (grad_gated * swish_act).astype(bf16).astype(f32).reshape(2, block, val)
-    grad_retained = norm_back(grad_head, head_normed, head_inverse).astype(bf16)
-    grad_scores = (pair_dot(2, 2, grad_retained, v) * mask).astype(bf16)
-    q_reach = (q.astype(f32) * (reach * scale)).astype(bf16)
-    grad_state = pair_dot(1, 1, q_reach, grad_retained)
-    grad_states = state_exchange(grad_state.astype(bf16), 8).astype(f32)
-    grad_update = jnp.sum(after[:, :, None, None] * grad_states, axis=0).astype(bf16)
-    grad_q = pair_dot(2, 1, grad_scores, k) + scale * reach * pair_dot(2, 2, grad_retained, state_in
-    )
-    grad_k = pair_dot(1, 1, grad_scores, q) + tail * pair_dot(2, 2, v, grad_update)
-    grad_v = pair_dot(1, 1, weights, grad_retained) + tail * pair_dot(2, 1, k, grad_update
-    )
-    grad_cat = jnp.concatenate(
-        [
-            grad_q.astype(bf16).reshape(2 * block, key),
-            grad_k.astype(bf16).reshape(2 * block, key),
-            grad_v.astype(bf16).reshape(2 * block, val),
-            grad_swish_pre,
-        ],
-        axis=1,
-    )
     gs1, gcat, g_out, ggu, gain_terms = last_exchange(
         dot_nt(grad_cat, w_attn).astype(bf16).reshape(8, tokens, width),
         dot_t(scaled_one, grad_cat).astype(bf16).reshape(2, 4, 4, rows, attn_cols),
-        g_out.reshape(4, out_rows, width),
-        ggu,
+        g_out,
+        ggu.reshape(8, rows, 2 * ff),
         hidden_in[0],
         gain_two_term,
     )

time: 723 us -> 613 us (0.85)
  matrix products: 92.8 us -> 46.3 us
  local copies, waits for them, and re-layouts: 67.2 us -> 35.9 us
  between operations: 15.2 us -> 1.35 us
  other arithmetic: 24.4 us -> 11 us
    pallas_call x8 -> x2, Pallas kernels: 510 us -> 166 us  [run_kernel(): pl.pallas_call(kernel, out_shape=[jax.ShapeDtypeStruct(*o[:2]) for o in o...]
    pallas_call x0 -> x2, Pallas kernels: none -> 337 us  [the longest x1 231 us: forward(): pl.pallas_call(kernel, out_shape=[jax.ShapeDtypeStruct(shape, kind) for s...]
    dot_general x13 -> x0, matrix products: 19.9 us -> none  [the longest x12 19.6 us: pair_dot(): return lax.dot_general(left, right, dims, preferred_element_type=F32)]
    dot_general x4 -> x2, matrix products: 24.7 us -> 10.2 us  [matmul(): return jnp.dot(left, right, preferred_element_type=jnp.float32)]
    reshape x8 -> x1, local copies, waits for them, and re-layouts: 11.7 us -> 1.65 us  [local(): w_dn = w_dn.reshape(4 * out_rows, width)]
    unnamed x108 -> x51, local copies, waits for them, and re-layouts: 22.5 us -> 13.1 us
    convert_element_type x5 -> x0, other arithmetic: 8.91 us -> none  [the longest x1 3.22 us: local(): scaled_one = (normed_all * gain_one).astype(bf16)]
    dot_general x4 -> x3, matrix products: 23.3 us -> 15.9 us  [dot_t(): lax.dot_general(left, right, (((0,), (0,)), ((), ())), preferred_element_...]
  transfers between devices with their start and end apart: 2 -> 0, of which waited for: 0 -> 0; matrix products, arithmetic and copies ran while one was open for 7% -> 0% of each run, Pallas kernels for 19% -> 0%
where the time goes in v3:
time: 613 us; the launch traced here: 601 us
  Pallas kernels  507 us (83%)
  matrix products  46.3 us (8%)
  local copies, waits for them, and re-layouts  35.9 us (6%)
  other arithmetic  11 us (2%)
    pallas_call x1, Pallas kernels, forward(): pl.pallas_call(kernel, out_shape=[jax.ShapeDtypeStruct(shape, kind) for s...  231 us
    pallas_call x2, Pallas kernels, run_kernel(): pl.pallas_call(kernel, out_shape=[jax.ShapeDtypeStruct(*o[:2]) for o in o...  166 us
    pallas_call x1, Pallas kernels, attention_back(): pl.pallas_call(kernel, out_shape=[jax.ShapeDtypeStruct((both, 2 * key + 2...  106 us
    dot_general x3, matrix products, dot_nt(): lax.dot_general(left, right, (((1,), (1,)), ((), ())), preferred_element_...  20.2 us
    dot_general x3, matrix products, dot_t(): lax.dot_general(left, right, (((0,), (0,)), ((), ())), preferred_element_...  15.9 us
    unnamed x51, local copies, waits for them, and re-layouts  13.1 us

profile of v3, /device:TPU:9, one launch (start us, length us, event | category | flops | bytes accessed | tf_op | source)
XLA Modules:
  0.0 601.2 jit_solution(3563438523325258172)
XLA Ops:
  1.3 1.2 fusion.13
  2.7 1.0 copy-done.6
  3.7 1.0 copy-done.8
  4.7 1.0 copy-done.9
  5.7 1.0 copy-done.10
  6.8 1.0 copy-done.11
  7.8 0.9 copy-done.12
  8.7 0.9 copy-done.13
  10.4 1.1 copy-done.1
  13.2 231.2 %forward.1 = (bf16[2048,1408]{1,0:T(8,128)(2,1)}, bf16[8,128,2048]{2,1,0:T(8,128)(2,1)}, bf16[432,2048]{1,0:T(8,128)(2,1)}, bf16[2,512,256]{2,1,0:T(8,128)(2,1)}...) custom-call(bf16[128,2048]{1,0:T(8,128)(2,1)} %bitcast.50, ...), custom_call_target="tpu_custom_call" | custom-call | tf_op jit(solution)/shard_map/forward/pallas_call | solution.py:1054
  244.3 1.4 multiply_reduce_fusion.2
  246.7 1.7 reshape.85
  248.3 3.1 copy.35
  252.3 4.0 fusion.18
  256.3 2.7 multiply_convert_fusion.2
  259.0 2.0 convolution_convert_fusion.4
  261.0 6.1 %convolution_convert_fusion.3 = bf16[2048,864]{0,1:T(8,128)(2,1)} fusion(bf16[1024,2048]{1,0:T(8,128)(2,1)S(1)} %bitcast.69, bf16[1024,432]{0,1:T(8,128)(2,1)S(1)} %get-tuple-element.101, bf16[1024,432]{0,1:T(8,128)(2,1)S(1)} %get-tuple-element.100), kind=kOutput, calls=%fused_computation.6 | convolution fusion | flops 3629187072 | bytes 9502720 | tf_op jit(solution)/shard_map/dot_general | solution.py:278
  267.1 6.4 %convolution_convert_fusion.2 = bf16[1024,2048]{1,0:T(8,128)(2,1)} fusion(bf16[2048,864]{1,0:T(8,128)(2,1)S(1)} %bitcast.58, bf16[1024,432]{0,1:T(8,128)(2,1)S(1)} %get-tuple-element.101, bf16[1024,432]{0,1:T(8,128)(2,1)S(1)} %get-tuple-element.100), kind=kOutput, calls=%fused_computation.5 | convolution fusion | flops 3629514752 | bytes 9502720 | tf_op jit(solution)/shard_map/dot_general | solution.py:282
  273.5 1.4 reshape.89.refs_1_
  274.9 1.5 copy-done
  276.4 42.9 %reduce_plane.1 = (f32[128,2048]{1,0:T(8,128)S(1)}, f32[108,2048]{1,0:T(8,128)S(1)}) custom-call(bf16[8,128,2048]{2,1,0:T(8,128)(2,1)} %bitcast.54, bf16[4,108,2048]{2,1,0:T(8,128)(2,1)S(1)} %copy-done), custom_call_target="tpu_custom_call" | custom-call | bytes 148000000 | tf_op jit(solution)/shard_map/reduce_plane/pallas_call | solution.py:551
  320.1 6.1 %copy.36 = bf16[2048,864]{1,0:T(8,128)(2,1)} copy(bf16[2048,864]{0,1:T(8,128)(2,1)} %convolution_convert_fusion.3) | data formatting | bytes 7077888 | tf_op jit(solution)/shard_map/convert_element_type | solution.py:1564
  326.2 2.2 fusion.16.own_ref
  328.4 6.2 %convolution_convert_fusion.1 = bf16[1024,2048]{1,0:T(8,128)(2,1)} fusion(bf16[1024,432]{0,1:T(8,128)(2,1)} %copy-done.24, bf16[432,2048]{1,0:T(8,128)(2,1)} %copy-done.18), kind=kOutput, calls=%fused_computation.3 | convolution fusion | flops 1814036480 | bytes 6848512 | tf_op jit(solution)/shard_map/dot_general | solution.py:69
  334.6 105.7 %attention_back.1 = (bf16[1024,1376]{1,0:T(8,128)(2,1)}, f32[128,2048]{1,0:T(8,128)}, bf16[4,108,2048]{2,1,0:T(8,128)(2,1)}, bf16[2,4,64,864]{3,2,1,0:T(8,128)(2,1)}) custom-call(bf16[128,2048]{1,0:T(8,128)(2,1)} %fusion.16.own_ref, bf16[8,128,2048]{2,1,0:T(8,128)(2,1)} %bitcast.53, bf16[2,4,4,64,864]{4,3,2,1,0:T(8,128)(2,1)} %bitcast.49, ...), custom_call_target="tpu_custom_call" | custom-call | tf_op jit(solution)/shard_map/attention_back/pallas_call | solution.py:1240
  440.3 11.1 %fusion.2 = bf16[1024,2048]{1,0:T(8,128)(2,1)} fusion(bf16[1024,1376]{1,0:T(8,128)(2,1)} %get-tuple-element.80, bf16[2048,1408]{1,0:T(8,128)(2,1)} %get-tuple-element.81), kind=kOutput, calls=%fused_computation.4 | convolution fusion | flops 5773459456 | bytes 12779520 | tf_op jit(solution)/shard_map/dot_general | solution.py:282
  451.4 7.8 %convolution_convert_fusion = bf16[2048,1376]{0,1:T(8,128)(2,1)} fusion(bf16[1024,2048]{1,0:T(8,128)(2,1)S(1)} %bitcast.67, bf16[1024,1376]{1,0:T(8,128)(2,1)S(1)} %copy-done.23), kind=kOutput, calls=%fused_computation | convolution fusion | flops 5774180352 | bytes 12648448 | tf_op jit(solution)/shard_map/dot_general | solution.py:278
  459.3 8.3 %copy.37 = bf16[2048,1376]{1,0:T(8,128)(2,1)} copy(bf16[2048,1376]{0,1:T(8,128)(2,1)} %convolution_convert_fusion) | data formatting | bytes 11272192 | tf_op jit(solution)/shard_map/convert_element_type | solution.py:1583
  467.6 123.3 %last.1 = (f32[128,2048]{1,0:T(8,128)}, bf16[8,64,1376]{2,1,0:T(8,128)(2,1)}, bf16[4,108,512]{2,1,0:T(8,128)(2,1)}, bf16[8,64,864]{2,1,0:T(8,128)(2,1)}, f32[8,2048]{1,0:T(8,128)}) custom-call(bf16[8,128,2048]{2,1,0:T(8,128)(2,1)} %bitcast.55, bf16[2,4,4,64,1376]{4,3,2,1,0:T(8,128)(2,1)} %bitcast.48, bf16[4,108,2048]{2,1,0:T(8,128)(2,1)} %get-tuple-element.83.refs_2_, ...), custom_call_target="tpu_custom_call" | custom-call | bytes 148000000 | tf_op jit(solution)/shard_map/last/pallas_call | solution.py:551
  590.9 1.5 fusion.8
  592.5 3.2 fusion.12
  596.9 2.9 unpack.1
  (53 shorter events, 8.1 us)
Async XLA Ops:
  2.7 1.0 copy-start.6
  3.7 1.0 copy-start.8
  4.7 1.0 copy-start.9
  5.7 1.0 copy-start.10
  6.7 1.0 copy-start.11
  7.8 0.9 copy-start.12
  8.7 0.9 copy-start.13
  10.4 1.1 copy-start.1
  11.5 0.9 copy-start.3
  12.4 0.8 copy-start.5
  248.3 7.9 %copy-start.18 = (bf16[432,2048]{1,0:T(8,128)(2,1)}, bf16[432,2048]{1,0:T(8,128)(2,1)S(1)}, u32[]{:S(2)}) copy-start(bf16[432,2048]{1,0:T(8,128)(2,1)S(1)} %reshape.85) | copy-start | bytes 5308420
  248.3 3.9 copy-start.21
  252.3 4.0 copy-start.22
  258.9 2.1 copy-start.24
  274.9 1.5 copy-start
  276.4 42.9 %copy-start.14 = (f32[128,2048]{1,0:T(8,128)S(1)}, f32[128,2048]{1,0:T(8,128)}, u32[]{:S(2)}) copy-start(f32[128,2048]{1,0:T(8,128)} %get-tuple-element.58) | copy-start | bytes 3145732
  440.3 11.2 %copy-start.20 = (bf16[8,128,2048]{2,1,0:T(8,128)(2,1)S(1)}, bf16[8,128,2048]{2,1,0:T(8,128)(2,1)}, u32[]{:S(2)}) copy-start(bf16[8,128,2048]{2,1,0:T(8,128)(2,1)} %get-tuple-element.82) | copy-start | bytes 12582916
  440.3 11.1 %copy-start.23 = (bf16[1024,1376]{1,0:T(8,128)(2,1)S(1)}, bf16[1024,1376]{1,0:T(8,128)(2,1)}, u32[]{:S(2)}) copy-start(bf16[1024,1376]{1,0:T(8,128)(2,1)} %get-tuple-element.80) | copy-start | bytes 8454148
  467.6 123.3 %copy-start.16 = (bf16[1,128,2048]{2,1,0:T(8,128)(2,1)S(1)}, bf16[1,128,2048]{2,1,0:T(8,128)(2,1)}, u32[]{:S(2)}) copy-start(bf16[1,128,2048]{2,1,0:T(8,128)(2,1)} %param.13) | copy-start | bytes 1572868
  467.6 124.8 %copy-start.15 = (f32[128,2048]{1,0:T(8,128)S(1)}, f32[128,2048]{1,0:T(8,128)}, u32[]{:S(2)}) copy-start(f32[128,2048]{1,0:T(8,128)} %get-tuple-element.58) | copy-start | bytes 3145732
  467.6 124.8 %copy-start.17 = (bf16[1,128,2048]{2,1,0:T(8,128)(2,1)S(1)}, bf16[1,128,2048]{2,1,0:T(8,128)(2,1)}, u32[]{:S(2)}) copy-start(bf16[1,128,2048]{2,1,0:T(8,128)(2,1)} %param.14) | copy-start | bytes 1572868
  467.6 124.8 %copy-start.19 = (f32[128,2048]{1,0:T(8,128)S(1)}, f32[128,2048]{1,0:T(8,128)}, u32[]{:S(2)}) copy-start(f32[128,2048]{1,0:T(8,128)} %get-tuple-element.79) | copy-start | bytes 3145732
  592.4 4.5 copy-start.2
  592.5 4.5 copy-start.4
  592.5 4.4 copy-start.7

commit v4 on v3

--- a/solution.py
+++ b/solution.py
@@ -305,10 +305,10 @@
 
 
 class Mover:
-    def __init__(self, place, names, send, recv, like=None):
-        self.like = like
+    def __init__(self, place, names, send, recv, like=None, like_whole=None):
+        self.like, self.like_whole = like, like_whole
         self.place, self.names, self.send_sems, self.recv_sems = place, names, send, recv
-        self.sent = []
+        self.sent, self.whole = [], []
 
     def number(self, name):
         return self.names.setdefault(name, len(self.names))
@@ -329,6 +329,11 @@
         copy.start()
         self.sent.append(copy if self.like is None else name)
 
+    def send_whole(self, name, src, dst, device):
+        copy = self.remote(name, src, dst, device)
+        copy.start()
+        self.whole.append((copy if self.like is None else None, name, None))
+
     def arrive(self, name, dst):
         self.remote(name, dst, dst, self.place.at(dp=self.place.other)).wait_recv()
 
@@ -338,6 +343,11 @@
         return copy
 
     def finish(self):
+        for copy, name, _ in self.whole:
+            if self.like is not None:
+                ref = self.like_whole()
+                copy = self.remote(name, ref, ref, self.place.at(dp=self.place.other))
+            copy.wait_send()
         for copy in self.sent:
             if self.like is not None:
                 ref = self.like()
@@ -452,46 +462,62 @@
     copy.wait()
 
 
-def line_reduce(m, tag, part, out, sib, right, left):
+def halves_of_rows(view, i):
+    rows = view.shape[0] // 2
+    return view.at[pl.ds(i * rows, rows)]
+
+
+def halves_of_columns(view, i):
+    columns = view.shape[1] // 2
+    return view.at[:, pl.ds(i * columns, columns)]
+
+
+def line_reduce(m, tag, part, out, sib, right, left, cut=halves_of_rows):
     p = m.place
     u = p.uly
     order = (3, 0, 2, 1) if u < 2 else (0, 3, 1, 2)
     for b in order if sib is not None else ():
-        m.send((tag, "c", b), part(p.other * 4 + b), sib.at[b], p.at(dp=p.other))
+        m.send_whole((tag, "c", b), part(p.other * 4 + b), sib.at[b], p.at(dp=p.other))
     met = set()
 
-    def meet(b):
+    def meet(b, i):
         if sib is None:
-            return [part(b)]
+            return [cut(part(b), i)]
         if b not in met:
             met.add(b)
             m.arrive((tag, "c", b), sib.at[b])
-        return [part(p.dp * 4 + b), sib.at[b]]
-
-    def onward(way, b, arrived, there):
-        terms = meet(b)
+        return [cut(part(p.dp * 4 + b), i), cut(sib.at[b], i)]
+
+    def onward(way, b, i, arrived, there):
+        terms = meet(b, i)
         if arrived is not None:
-            m.arrive((tag, way, b), arrived)
+            arrived = cut(arrived.at[b], i)
+            m.arrive((tag, way, b, i), arrived)
             terms.append(arrived)
         if len(terms) > 1:
             add_up(terms[-1], terms)
-        m.send((tag, way, b), terms[-1], (right if way == "r" else left).at[b], p.at(uly=there))
+        away = cut((right if way == "r" else left).at[b], i)
+        m.send((tag, way, b, i), terms[-1], away, p.at(uly=there))
 
     for slot in range(3):
         for b in range(4):
-            if u < b and u + 3 - b == slot:
-                onward("r", b, right.at[b] if u > 0 else None, u + 1)
-            if u > b and 3 - u + b == slot:
-                onward("l", b, left.at[b] if u < 3 else None, u - 1)
+            for i in range(2):
+                if u < b and u + 3 - b == slot:
+                    onward("r", b, i, right if u > 0 else None, u + 1)
+        for b in range(4):
+            for i in range(2):
+                if u > b and 3 - u + b == slot:
+                    onward("l", b, i, left if u < 3 else None, u - 1)
         yield
-    terms = meet(u)
-    if u > 0:
-        m.arrive((tag, "r", u), right.at[u])
-        terms.append(right.at[u])
-    if u < 3:
-        m.arrive((tag, "l", u), left.at[u])
-        terms.append(left.at[u])
-    add_up(out, terms)
+    for i in range(2):
+        terms = meet(u, i)
+        if u > 0:
+            m.arrive((tag, "r", u, i), cut(right.at[u], i))
+            terms.append(cut(right.at[u], i))
+        if u < 3:
+            m.arrive((tag, "l", u, i), cut(left.at[u], i))
+            terms.append(cut(left.at[u], i))
+        add_up(cut(out, i), terms)
 
 
 def plane_reduce(m, tag, part, out, sib, sums, got, got2):
@@ -664,21 +690,21 @@
     )(heads, outg, slices)
 
 
-def line_spread(m, tag, own, out):
+def line_spread(m, tag, own, slot):
     u = m.place.uly
-    copy = m.local((tag, 8), own, out.at[u])
+    copy = m.local((tag, 8), own, slot(u))
     if u < 3:
-        m.send((tag, "r", u), own, out.at[u], m.place.at(uly=u + 1))
+        m.send((tag, "r", u), own, slot(u), m.place.at(uly=u + 1))
     if u > 0:
-        m.send((tag, "l", u), own, out.at[u], m.place.at(uly=u - 1))
+        m.send((tag, "l", u), own, slot(u), m.place.at(uly=u - 1))
     copy.wait()
     yield
     for d in range(1, 4):
         for way, b, onward in (("r", u - d, u + 1), ("l", u + d, u - 1)):
             if 0 <= b <= 3:
-                m.arrive((tag, way, b), out.at[b])
+                m.arrive((tag, way, b), slot(b))
                 if 0 <= onward <= 3:
-                    m.send((tag, way, b), out.at[b], out.at[b], m.place.at(uly=onward))
+                    m.send((tag, way, b), slot(b), slot(b), m.place.at(uly=onward))
         yield
 
 
@@ -707,7 +733,7 @@
     scale = 1.0 / math.sqrt(key)
     at_s = 2 * key + val
 
-    def start_streams(m, hid_ref, dec_ref, pk_ref, ow_ref, gu_ref, hall, dall, wall, oall, gall):
+    def start_streams(m, hid_ref, dec_ref, pk_ref, gu_ref, hall, dall, wall, gall):
         p = m.place
         u = p.uly
 
@@ -762,69 +788,6 @@
                 m.arrive(("Y", q, us), tile)
                 m.send(("Z", q, us), tile, tile, p.at(ctx=p.xn))
 
-        def out_proj():
-            head_dp, head_u = lax.rem(p.ctx, 2), p.dp * 2 + lax.div(p.ctx, 2)
-            source_dp, source_ctx = u // 2, 2 * (u % 2) + p.dp
-
-            def column(part, c):
-                return oall.at[part, :, pl.ds(pl.multiple_of(c * quarter, quarter), quarter)]
-
-            own = [
-                (head_dp == p.dp) & (p.ctx == j) & (head_u == u) for j in range(4)
-            ]
-            for j in range(4):
-                there = oall.at[u, :, pl.ds(j * quarter, quarter)]
-                here = pltpu.make_async_copy(
-                    ow_ref.at[j], there, m.send_sems.at[m.number("O")]
-                )
-
-                @pl.when(own[j])
-                def _(here=here):
-                    here.start()
-                    here.wait()
-
-                other = pltpu.make_async_remote_copy(
-                    src_ref=ow_ref.at[j],
-                    dst_ref=there,
-                    send_sem=m.send_sems.at[m.number(("S", j))],
-                    recv_sem=m.recv_sems.at[m.number(("o", u))],
-                    device_id=(head_dp, j, head_u),
-                    device_id_type=MESH,
-                )
-                pl.when(jnp.logical_not(own[j]))(other.start)
-            for _ in range(7):
-                yield
-            for us in range(4):
-                mine = (source_dp == p.dp) & (source_ctx == p.ctx) & (us == u)
-
-                @pl.when(jnp.logical_not(mine))
-                def _(us=us):
-                    m.arrive(("o", us), column(us, p.ctx))
-
-            yield
-            mine = column(pl.ds(0, 4), p.ctx)
-            m.send("ox", mine, mine, p.at(ctx=p.xn))
-            m.send("oy", mine, mine, p.at(ctx=p.yn))
-            yield
-            low, high = pl.ds(0, 2), pl.ds(2, 2)
-            m.arrive("ox", column(pl.ds(0, 4), p.xn))
-            m.send("o0", column(low, p.xn), column(low, p.xn), p.at(ctx=p.yn))
-            m.arrive("oy", column(pl.ds(0, 4), p.yn))
-            m.send("o1", column(high, p.yn), column(high, p.yn), p.at(ctx=p.xn))
-            yield
-            for j in range(4):
-                other = pltpu.make_async_remote_copy(
-                    src_ref=ow_ref.at[j],
-                    dst_ref=ow_ref.at[j],
-                    send_sem=m.send_sems.at[m.number(("S", j))],
-                    recv_sem=m.recv_sems.at[m.number(("o", u))],
-                    device_id=p.at(dp=p.other),
-                    device_id_type=MESH,
-                )
-                pl.when(jnp.logical_not(own[j]))(other.wait_send)
-            m.arrive("o0", column(low, p.dg))
-            m.arrive("o1", column(high, p.dg))
-
         def feed():
             mine = gall.at[p.dp * 4 + p.ctx]
             copy = m.local("F", gu_ref.at[p.dp * 4 + p.ctx], mine)
@@ -846,9 +809,71 @@
         return [
             attn(),
             later(line_gather(m, "h", hid_ref, hall, 6), 1),
-            later(out_proj(), 1),
             later(feed(), 6),
         ]
+
+    def quarter_of(oall, part, c):
+        return oall.at[part, :, pl.ds(pl.multiple_of(c * quarter, quarter), quarter)]
+
+    def out_rows_go(m, ow_ref, oall):
+        p = m.place
+        u = p.uly
+        head_dp, head_u = lax.rem(p.ctx, 2), p.dp * 2 + lax.div(p.ctx, 2)
+        found = []
+        for j in range(4):
+            there = oall.at[u, :, pl.ds(j * quarter, quarter)]
+            away = pltpu.make_async_remote_copy(
+                src_ref=ow_ref.at[j],
+                dst_ref=there,
+                send_sem=m.send_sems.at[m.number(("S", j))],
+                recv_sem=m.recv_sems.at[m.number(("o", u))],
+                device_id=(head_dp, j, head_u),
+                device_id_type=MESH,
+            )
+            here = (ow_ref.at[j], there, m.send_sems.at[m.number("O")])
+            own = (head_dp == p.dp) & (p.ctx == j) & (head_u == u)
+            found.append((own, away, here))
+        return found
+
+    def out_start(m, ow_ref, oall):
+        for own, away, here in out_rows_go(m, ow_ref, oall):
+
+            @pl.when(own)
+            def _(here=here):
+                copy = pltpu.make_async_copy(*here)
+                copy.start()
+                copy.wait()
+
+            pl.when(jnp.logical_not(own))(away.start)
+
+    def out_share(m, ow_ref, oall):
+        p = m.place
+        u = p.uly
+        for us in range(4):
+            mine = (u // 2 == p.dp) & (2 * (u % 2) + p.dp == p.ctx) & (us == u)
+
+            @pl.when(jnp.logical_not(mine))
+            def _(us=us):
+                m.arrive(("o", us), quarter_of(oall, us, p.ctx))
+
+        mine = quarter_of(oall, pl.ds(0, 4), p.ctx)
+        m.send("ox", mine, mine, p.at(ctx=p.xn))
+        m.send("oy", mine, mine, p.at(ctx=p.yn))
+        for own, away, _ in out_rows_go(m, ow_ref, oall):
+            pl.when(jnp.logical_not(own))(away.wait_send)
+
+    def out_relay(m, oall):
+        p = m.place
+        low, high = pl.ds(0, 2), pl.ds(2, 2)
+        m.arrive("ox", quarter_of(oall, pl.ds(0, 4), p.xn))
+        m.send("o0", quarter_of(oall, low, p.xn), quarter_of(oall, low, p.xn), p.at(ctx=p.yn))
+        m.arrive("oy", quarter_of(oall, pl.ds(0, 4), p.yn))
+        m.send("o1", quarter_of(oall, high, p.yn), quarter_of(oall, high, p.yn), p.at(ctx=p.xn))
+
+    def out_end(m, oall):
+        p = m.place
+        m.arrive("o0", quarter_of(oall, pl.ds(0, 2), p.dg))
+        m.arrive("o1", quarter_of(oall, pl.ds(2, 2), p.dg))
 
     def kernel(
         hid_ref, cot_ref, dec_ref, pk_ref, ow_ref, gu_ref, wd_ref,
@@ -869,9 +894,12 @@
 
         spread = []
         for u in range(4):
-            for tag, own, out in (("g", gall, gu_all), ("e", wd_ref, wd_all)):
-                m = Mover(Place(u), names, send, recv, lambda out=out: out.at[0])
-                spread.append((u, m, line_spread(m, tag, own, out)))
+            for tag, own, slot in (
+                ("g", gall, lambda b: gu_all.at[:, b]),
+                ("e", wd_ref, lambda b: wd_all.at[b]),
+            ):
+                m = Mover(Place(u), names, send, recv, lambda slot=slot: slot(0))
+                spread.append((u, m, line_spread(m, tag, own, slot)))
 
         def spread_on(u):
             for v, _, stream in spread:
@@ -881,9 +909,10 @@
         def first(u):
             m = Mover(Place(u), names, send, recv)
             together(
-                start_streams(m, hid_ref, dec_ref, pk_ref, ow_ref, gu_ref, s1, dall, wall, oall, gall)
+                start_streams(m, hid_ref, dec_ref, pk_ref, gu_ref, s1, dall, wall, gall)
             )
             m.finish()
+            out_start(Mover(Place(u), names, send, recv), ow_ref, oall)
             spread_on(u)
 
         for_each(first)
@@ -932,6 +961,11 @@
             common, "t", upd, upds, state_slot, (pl.ds(0, 1), pl.ds(1, 1)), pair=False
         )
         next(states)
+        whole = [
+            Mover(Place(u), names, send, recv, lambda: quarter_of(oall, pl.ds(0, 4), 0))
+            for u in range(4)
+        ]
+        for_each(lambda u: out_share(whole[u], ow_ref, oall))
 
         def intra(c, carry):
             s, h = lax.div(c, 2), lax.rem(c, 2)
@@ -951,8 +985,10 @@
 
         lax.fori_loop(0, 2, intra, 0)
         next(states)
+        out_relay(common, oall)
         for_each(spread_on)
         lax.fori_loop(2, 4, intra, 0)
+        out_end(common, oall)
         for i in range(4):
             w2d[i * out_rows : (i + 1) * out_rows, :] = oall[i]
         for _ in states:
@@ -1016,6 +1052,7 @@
 
         def last(u):
             spread_on(u)
+            whole[u].finish()
             for v, m, _ in spread:
                 if u == v:
                     m.finish()
@@ -1046,10 +1083,10 @@
         ((both, 1), F32, vmem),
         ((both, val), BF16, vmem),
         ((tokens, width), F32, vmem),
-        ((8, tokens, width), BF16, hbm),
-        ((8, tokens, width), BF16, hbm),
-        ((4, 8, rows, ff2), BF16, hbm),
-        ((4, out_rows, width), BF16, hbm),
+        ((8, tokens, width), BF16, vmem),
+        ((8, tokens, width), BF16, vmem),
+        ((8, 4, rows, ff2), BF16, vmem),
+        ((4, out_rows, width), BF16, vmem),
     ]
     return pl.pallas_call(
         kernel,
@@ -1082,32 +1119,161 @@
     )(hidden, cot, decay, packed, outw, gu, w_down)
 
 
-def reduce_plane(part, down, number):
-    _, tokens, width = part.shape
-
-    def streams(m, part_ref, down_ref, out, dout, sib, sums, got, got2, right, left):
-        return [
-            plane_reduce(m, "s", part_ref, out, sib, sums, got, got2),
-            line_reduce(m, "d", lambda b: down_ref.at[b], dout, None, right, left),
+def feed_forward(scaled, top, w_gu, w_dn, residual, cot, gains):
+    _, tokens, width = scaled.shape
+    out_rows = w_dn.shape[1]
+    rows, ff2 = w_gu.shape[2:]
+    ff = ff2 // 2
+    block = 4 * tokens
+
+    def kernel(
+        s2_ref, top_ref, gu_ref, wd_ref, res_ref, cot_ref, gain_ref, grad, grad_low, term, dout, lo, ggu,
+        w_d, prod, grad_gu, part, down, total, sib, sums, got, got2, right, left, send, recv,
+    ):
+        uly = lax.axis_index(ULY)
+        names = {}
+        p = Place(uly)
+        greet(line_partners(p) + plane_partners(p)[1:])
+        common = Mover(p, names, send, recv)
+        movers = [
+            Mover(Place(u), names, send, recv, lambda: halves_of_columns(right.at[0], 0))
+            for u in range(4)
         ]
-
-    return run_kernel(
-        "reduce_plane",
-        number,
-        4,
-        lambda p: line_partners(p) + plane_partners(p)[1:],
-        streams,
-        [((tokens, width), F32, VMEM), (down.shape[1:], F32, VMEM)],
-        [(part, VMEM), (down, VMEM)],
-        [
-            ((4, tokens, width), BF16),
-            ((4, tokens, width), BF16),
-            ((2, tokens, width), BF16),
-            ((tokens, width), BF16),
-            (down.shape, BF16),
-            (down.shape, BF16),
+        lines = [
+            line_reduce(m, "d", lambda b: down.at[b], dout, None, right, left, halves_of_columns)
+            for m in movers
+        ]
+
+        def for_each(body):
+            for u in range(4):
+                pl.when(uly == u)(functools.partial(body, u))
+
+        for i in range(4):
+            w_d[i * out_rows : (i + 1) * out_rows, :] = wd_ref[i]
+
+        def weights():
+            return gu_ref[...].reshape(32 * rows, ff2)
+
+        def tokens_of(s):
+            here = pl.ds(pl.multiple_of(s * block, block), block)
+            lhs = s2_ref[pl.ds(4 * s, 4)].reshape(block, width)
+            pre = matmul(lhs, weights())
+            gate_pre, up_pre = pre[:, :ff], pre[:, ff:]
+            grad_product = dot_nt(top_ref[pl.ds(4 * s, 4)].reshape(block, width), w_d[...])
+            sigma = jax.nn.sigmoid(gate_pre)
+            act = gate_pre * sigma
+            prod[here, :] = (act * up_pre).astype(BF16)
+            slope = sigma * (1.0 + gate_pre * (1.0 - sigma))
+            grad_gu[here, :ff] = (grad_product * up_pre * slope).astype(BF16)
+            grad_gu[here, ff:] = (grad_product * act).astype(BF16)
+
+        def tokens_back(s):
+            here = pl.ds(pl.multiple_of(s * block, block), block)
+
+            def back(n, carry):
+                at = pl.ds(pl.multiple_of(n * 512, 512), 512)
+                right_side = gu_ref[pl.ds(2 * n, 2)].reshape(512, ff2)
+                value = dot_nt(grad_gu[here, :], right_side).astype(BF16)
+                part[pl.ds(4 * s, 4), :, at] = value.reshape(4, tokens, 512)
+                return carry
+
+            lax.fori_loop(0, width // 512, back, 0)
+
+        reduced = plane_reduce(common, "s", part, total, sib, sums, got, got2)
+        tokens_of(p.other)
+        tokens_of(p.dp)
+
+        def down_grad(n, carry):
+            at = pl.ds(pl.multiple_of(n * 512, 512), 512)
+            value = dot_t(prod[...], top_ref[:, :, at].reshape(2 * block, 512)).astype(BF16)
+            for i in range(4):
+                down[i, :, at] = value[i * out_rows : (i + 1) * out_rows]
+            return carry
+
+        lax.fori_loop(0, width // 512, down_grad, 0)
+        for_each(lambda u: next(lines[u]))
+        tokens_back(p.other)
+        next(reduced)
+        tokens_back(p.dp)
+        next(reduced)
+
+        def up_grad(n, carry):
+            at = pl.ds(pl.multiple_of(n * 4 * rows, 4 * rows), 4 * rows)
+            value = dot_t(s2_ref[:, :, at].reshape(2 * block, 4 * rows), grad_gu[...])
+            ggu[n] = value.astype(BF16).reshape(4, rows, ff2)
+            return carry
+
+        lax.fori_loop(0, 4, up_grad, 0)
+        next(reduced)
+        lax.fori_loop(4, 8, up_grad, 0)
+        for_each(lambda u: next(lines[u]))
+
+        def out_part(n, carry):
+            at = pl.ds(pl.multiple_of(n * 512, 512), 512)
+            value = matmul(prod[...], w_d[:, at]).astype(BF16)
+            lo[:, :, at] = value.reshape(8, tokens, 512)
+            return carry
+
+        lax.fori_loop(0, width // 512, out_part, 0)
+        for _ in reduced:
+            pass
+
+        def back(i, carry):
+            at = pl.ds(pl.multiple_of(i * 16, 16), 16)
+            normed, inverse = normalize(res_ref[at, :])
+            scaled_grad = total[at, :]
+            value = cot_ref[at, :].astype(F32) + norm_back(
+                scaled_grad * gain_ref[1:2, :], normed, inverse
+            )
+            grad[at, :] = value
+            grad_low[at, :] = value.astype(BF16)
+            return carry + jnp.sum(scaled_grad * normed, axis=0, keepdims=True)
+
+        term[...] = lax.fori_loop(0, tokens // 16, back, jnp.zeros((1, width), F32))
+
+        def last(u):
+            for _ in lines[u]:
+                pass
+            movers[u].finish()
+
+        for_each(last)
+        common.finish()
+        assert len(names) <= N_SEMS
+
+    vmem = pl.BlockSpec(memory_space=VMEM)
+    return pl.pallas_call(
+        kernel,
+        out_shape=[
+            jax.ShapeDtypeStruct((tokens, width), F32),
+            jax.ShapeDtypeStruct((tokens, width), BF16),
+            jax.ShapeDtypeStruct((1, width), F32),
+            jax.ShapeDtypeStruct((out_rows, width), F32),
+            jax.ShapeDtypeStruct((8, tokens, width), BF16),
+            jax.ShapeDtypeStruct((8, 4, rows, ff2), BF16),
         ],
-    )
+        in_specs=[vmem] * 7,
+        out_specs=[vmem] * 6,
+        scratch_shapes=[
+            pltpu.VMEM((4 * out_rows, width), BF16),
+            pltpu.VMEM((2 * block, ff), BF16),
+            pltpu.VMEM((2 * block, ff2), BF16),
+            pltpu.VMEM((8, tokens, width), BF16),
+            pltpu.VMEM((4, out_rows, width), BF16),
+            pltpu.VMEM((tokens, width), F32),
+            pltpu.VMEM((4, tokens, width), BF16),
+            pltpu.VMEM((4, tokens, width), BF16),
+            pltpu.VMEM((2, tokens, width), BF16),
+            pltpu.VMEM((tokens, width), BF16),
+            pltpu.VMEM((4, out_rows, width), BF16),
+            pltpu.VMEM((4, out_rows, width), BF16),
+            pltpu.SemaphoreType.DMA((N_SEMS,)),
+            pltpu.SemaphoreType.DMA((N_SEMS,)),
+        ],
+        name="feed_forward",
+        compiler_params=pltpu.CompilerParams(
+            collective_id=3, has_side_effects=True, vmem_limit_bytes=62 << 20
+        ),
+    )(scaled, top, w_gu, w_dn, residual, cot, gains)
 
 
 def attention_back(
@@ -1131,9 +1297,18 @@
         place = Place(uly)
         greet(line_partners(place) + plane_partners(place)[1:])
         common = Mover(place, names, send, recv)
-        movers = [Mover(Place(u), names, send, recv, lambda: right.at[0]) for u in range(4)]
+        movers = [Mover(Place(u), names, send, recv, lambda: right.at[0, 0]) for u in range(4)]
         ways = [
-            line_reduce(movers[u], "f", lambda b: g_ref.at[:, :, b], gsum, None, right, left)
+            line_reduce(
+                movers[u],
+                "f",
+                lambda b: g_ref.at[:, :, b],
+                gsum,
+                None,
+                right,
+                left,
+                lambda view, i: view.at[i],
+            )
             for u in range(4)
         ]
 
@@ -1155,6 +1330,7 @@
                 ]
             )
             m.finish()
+            next(ways[u])
 
         for_each(first)
 
@@ -1190,7 +1366,6 @@
             common, "t", gst, gsts, state_slot, (pl.ds(0, 1), pl.ds(1, 1)), pair=False
         )
         next(states)
-        for_each(lambda u: next(ways[u]))
 
         for s in range(2):
             at = pl.ds(s * block, block)
@@ -1272,32 +1447,28 @@
     )(own, lo, ggu, w_out, gated, normed, inverse, swish, q, k, v, weights, mask, state_in, reach, tail, cum)
 
 
-def last_exchange(part, grads, gout, gffn, inputs, term):
-    _, tokens, width = part.shape
-    rows, cols = grads.shape[3:]
+def last_exchange(grad_cat, w_all, scaled, gout, gffn, inputs, term):
+    tokens, width = inputs.shape
+    both, cols = grad_cat.shape
+    block = both // 2
     out_rows = gout.shape[1]
     quarter = width // 4
-    ff2 = gffn.shape[2]
+    rows, ff2 = gffn.shape[1:]
 
     def streams(
-        m, part_ref, g_ref, o_ref, f_ref, in_ref, t_ref, out, gall, oall, fall, gains,
-        sib, right, left, gotx, goty, gotx2, goty2, oxs, oys, ox2, oy2, away,
+        m, line, tile, o_ref, f_ref, in_ref, t_ref, out, gall, oall, fall, gains,
+        gotx, goty, gotx2, goty2, oxs, oys, ox2, oy2, away,
     ):
         p = m.place
         u = p.uly
 
         def attn():
-            for i, (cx, cy) in ((1, (p.dg, p.dg)), (0, (p.xn, p.yn))):
-                for t in range(4):
-                    m.send(("gx", i, t), g_ref.at[0, cx, t], gotx.at[i, t], p.at(ctx=p.xn))
-                    m.send(("gy", i, t), g_ref.at[1, cy, t], goty.at[i, t], p.at(ctx=p.yn))
-            yield
             for t in range(4):
                 m.arrive(("gx", 1, t), gotx.at[1, t])
-                add_up(gotx.at[1, t], [g_ref.at[0, p.yn, t], gotx.at[1, t]])
+                add_up(gotx.at[1, t], [tile(0, p.yn, t), gotx.at[1, t]])
                 m.send(("gy2", t), gotx.at[1, t], goty2.at[t], p.at(ctx=p.yn))
                 m.arrive(("gy", 1, t), goty.at[1, t])
-                add_up(goty.at[1, t], [g_ref.at[1, p.xn, t], goty.at[1, t]])
+                add_up(goty.at[1, t], [tile(1, p.xn, t), goty.at[1, t]])
                 m.send(("gx2", t), goty.at[1, t], gotx2.at[t], p.at(ctx=p.xn))
             yield
             yield
@@ -1308,7 +1479,7 @@
                 ):
                     m.arrive((tags[0], 0, t), got.at[0, t])
                     m.arrive((tags[1], t), got2.at[t])
-                    add_up(got.at[0, t], [g_ref.at[dp, p.ctx, t], got.at[0, t], got2.at[t]])
+                    add_up(got.at[0, t], [tile(dp, p.ctx, t), got.at[0, t], got2.at[t]])
                     there = gall.at[p.dp * 4 + u]
                     if t == u:
 
@@ -1428,7 +1599,7 @@
             copy.wait()
 
         def tokens_stream():
-            yield from line_reduce(m, "s", lambda i: part_ref.at[i], out, sib, right, left)
+            yield from line
 
             def body(i, total):
                 at = pl.ds(pl.multiple_of(i * 16, 16), 16)
@@ -1466,36 +1637,115 @@
             gains[...] = mine
 
         return [
+            attn(),
             tokens_stream(),
-            attn(),
             later(out_proj(), 1),
             later(feed(), 5),
         ]
 
-    return run_kernel(
-        "last",
-        2,
-        4,
-        everyone,
-        streams,
-        [
-            ((tokens, width), F32, VMEM),
-            ((8, rows, cols), BF16, HBM),
-            ((4, out_rows, quarter), BF16, HBM),
-            ((8, rows, ff2), BF16, HBM),
-            ((8, width), F32, VMEM),
+    def kernel(
+        cat_ref, wa_ref, s1_ref, o_ref, f_ref, in_ref, t_ref, out, gall, oall, fall, gains,
+        grads, part, sib, right, left, gotx, goty, gotx2, goty2, oxs, oys, ox2, oy2, away, send, recv,
+    ):
+        uly = lax.axis_index(ULY)
+        names = {}
+        p = Place(uly)
+        greet(everyone(p))
+        common = Mover(p, names, send, recv)
+
+        def for_each(body):
+            for u in range(4):
+                pl.when(uly == u)(functools.partial(body, u))
+
+        def tile(dp, c, t):
+            return grads.at[dp, c, pl.ds(t * rows, rows)]
+
+        def weight_grad(dp, c):
+            at = pl.ds(pl.multiple_of((dp * 4 + c) * 4 * rows, 4 * rows), 4 * rows)
+            grads[dp, c] = dot_t(s1_ref[:, :, at].reshape(both, 4 * rows), cat_ref[...]).astype(BF16)
+
+        def token_grad(i, carry):
+            s = jnp.where(i < 4, p.other, p.dp)
+            n = pl.ds(pl.multiple_of(lax.rem(i, 4) * quarter, quarter), quarter)
+            rows_s = pl.ds(pl.multiple_of(s * block, block), block)
+            value = dot_nt(cat_ref[rows_s, :], wa_ref[n, :cols]).astype(BF16)
+            part[pl.ds(4 * s, 4), :, n] = value.reshape(4, tokens, quarter)
+            return carry
+
+        def to_x(i, c):
+            weight_grad(0, c)
+            for t in range(4):
+                common.send(("gx", i, t), tile(0, c, t), gotx.at[i, t], p.at(ctx=p.xn))
+
+        def to_y(i, c):
+            weight_grad(1, c)
+            for t in range(4):
+                common.send(("gy", i, t), tile(1, c, t), goty.at[i, t], p.at(ctx=p.yn))
+
+        to_x(1, p.dg)
+        to_y(1, p.dg)
+        lax.fori_loop(0, 8, token_grad, 0)
+        movers = [
+            Mover(
+                Place(u), names, send, recv, lambda: halves_of_rows(sib.at[0], 0), lambda: sib.at[0]
+            )
+            for u in range(4)
+        ]
+        lines = [
+            line_reduce(m, "s", lambda i: part.at[i], out, sib, right, left) for m in movers
+        ]
+        for_each(lambda u: next(lines[u]))
+        to_x(0, p.xn)
+        to_y(0, p.yn)
+        weight_grad(0, p.yn)
+        weight_grad(1, p.xn)
+        weight_grad(0, p.ctx)
+        weight_grad(1, p.ctx)
+
+        def rest(u):
+            m = Mover(Place(u), names, send, recv)
+            together(
+                streams(
+                    m, lines[u], tile, o_ref, f_ref, in_ref, t_ref, out, gall, oall, fall, gains,
+                    gotx, goty, gotx2, goty2, oxs, oys, ox2, oy2, away,
+                )
+            )
+            m.finish()
+            movers[u].finish()
+
+        for_each(rest)
+        common.finish()
+        assert len(names) <= N_SEMS
+
+    vmem, hbm = pl.BlockSpec(memory_space=VMEM), pl.BlockSpec(memory_space=HBM)
+    return pl.pallas_call(
+        kernel,
+        out_shape=[
+            jax.ShapeDtypeStruct((tokens, width), F32),
+            jax.ShapeDtypeStruct((8, rows, cols), BF16),
+            jax.ShapeDtypeStruct((4, out_rows, quarter), BF16),
+            jax.ShapeDtypeStruct((8, rows, ff2), BF16),
+            jax.ShapeDtypeStruct((8, width), F32),
         ],
-        [(part, VMEM), (grads, VMEM), (gout, VMEM), (gffn, HBM), (inputs, VMEM), (term, VMEM)],
-        [
-            *[((4, tokens, width), BF16)] * 3,
-            *[((2, 4, rows, cols), BF16)] * 2,
-            *[((4, rows, cols), BF16)] * 2,
-            *[((2, 2, out_rows, quarter), BF16)] * 2,
-            *[((2, out_rows, quarter), BF16)] * 2,
-            ((7, 8, width), F32),
+        in_specs=[vmem, vmem, vmem, vmem, hbm, vmem, vmem],
+        out_specs=[vmem, hbm, hbm, hbm, vmem],
+        scratch_shapes=[
+            pltpu.VMEM((2, 4, 4 * rows, cols), BF16),
+            pltpu.VMEM((8, tokens, width), BF16),
+            *[pltpu.VMEM((4, tokens, width), BF16)] * 3,
+            *[pltpu.VMEM((2, 4, rows, cols), BF16)] * 2,
+            *[pltpu.VMEM((4, rows, cols), BF16)] * 2,
+            *[pltpu.VMEM((2, 2, out_rows, quarter), BF16)] * 2,
+            *[pltpu.VMEM((2, out_rows, quarter), BF16)] * 2,
+            pltpu.VMEM((7, 8, width), F32),
+            pltpu.SemaphoreType.DMA((N_SEMS,)),
+            pltpu.SemaphoreType.DMA((N_SEMS,)),
         ],
-        vmem=56,
-    )
+        name="last",
+        compiler_params=pltpu.CompilerParams(
+            collective_id=2, has_side_effects=True, vmem_limit_bytes=62 << 20
+        ),
+    )(grad_cat, w_all, scaled, gout, gffn, inputs, term)
 
 
 def local(
@@ -1523,45 +1773,20 @@
 
     gains = jnp.pad(jnp.stack([gain_attn, gain_ffn], axis=1), ((0, 0), (0, 30)))
     packed, outw, gate_up = pack(w_query, w_key, w_value, w_swish, w_output, w_gate, w_up, gains)
-    attn_cols = 2 * key + 2 * val
     block = 4 * tokens
     (
         w_all, scaled_one, w_out, q, k, v, swish_pre, weights, mask, state_in, reach, tail, cum,
         gains, head_normed, head_inverse, gated, residual, scaled_two, top_all, w_gu, w_dn,
     ) = forward(hidden_in[0], cotangent[0], log_decay[0], packed, outw, gate_up, w_down)
-    w_attn = w_all[:, :attn_cols]
-    gain_one, gain_two = gains[0], gains[1]
-    scaled_one = scaled_one.reshape(8 * tokens, width)
-    scaled_two = scaled_two.reshape(8 * tokens, width)
-    top_all = top_all.reshape(8 * tokens, width)
-    w_gu = w_gu.transpose(1, 0, 2, 3).reshape(32 * rows, 2 * ff)
-    w_dn = w_dn.reshape(4 * out_rows, width)
+    gain_one = gains[0]
+    grad_residual, grad_y, gain_two_term, grad_down, layer_part, ggu = feed_forward(
+        scaled_two, top_all, w_gu, w_dn, residual, cotangent[0], gains
+    )
     inputs = hidden_in[0].astype(f32)
-    normed_two, inverse_two = normalize(residual)
-    gu = matmul(scaled_two, w_gu)
-    gate_pre, up_pre = gu[:, :ff], gu[:, ff:]
-    gate_act = jax.nn.silu(gate_pre)
-    product = (gate_act * up_pre).astype(bf16)
-    grad_product = dot_nt(top_all, w_dn)
-    grad_gu = jnp.concatenate(
-        [
-            (grad_product * up_pre * swish_slope(gate_pre)).astype(bf16),
-            (grad_product * gate_act).astype(bf16),
-        ],
-        axis=1,
-    )
-    gs2, grad_down = reduce_plane(
-        dot_nt(grad_gu, w_gu).astype(bf16).reshape(8, tokens, width),
-        dot_t(product, top_all).astype(bf16).reshape(4, out_rows, width),
-        6,
-    )
-    grad_top = cotangent[0].astype(f32)
-    gain_two_term = jnp.sum(gs2 * normed_two, axis=0, keepdims=True)
-    grad_residual = grad_top + norm_back(gs2 * gain_two, normed_two, inverse_two)
     grad_cat, out_part, g_out, ggu = attention_back(
-        grad_residual.astype(bf16),
-        matmul(product, w_dn).astype(bf16).reshape(8, tokens, width),
-        dot_t(scaled_two, grad_gu).astype(bf16).reshape(2, 4, 4, rows, 2 * ff),
+        grad_y,
+        layer_part,
+        ggu.reshape(2, 4, 4, rows, 2 * ff),
         w_out,
         gated,
         head_normed,
@@ -1579,8 +1804,9 @@
     )
     layer_out = residual + out_part
     gs1, gcat, g_out, ggu, gain_terms = last_exchange(
-        dot_nt(grad_cat, w_attn).astype(bf16).reshape(8, tokens, width),
-        dot_t(scaled_one, grad_cat).astype(bf16).reshape(2, 4, 4, rows, attn_cols),
+        grad_cat,
+        w_all,
+        scaled_one,
         g_out,
         ggu.reshape(8, rows, 2 * ff),
         hidden_in[0],

time: 613 us -> 524 us (0.85)
  matrix products: 46.3 us -> 0 us
  local copies, waits for them, and re-layouts: 35.9 us -> 16.5 us
  Pallas kernels: 507 us -> 494 us
  other arithmetic: 11 us -> 2.98 us
    dot_general x8 -> x0, matrix products: 46.3 us -> none  [the longest x3 20.2 us: dot_nt(): lax.dot_general(left, right, (((1,), (1,)), ((), ())), preferred_element_...]
    pallas_call x1, Pallas kernels: 231 us -> 211 us  [forward(): pl.pallas_call(kernel, out_shape=[jax.ShapeDtypeStruct(shape, kind) for s...]
    convert_element_type x2 -> x0, local copies, waits for them, and re-layouts: 14.4 us -> none  [the longest x1 8.32 us: local(): dot_t(scaled_one, grad_cat).astype(bf16).reshape(2, 4, 4, rows, attn_cols)]
    pallas_call x2, Pallas kernels: 166 us -> 178 us  [the longest x1 114 us: last_exchange(): pl.pallas_call(kernel, out_shape=[jax.ShapeDtypeStruct((tokens, width), F...]
    unnamed x51 -> x39, local copies, waits for them, and re-layouts: 13.1 us -> 14.3 us
where the time goes in v4:
time: 524 us; the launch traced here: 515 us
  Pallas kernels  494 us (94%)
  local copies, waits for them, and re-layouts  16.5 us (3%)
    pallas_call x1, Pallas kernels, forward(): pl.pallas_call(kernel, out_shape=[jax.ShapeDtypeStruct(shape, kind) for s...  211 us
    pallas_call x1, Pallas kernels, last_exchange(): pl.pallas_call(kernel, out_shape=[jax.ShapeDtypeStruct((tokens, width), F...  114 us
    pallas_call x1, Pallas kernels, attention_back(): pl.pallas_call(kernel, out_shape=[jax.ShapeDtypeStruct((both, 2 * key + 2...  102 us
    pallas_call x1, Pallas kernels, feed_forward(): pl.pallas_call(kernel, out_shape=[jax.ShapeDtypeStruct((tokens, width), F...  63.7 us
    unnamed x39, local copies, waits for them, and re-layouts  14.3 us

profile of v4, /device:TPU:9, one launch (start us, length us, event | category | flops | bytes accessed | tf_op | source)
XLA Modules:
  0.0 514.7 jit_solution(15305277035614469181)
XLA Ops:
  0.6 0.7 pad_maximum_fusion
  1.3 0.1 copy.27
  1.5 1.0 copy-done.5
  2.5 1.0 copy-done.7
  3.5 1.0 copy-done.8
  4.5 1.0 copy-done.9
  5.5 1.0 copy-done.10
  6.5 0.9 copy-done.11
  7.5 0.9 copy-done.12
  8.4 0.7 pack.1
  9.1 1.1 copy-done
  10.2 0.9 copy-done.2
  11.2 0.8 copy-done.4
  11.9 210.9 %forward.1 = (bf16[2048,1408]{1,0:T(8,128)(2,1)}, bf16[8,128,2048]{2,1,0:T(8,128)(2,1)}, bf16[432,2048]{1,0:T(8,128)(2,1)}, bf16[2,512,256]{2,1,0:T(8,128)(2,1)}...) custom-call(bf16[128,2048]{1,0:T(8,128)(2,1)} %bitcast.19, ...), custom_call_target="tpu_custom_call" | custom-call | tf_op jit(solution)/shard_map/forward/pallas_call | solution.py:1091
  222.9 63.7 %feed_forward.1 = (f32[128,2048]{1,0:T(8,128)}, bf16[128,2048]{1,0:T(8,128)(2,1)}, f32[1,2048]{1,0:T(1,128)}, f32[108,2048]{1,0:T(8,128)}, bf16[8,128,2048]{2,1,...) custom-call(bf16[8,128,2048]{2,1,0:T(8,128)(2,1)} %get-tuple-element.63.s2_ref, ...), custom_call_target="tpu_custom_call" | custom-call | tf_op jit(solution)/shard_map/feed_forward/pallas_call | solution.py:1244
  286.6 102.1 %attention_back.1 = (bf16[1024,1376]{1,0:T(8,128)(2,1)}, f32[128,2048]{1,0:T(8,128)}, bf16[4,108,2048]{2,1,0:T(8,128)(2,1)}, bf16[2,4,64,864]{3,2,1,0:T(8,128)(2,1)}) custom-call(bf16[128,2048]{1,0:T(8,128)(2,1)} %get-tuple-element.68.own_ref, bf16[8,128,2048]{2,1,0:T(8,128)(2,1)} %get-tuple-element.69.lo_ref, bf16[2,4,4,64,864]{4,3,2,1,0:T(8,128)(2,1)} %bitcast.21, ...), custom_call_target="tpu_custom_call" | custom-call | tf_op jit(solution)/shard_map/attention_back/pallas_call | solution.py:1415
  388.7 0.0 copy-start.13
  388.7 0.0 copy-start.15
  388.7 114.0 %last.1 = (f32[128,2048]{1,0:T(8,128)}, bf16[8,64,1376]{2,1,0:T(8,128)(2,1)}, bf16[4,108,512]{2,1,0:T(8,128)(2,1)}, bf16[8,64,864]{2,1,0:T(8,128)(2,1)}, f32[8,2048]{1,0:T(8,128)}) custom-call(bf16[1024,1376]{1,0:T(8,128)(2,1)} %get-tuple-element.87.cat_ref, bf16[2048,1408]{1,0:T(8,128)(2,1)} %get-tuple-element.88.wa_ref, ...), custom_call_target="tpu_custom_call" | custom-call | tf_op jit(solution)/shard_map/last/pallas_call | solution.py:1721
  502.7 0.0 copy-start.1
  502.7 1.4 copy-done.1
  504.1 1.2 copy-done.3
  505.2 1.0 copy-done.6
  506.3 2.9 unpack.1
  509.2 0.8 slice.9
  510.0 0.2 fusion.7
  510.2 0.0 copy-done.14
  510.2 0.3 fusion.2
  510.6 1.8 fusion.6
  512.3 0.7 constant_dynamic-slice_fusion
  513.1 0.5 slice_bitcast_fusion
  513.6 0.9 copy.29
  (24 shorter events, 0.1 us)
Async XLA Ops:
  1.5 1.0 copy-start.5
  2.5 1.0 copy-start.7
  3.5 1.0 copy-start.8
  4.5 1.0 copy-start.9
  5.5 1.0 copy-start.10
  6.5 0.9 copy-start.11
  7.5 0.9 copy-start.12
  9.1 1.1 copy-start
  10.2 0.9 copy-start.2
  11.2 0.8 copy-start.4
  388.7 121.3 %copy-start.13 = (bf16[1,128,2048]{2,1,0:T(8,128)(2,1)S(1)}, bf16[1,128,2048]{2,1,0:T(8,128)(2,1)}, u32[]{:S(2)}) copy-start(bf16[1,128,2048]{2,1,0:T(8,128)(2,1)} %param.13) | copy-start | bytes 1572868
  388.7 121.8 %copy-start.15 = (f32[128,2048]{1,0:T(8,128)S(1)}, f32[128,2048]{1,0:T(8,128)}, u32[]{:S(2)}) copy-start(f32[128,2048]{1,0:T(8,128)} %get-tuple-element.62.res_ref) | copy-start | bytes 3145732
  502.7 1.4 copy-start.1
  504.1 1.2 copy-start.3
  505.2 1.0 copy-start.6
  506.3 3.9 copy-start.14
  506.3 4.3 copy-start.16
  506.3 4.3 copy-start.17
  510.5 3.1 copy-start.18

commit v5 on v4

--- a/solution.py
+++ b/solution.py
@@ -399,24 +399,41 @@
     lax.fori_loop(0, (rows if by_rows else columns) // step, body, 0)
 
 
+def halves_of_rows(view, i):
+    rows = view.shape[0] // 2
+    return view.at[pl.ds(i * rows, rows)]
+
+
+def halves_of_columns(view, i):
+    columns = view.shape[1] // 2
+    return view.at[:, pl.ds(i * columns, columns)]
+
+
 def line_gather(m, tag, own, out, pause=1):
     p = m.place
     u = p.uly
-    copy = m.local(tag + "=", own, out.at[p.dp * 4 + u])
-    if u < 3:
-        m.send((tag, "r", u), own, out.at[p.dp * 4 + u], p.at(uly=u + 1))
-    if u > 0:
-        m.send((tag, "l", u), own, out.at[p.dp * 4 + u], p.at(uly=u - 1))
-    m.send((tag, "c", u), own, out.at[p.dp * 4 + u], p.at(dp=p.other))
+    mine = out.at[p.dp * 4 + u]
+    copy = m.local((tag, "="), own, mine)
+    for i in range(2):
+        src, dst = halves_of_rows(own, i), halves_of_rows(mine, i)
+        if u < 3:
+            m.send((tag, "r", u, i), src, dst, p.at(uly=u + 1))
+        if u > 0:
+            m.send((tag, "l", u, i), src, dst, p.at(uly=u - 1))
+    m.send((tag, "c", u), own, mine, p.at(dp=p.other))
     for _ in range(pause):
         yield
     for d in range(1, 4):
-        for way, b, onward in (("r", u - d, u + 1), ("l", u + d, u - 1)):
+        for i in range(2):
+            for way, b, onward in (("r", u - d, u + 1), ("l", u + d, u - 1)):
+                if 0 <= b <= 3:
+                    half = halves_of_rows(out.at[p.dp * 4 + b], i)
+                    m.arrive((tag, way, b, i), half)
+                    if 0 <= onward <= 3:
+                        m.send((tag, way, b, i), half, half, p.at(uly=onward))
+        for b in (u - d, u + d):
             if 0 <= b <= 3:
                 block = out.at[p.dp * 4 + b]
-                m.arrive((tag, way, b), block)
-                if 0 <= onward <= 3:
-                    m.send((tag, way, b), block, block, p.at(uly=onward))
                 m.send((tag, "c", b), block, block, p.at(dp=p.other))
         yield
     for b in range(4):
@@ -431,7 +448,7 @@
         return slot(out, p.dp, c, halves[i])
 
     mine = slot(out, p.dp, p.ctx, None)
-    copy = m.local(tag + "=", own, mine)
+    copy = m.local((tag, "="), own, mine)
     m.send((tag, "x"), own, mine, p.at(ctx=p.xn))
     m.send((tag, "y"), own, mine, p.at(ctx=p.yn))
     if pair:
@@ -460,16 +477,6 @@
         for i in range(2):
             m.arrive((tag, "c", 3 + i), slot(out, p.other, p.dg, halves[i]))
     copy.wait()
-
-
-def halves_of_rows(view, i):
-    rows = view.shape[0] // 2
-    return view.at[pl.ds(i * rows, rows)]
-
-
-def halves_of_columns(view, i):
-    columns = view.shape[1] // 2
-    return view.at[:, pl.ds(i * columns, columns)]
 
 
 def line_reduce(m, tag, part, out, sib, right, left, cut=halves_of_rows):
@@ -554,44 +561,64 @@
     add_up(out, [sums.at[p.ctx], got.at[0], got2])
 
 
-def run_kernel(name, number, branches, partners, streams, outs, ins, scratch=(), vmem=48, time=40):
-    def kernel(*refs):
-        send, recv = refs[-2:]
-        refs = refs[:-2]
-        uly = lax.axis_index(ULY)
-        names = {}
-        greet(partners(Place(uly)) if partners else [])
-
-        def body(u):
-            m = Mover(Place(u), names, send, recv)
-            together(streams(m, *refs))
-            m.finish()
-
-        if branches == 1:
-            body(uly)
-        else:
-            for u in range(4):
-                pl.when(uly == u)(functools.partial(body, u))
-        assert len(names) <= N_SEMS
-
+class Stage:
+    def __init__(self, loads, stores):
+        self.loads, self.stores, self.started = loads, stores, []
+        for copy in loads.values():
+            copy.start()
+
+    def need(self, *which):
+        for i in which:
+            self.loads.pop(i).wait()
+
+    def put(self, *which):
+        for i in which:
+            copy = self.stores.pop(i)
+            copy.start()
+            self.started.append(copy)
+
+    def end(self):
+        self.need(*list(self.loads))
+        self.put(*list(self.stores))
+        for copy in self.started:
+            copy.wait()
+
+
+def staged_call(kernel, name, ins, outs, scratch, remote=None):
+    in_held = [i for i, (_, held) in enumerate(ins) if held]
+    out_held = [i for i, (_, _, held) in enumerate(outs) if held]
+
+    def body(*refs):
+        given, results = list(refs[: len(ins)]), list(refs[len(ins) : len(ins) + len(outs)])
+        rest = refs[len(ins) + len(outs) :]
+        held, own, sems = rest[: len(in_held) + len(out_held)], rest[len(in_held) + len(out_held) : -1], rest[-1]
+        loads, stores = {}, {}
+        for j, i in enumerate(in_held):
+            loads[i] = pltpu.make_async_copy(given[i], held[j], sems.at[j])
+            given[i] = held[j]
+        for j, i in enumerate(out_held, len(in_held)):
+            stores[i] = pltpu.make_async_copy(held[j], results[i], sems.at[j])
+            results[i] = held[j]
+        stage = Stage(loads, stores)
+        kernel(stage, *given, *results, *own)
+        stage.end()
+
+    params = {} if remote is None else {"collective_id": remote, "has_side_effects": True}
     return pl.pallas_call(
-        kernel,
-        out_shape=[jax.ShapeDtypeStruct(*o[:2]) for o in outs],
-        in_specs=[pl.BlockSpec(memory_space=s) for _, s in ins],
-        out_specs=[pl.BlockSpec(memory_space=o[2]) for o in outs],
+        body,
+        out_shape=[jax.ShapeDtypeStruct(shape, kind) for shape, kind, _ in outs],
+        in_specs=[pl.BlockSpec(memory_space=HBM)] * len(ins),
+        out_specs=[pl.BlockSpec(memory_space=HBM)] * len(outs),
         scratch_shapes=[
-            *[pltpu.VMEM(shape, dtype) for shape, dtype in scratch],
-            pltpu.SemaphoreType.DMA((N_SEMS,)),
-            pltpu.SemaphoreType.DMA((N_SEMS,)),
+            *[pltpu.VMEM(ins[i][0].shape, ins[i][0].dtype) for i in in_held],
+            *[pltpu.VMEM(*outs[i][:2]) for i in out_held],
+            *[pltpu.VMEM(shape, kind) for shape, kind in scratch],
+            *([pltpu.SemaphoreType.DMA((N_SEMS,))] * 2 if remote is not None else []),
+            pltpu.SemaphoreType.DMA((len(in_held) + len(out_held),)),
         ],
         name=name,
-        cost_estimate=pl.CostEstimate(
-            flops=0, bytes_accessed=time * 3_700_000, transcendentals=0
-        ),
-        compiler_params=pltpu.CompilerParams(
-            collective_id=number, has_side_effects=True, vmem_limit_bytes=vmem << 20
-        ),
-    )(*[a for a, _ in ins])
+        compiler_params=pltpu.CompilerParams(vmem_limit_bytes=62 << 20, **params),
+    )(*[array for array, _ in ins])
 
 
 def everyone(p):
@@ -630,7 +657,8 @@
     key, val, ff, quarter = KEY_DIM, VALUE_DIM, w_gate.shape[1] // 8, width // 4
     cols = 2 * key + 2 * val + 32
 
-    def kernel(q, k, v, s, o, g, u, n, packed, outw, gu):
+    def kernel(stage, q, k, v, s, o, g, u, n, packed, outw, gu):
+        stage.need(*range(8))
         for d in range(2):
             for z in range(4):
                 h, i = 2 * z + d, 4 * d + z
@@ -645,23 +673,26 @@
         for j in range(4):
             outw[j] = o[:, j * quarter : (j + 1) * quarter]
 
-    return pl.pallas_call(
+    weights = (w_query, w_key, w_value, w_swish, w_output, w_gate, w_up, gains)
+    return staged_call(
         kernel,
-        out_shape=[
-            jax.ShapeDtypeStruct((8, rows, cols), BF16),
-            jax.ShapeDtypeStruct((4, out_rows, quarter), BF16),
-            jax.ShapeDtypeStruct((8, rows, 2 * ff), BF16),
+        "pack",
+        [(w, True) for w in weights],
+        [
+            ((8, rows, cols), BF16, True),
+            ((4, out_rows, quarter), BF16, True),
+            ((8, rows, 2 * ff), BF16, True),
         ],
-        name="pack",
-        compiler_params=pltpu.CompilerParams(vmem_limit_bytes=32 << 20),
-    )(w_query, w_key, w_value, w_swish, w_output, w_gate, w_up, gains)
+        [],
+    )
 
 
 def unpack(heads, outg, slices):
     rows, (_, out_rows, quarter) = heads.shape[1], outg.shape
     key, val, ff = KEY_DIM, VALUE_DIM, slices.shape[2] // 2
 
-    def kernel(hs, og, sl, q, k, v, s, o, g, u):
+    def kernel(stage, hs, og, sl, q, k, v, s, o, g, u):
+        stage.need(0, 1, 2)
         for d in range(2):
             for z in range(4):
                 h, i = 2 * z + d, 4 * d + z
@@ -675,19 +706,15 @@
         for j in range(4):
             o[:, j * quarter : (j + 1) * quarter] = og[j].astype(F32)
 
-    wide = jax.ShapeDtypeStruct((rows, 8 * key), F32)
-    wider = jax.ShapeDtypeStruct((rows, 8 * val), F32)
-    ffs = jax.ShapeDtypeStruct((rows, 8 * ff), F32)
-    return pl.pallas_call(
+    widths = (8 * key, 8 * key, 8 * val, 8 * val, 4 * quarter, 8 * ff, 8 * ff)
+    heights = (rows, rows, rows, rows, out_rows, rows, rows)
+    return staged_call(
         kernel,
-        out_shape=[
-            wide, wide, wider, wider,
-            jax.ShapeDtypeStruct((out_rows, 4 * quarter), F32),
-            ffs, ffs,
-        ],
-        name="unpack",
-        compiler_params=pltpu.CompilerParams(vmem_limit_bytes=32 << 20),
-    )(heads, outg, slices)
+        "unpack",
+        [(heads, True), (outg, True), (slices, True)],
+        [(shape, F32, True) for shape in zip(heights, widths)],
+        [],
+    )
 
 
 def line_spread(m, tag, own, slot):
@@ -809,7 +836,7 @@
         return [
             attn(),
             later(line_gather(m, "h", hid_ref, hall, 6), 1),
-            later(feed(), 6),
+            later(feed(), 2),
         ]
 
     def quarter_of(oall, part, c):
@@ -876,7 +903,7 @@
         m.arrive("o1", quarter_of(oall, pl.ds(2, 2), p.dg))
 
     def kernel(
-        hid_ref, cot_ref, dec_ref, pk_ref, ow_ref, gu_ref, wd_ref,
+        stage, hid_ref, cot_ref, dec_ref, pk_ref, ow_ref, gu_ref, wd_ref,
         w_all, s1_all, w2d, q_ref, k_ref, v_ref, sw_ref, w_ref, mask_ref, st_ref, reach_ref, tail_ref, cum_ref,
         gain_ref, hn_ref, hi_ref, ga_ref, res_ref, s2_all, top_all, gu_all, wd_all,
         wall, s1, oall, dall, gall, dec8, cols8, upd, upds, ret, part, sib, right, left, s2, send, recv,
@@ -885,6 +912,7 @@
         names = {}
         place = Place(uly)
         greet(everyone(place))
+        stage.need(0)
         common = Mover(place, names, send, recv)
         ctx = place.ctx
 
@@ -908,12 +936,19 @@
 
         def first(u):
             m = Mover(Place(u), names, send, recv)
+
+            def spread_stage():
+                out_start(Mover(Place(u), names, send, recv), ow_ref, oall)
+                spread_on(u)
+                yield
+
             together(
-                start_streams(m, hid_ref, dec_ref, pk_ref, gu_ref, s1, dall, wall, gall)
+                [
+                    *start_streams(m, hid_ref, dec_ref, pk_ref, gu_ref, s1, dall, wall, gall),
+                    later(spread_stage(), 8),
+                ]
             )
             m.finish()
-            out_start(Mover(Place(u), names, send, recv), ow_ref, oall)
-            spread_on(u)
 
         for_each(first)
         keep = [common.local("w", wall, w_all)]
@@ -947,6 +982,12 @@
             reach_ref[s] = jnp.exp(column) * scale
             tail_ref[s] = jnp.exp(dec8[s : s + 1, block - 1 : block] - column)
 
+        whole = [
+            Mover(Place(u), names, send, recv, lambda: quarter_of(oall, pl.ds(0, 4), 0))
+            for u in range(4)
+        ]
+        for_each(lambda u: out_share(whole[u], ow_ref, oall))
+
         for s in range(2):
             lhs = s1[4 * s : 4 * s + 4].reshape(block, width)
             q_ref[s] = matmul(lhs, wall[:, :key]).astype(BF16)
@@ -954,6 +995,8 @@
             rest = matmul(lhs, wall[:, 2 * key :])
             v_ref[s] = rest[:, :val].astype(BF16)
             sw_ref[pl.ds(s * block, block), :] = rest[:, val : 2 * val]
+        out_relay(common, oall)
+        for_each(spread_on)
         for s in range(2):
             k_tail = (k_ref[s].astype(F32) * tail_ref[s]).astype(BF16)
             upd[s] = dot_t(k_tail, v_ref[s]).astype(BF16)
@@ -961,11 +1004,6 @@
             common, "t", upd, upds, state_slot, (pl.ds(0, 1), pl.ds(1, 1)), pair=False
         )
         next(states)
-        whole = [
-            Mover(Place(u), names, send, recv, lambda: quarter_of(oall, pl.ds(0, 4), 0))
-            for u in range(4)
-        ]
-        for_each(lambda u: out_share(whole[u], ow_ref, oall))
 
         def intra(c, carry):
             s, h = lax.div(c, 2), lax.rem(c, 2)
@@ -985,8 +1023,6 @@
 
         lax.fori_loop(0, 2, intra, 0)
         next(states)
-        out_relay(common, oall)
-        for_each(spread_on)
         lax.fori_loop(2, 4, intra, 0)
         out_end(common, oall)
         for i in range(4):
@@ -1018,20 +1054,26 @@
             return carry
 
         lax.fori_loop(0, 4, outer, 0)
+        stage.put(*range(2, 17))
 
         def reduce(u):
             m = Mover(Place(u), names, send, recv)
             low = tokens // 2
+
+            def spread_stage():
+                spread_on(u)
+                yield
+
             together(
                 [
                     line_reduce(m, "s", lambda i: part.at[i], res_ref, sib, right, left),
                     plane_gather(
                         m, "C", cot_ref, top_all, token_slot, (pl.ds(0, low), pl.ds(low, low))
                     ),
+                    later(spread_stage(), 2),
                 ]
             )
             m.finish()
-            spread_on(u)
 
         for_each(reduce)
 
@@ -1063,60 +1105,55 @@
         common.finish()
         assert len(names) <= N_SEMS
 
-    vmem, hbm = pl.BlockSpec(memory_space=VMEM), pl.BlockSpec(memory_space=HBM)
-    outs = [
-        ((width, cols), BF16, hbm),
-        ((8, tokens, width), BF16, hbm),
-        ((4 * out_rows, width), BF16, vmem),
-        ((2, block, key), BF16, vmem),
-        ((2, block, key), BF16, vmem),
-        ((2, block, val), BF16, vmem),
-        ((both, val), F32, vmem),
-        ((2, block, block), BF16, vmem),
-        ((2, block, block), F32, vmem),
-        ((2, key, val), BF16, vmem),
-        ((2, block, 1), F32, vmem),
-        ((2, block, 1), F32, vmem),
-        ((8, block), F32, vmem),
-        ((8, width), F32, vmem),
-        ((both, val), F32, vmem),
-        ((both, 1), F32, vmem),
-        ((both, val), BF16, vmem),
-        ((tokens, width), F32, vmem),
-        ((8, tokens, width), BF16, vmem),
-        ((8, tokens, width), BF16, vmem),
-        ((8, 4, rows, ff2), BF16, vmem),
-        ((4, out_rows, width), BF16, vmem),
-    ]
-    return pl.pallas_call(
+    return staged_call(
         kernel,
-        out_shape=[jax.ShapeDtypeStruct(shape, kind) for shape, kind, _ in outs],
-        in_specs=[vmem, hbm, vmem, hbm, hbm, hbm, hbm],
-        out_specs=[spec for _, _, spec in outs],
-        scratch_shapes=[
-            pltpu.VMEM((width, cols), BF16),
-            pltpu.VMEM((8, tokens, width), BF16),
-            pltpu.VMEM((4, out_rows, width), BF16),
-            pltpu.VMEM((8, 2, block), F32),
-            pltpu.VMEM((8, rows, ff2), BF16),
-            pltpu.VMEM((8, block), F32),
-            pltpu.VMEM((block, 8), F32),
-            pltpu.VMEM((2, key, val), BF16),
-            pltpu.VMEM((4, 2, key, val), BF16),
-            pltpu.VMEM((both, val), F32),
-            pltpu.VMEM((8, tokens, width), BF16),
-            pltpu.VMEM((4, tokens, width), BF16),
-            pltpu.VMEM((4, tokens, width), BF16),
-            pltpu.VMEM((4, tokens, width), BF16),
-            pltpu.VMEM((tokens, width), BF16),
-            pltpu.SemaphoreType.DMA((N_SEMS,)),
-            pltpu.SemaphoreType.DMA((N_SEMS,)),
+        "forward",
+        [
+            (hidden, True), (cot, False), (decay, False), (packed, False), (outw, False), (gu, False), (w_down, False)
         ],
-        name="forward",
-        compiler_params=pltpu.CompilerParams(
-            collective_id=1, has_side_effects=True, vmem_limit_bytes=62 << 20
-        ),
-    )(hidden, cot, decay, packed, outw, gu, w_down)
+        [
+            ((width, cols), BF16, False),
+            ((8, tokens, width), BF16, False),
+            ((4 * out_rows, width), BF16, True),
+            ((2, block, key), BF16, True),
+            ((2, block, key), BF16, True),
+            ((2, block, val), BF16, True),
+            ((both, val), F32, True),
+            ((2, block, block), BF16, True),
+            ((2, block, block), F32, True),
+            ((2, key, val), BF16, True),
+            ((2, block, 1), F32, True),
+            ((2, block, 1), F32, True),
+            ((8, block), F32, True),
+            ((8, width), F32, True),
+            ((both, val), F32, True),
+            ((both, 1), F32, True),
+            ((both, val), BF16, True),
+            ((tokens, width), F32, True),
+            ((8, tokens, width), BF16, False),
+            ((8, tokens, width), BF16, False),
+            ((8, 4, rows, ff2), BF16, False),
+            ((4, out_rows, width), BF16, False),
+        ],
+        [
+            ((width, cols), BF16),
+            ((8, tokens, width), BF16),
+            ((4, out_rows, width), BF16),
+            ((8, 2, block), F32),
+            ((8, rows, ff2), BF16),
+            ((8, block), F32),
+            ((block, 8), F32),
+            ((2, key, val), BF16),
+            ((4, 2, key, val), BF16),
+            ((both, val), F32),
+            ((8, tokens, width), BF16),
+            ((4, tokens, width), BF16),
+            ((4, tokens, width), BF16),
+            ((4, tokens, width), BF16),
+            ((tokens, width), BF16),
+        ],
+        1,
+    )
 
 
 def feed_forward(scaled, top, w_gu, w_dn, residual, cot, gains):
@@ -1127,7 +1164,7 @@
     block = 4 * tokens
 
     def kernel(
-        s2_ref, top_ref, gu_ref, wd_ref, res_ref, cot_ref, gain_ref, grad, grad_low, term, dout, lo, ggu,
+        stage, s2_ref, top_ref, gu_ref, wd_ref, res_ref, cot_ref, gain_ref, grad, grad_low, term, dout, lo, ggu,
         w_d, prod, grad_gu, part, down, total, sib, sums, got, got2, right, left, send, recv,
     ):
         uly = lax.axis_index(ULY)
@@ -1148,6 +1185,7 @@
             for u in range(4):
                 pl.when(uly == u)(functools.partial(body, u))
 
+        stage.need(0, 1, 2, 3)
         for i in range(4):
             w_d[i * out_rows : (i + 1) * out_rows, :] = wd_ref[i]
 
@@ -1196,6 +1234,7 @@
         next(reduced)
         tokens_back(p.dp)
         next(reduced)
+        for_each(lambda u: next(lines[u]))
 
         def up_grad(n, carry):
             at = pl.ds(pl.multiple_of(n * 4 * rows, 4 * rows), 4 * rows)
@@ -1203,10 +1242,10 @@
             ggu[n] = value.astype(BF16).reshape(4, rows, ff2)
             return carry
 
-        lax.fori_loop(0, 4, up_grad, 0)
+        lax.fori_loop(0, 8, up_grad, 0)
+        stage.put(5)
+        for_each(lambda u: next(lines[u]))
         next(reduced)
-        lax.fori_loop(4, 8, up_grad, 0)
-        for_each(lambda u: next(lines[u]))
 
         def out_part(n, carry):
             at = pl.ds(pl.multiple_of(n * 512, 512), 512)
@@ -1215,8 +1254,10 @@
             return carry
 
         lax.fori_loop(0, width // 512, out_part, 0)
+        stage.put(4)
         for _ in reduced:
             pass
+        stage.need(4, 5, 6)
 
         def back(i, carry):
             at = pl.ds(pl.multiple_of(i * 16, 16), 16)
@@ -1240,40 +1281,34 @@
         common.finish()
         assert len(names) <= N_SEMS
 
-    vmem = pl.BlockSpec(memory_space=VMEM)
-    return pl.pallas_call(
+    return staged_call(
         kernel,
-        out_shape=[
-            jax.ShapeDtypeStruct((tokens, width), F32),
-            jax.ShapeDtypeStruct((tokens, width), BF16),
-            jax.ShapeDtypeStruct((1, width), F32),
-            jax.ShapeDtypeStruct((out_rows, width), F32),
-            jax.ShapeDtypeStruct((8, tokens, width), BF16),
-            jax.ShapeDtypeStruct((8, 4, rows, ff2), BF16),
+        "feed_forward",
+        [(array, True) for array in (scaled, top, w_gu, w_dn, residual, cot, gains)],
+        [
+            ((tokens, width), F32, True),
+            ((tokens, width), BF16, True),
+            ((1, width), F32, True),
+            ((out_rows, width), F32, True),
+            ((8, tokens, width), BF16, True),
+            ((8, 4, rows, ff2), BF16, True),
         ],
-        in_specs=[vmem] * 7,
-        out_specs=[vmem] * 6,
-        scratch_shapes=[
-            pltpu.VMEM((4 * out_rows, width), BF16),
-            pltpu.VMEM((2 * block, ff), BF16),
-            pltpu.VMEM((2 * block, ff2), BF16),
-            pltpu.VMEM((8, tokens, width), BF16),
-            pltpu.VMEM((4, out_rows, width), BF16),
-            pltpu.VMEM((tokens, width), F32),
-            pltpu.VMEM((4, tokens, width), BF16),
-            pltpu.VMEM((4, tokens, width), BF16),
-            pltpu.VMEM((2, tokens, width), BF16),
-            pltpu.VMEM((tokens, width), BF16),
-            pltpu.VMEM((4, out_rows, width), BF16),
-            pltpu.VMEM((4, out_rows, width), BF16),
-            pltpu.SemaphoreType.DMA((N_SEMS,)),
-            pltpu.SemaphoreType.DMA((N_SEMS,)),
+        [
+            ((4 * out_rows, width), BF16),
+            ((2 * block, ff), BF16),
+            ((2 * block, ff2), BF16),
+            ((8, tokens, width), BF16),
+            ((4, out_rows, width), BF16),
+            ((tokens, width), F32),
+            ((4, tokens, width), BF16),
+            ((4, tokens, width), BF16),
+            ((2, tokens, width), BF16),
+            ((tokens, width), BF16),
+            ((4, out_rows, width), BF16),
+            ((4, out_rows, width), BF16),
         ],
-        name="feed_forward",
-        compiler_params=pltpu.CompilerParams(
-            collective_id=3, has_side_effects=True, vmem_limit_bytes=62 << 20
-        ),
-    )(scaled, top, w_gu, w_dn, residual, cot, gains)
+        3,
+    )
 
 
 def attention_back(
@@ -1288,14 +1323,15 @@
     at_v, at_s = 2 * key, 2 * key + val
 
     def kernel(
-        own_ref, lo_ref, g_ref, wo_ref, ga_ref, hn_ref, hi_ref, sw_ref, q_ref, k_ref, v_ref, w_ref, mask_ref, st_ref,
+        stage, own_ref, lo_ref, g_ref, wo_ref, ga_ref, hn_ref, hi_ref, sw_ref, q_ref, k_ref, v_ref, w_ref, mask_ref, st_ref,
         reach_ref, tail_ref, cum_ref, cat_ref, total, gout, gsum,
-        gy, gr, gs, gq, gk, gv, gst, gsts, sib, sums, got, got2, right, left, send, recv,
+        gy, gr, gs, gq, gk, gv, gst, gsts, sib, chip, got, got2, right, left, send, recv,
     ):
         uly = lax.axis_index(ULY)
         names = {}
         place = Place(uly)
         greet(line_partners(place) + plane_partners(place)[1:])
+        stage.need(0, 1, 2)
         common = Mover(place, names, send, recv)
         movers = [Mover(Place(u), names, send, recv, lambda: right.at[0, 0]) for u in range(4)]
         ways = [
@@ -1317,22 +1353,27 @@
                 pl.when(uly == u)(functools.partial(body, u))
 
         def first(u):
-            def slot_zero():
+            def sums():
+                yield
                 next(ways[u])
                 yield
+                yield
+                next(ways[u])
 
             m = Mover(Place(u), names, send, recv)
             together(
                 [
-                    plane_reduce(m, "s", lo_ref, total, sib, sums, got, got2),
+                    plane_reduce(m, "s", lo_ref, total, sib, chip, got, got2),
+                    sums(),
                     line_gather(m, "k", own_ref, gy),
-                    slot_zero(),
                 ]
             )
             m.finish()
-            next(ways[u])
 
         for_each(first)
+
+        stage.put(1)
+        stage.need(*range(3, 17))
 
         def chunk(c):
             return pl.ds(pl.multiple_of(c * half, half), half)
@@ -1366,6 +1407,7 @@
             common, "t", gst, gsts, state_slot, (pl.ds(0, 1), pl.ds(1, 1)), pair=False
         )
         next(states)
+        for_each(lambda u: next(ways[u]))
 
         for s in range(2):
             at = pl.ds(s * block, block)
@@ -1385,9 +1427,9 @@
             return carry
 
         lax.fori_loop(0, width // 512, out_grad, 0)
+        stage.put(2)
         for _ in states:
             pass
-        for_each(lambda u: next(ways[u]))
         for s in range(2):
             at = pl.ds(s * block, block)
             factors = block_factors(cum_ref, place.ctx, s, True)
@@ -1411,40 +1453,35 @@
         common.finish()
         assert len(names) <= N_SEMS
 
-    vmem = pl.BlockSpec(memory_space=VMEM)
-    return pl.pallas_call(
+    arrays = (own, lo, ggu, w_out, gated, normed, inverse, swish, q, k, v, weights, mask, state_in, reach, tail, cum)
+    return staged_call(
         kernel,
-        out_shape=[
-            jax.ShapeDtypeStruct((both, 2 * key + 2 * val), BF16),
-            jax.ShapeDtypeStruct((tokens, width), F32),
-            jax.ShapeDtypeStruct((4, piece, width), BF16),
-            jax.ShapeDtypeStruct((2, 4, rows, cols), BF16),
+        "attention_back",
+        [(array, True) for array in arrays],
+        [
+            ((both, 2 * key + 2 * val), BF16, True),
+            ((tokens, width), F32, True),
+            ((4, piece, width), BF16, True),
+            ((2, 4, rows, cols), BF16, True),
         ],
-        in_specs=[vmem] * 17,
-        out_specs=[vmem] * 4,
-        scratch_shapes=[
-            pltpu.VMEM((8, tokens, width), BF16),
-            pltpu.VMEM((both, val), BF16),
-            pltpu.VMEM((both, block), BF16),
-            pltpu.VMEM((both, key), F32),
-            pltpu.VMEM((both, key), F32),
-            pltpu.VMEM((both, val), F32),
-            pltpu.VMEM((2, key, val), BF16),
-            pltpu.VMEM((4, 2, key, val), BF16),
-            pltpu.VMEM((4, tokens, width), BF16),
-            pltpu.VMEM((4, tokens, width), BF16),
-            pltpu.VMEM((2, tokens, width), BF16),
-            pltpu.VMEM((tokens, width), BF16),
-            pltpu.VMEM((4, 2, 4, rows, cols), BF16),
-            pltpu.VMEM((4, 2, 4, rows, cols), BF16),
-            pltpu.SemaphoreType.DMA((N_SEMS,)),
-            pltpu.SemaphoreType.DMA((N_SEMS,)),
+        [
+            ((8, tokens, width), BF16),
+            ((both, val), BF16),
+            ((both, block), BF16),
+            ((both, key), F32),
+            ((both, key), F32),
+            ((both, val), F32),
+            ((2, key, val), BF16),
+            ((4, 2, key, val), BF16),
+            ((4, tokens, width), BF16),
+            ((4, tokens, width), BF16),
+            ((2, tokens, width), BF16),
+            ((tokens, width), BF16),
+            ((4, 2, 4, rows, cols), BF16),
+            ((4, 2, 4, rows, cols), BF16),
         ],
-        name="attention_back",
-        compiler_params=pltpu.CompilerParams(
-            collective_id=7, has_side_effects=True, vmem_limit_bytes=62 << 20
-        ),
-    )(own, lo, ggu, w_out, gated, normed, inverse, swish, q, k, v, weights, mask, state_in, reach, tail, cum)
+        7,
+    )
 
 
 def last_exchange(grad_cat, w_all, scaled, gout, gffn, inputs, term):
@@ -1644,13 +1681,14 @@
         ]
 
     def kernel(
-        cat_ref, wa_ref, s1_ref, o_ref, f_ref, in_ref, t_ref, out, gall, oall, fall, gains,
+        stage, cat_ref, wa_ref, s1_ref, o_ref, f_ref, in_ref, t_ref, out, gall, oall, fall, gains,
         grads, part, sib, right, left, gotx, goty, gotx2, goty2, oxs, oys, ox2, oy2, away, send, recv,
     ):
         uly = lax.axis_index(ULY)
         names = {}
         p = Place(uly)
         greet(everyone(p))
+        stage.need(0, 2)
         common = Mover(p, names, send, recv)
 
         def for_each(body):
@@ -1684,6 +1722,7 @@
 
         to_x(1, p.dg)
         to_y(1, p.dg)
+        stage.need(1)
         lax.fori_loop(0, 8, token_grad, 0)
         movers = [
             Mover(
@@ -1701,6 +1740,7 @@
         weight_grad(1, p.xn)
         weight_grad(0, p.ctx)
         weight_grad(1, p.ctx)
+        stage.need(3, 5, 6)
 
         def rest(u):
             m = Mover(Place(u), names, send, recv)
@@ -1717,35 +1757,30 @@
         common.finish()
         assert len(names) <= N_SEMS
 
-    vmem, hbm = pl.BlockSpec(memory_space=VMEM), pl.BlockSpec(memory_space=HBM)
-    return pl.pallas_call(
+    arrays = (grad_cat, w_all, scaled, gout, gffn, inputs, term)
+    return staged_call(
         kernel,
-        out_shape=[
-            jax.ShapeDtypeStruct((tokens, width), F32),
-            jax.ShapeDtypeStruct((8, rows, cols), BF16),
-            jax.ShapeDtypeStruct((4, out_rows, quarter), BF16),
-            jax.ShapeDtypeStruct((8, rows, ff2), BF16),
-            jax.ShapeDtypeStruct((8, width), F32),
+        "last",
+        [(array, i != 4) for i, array in enumerate(arrays)],
+        [
+            ((tokens, width), F32, True),
+            ((8, rows, cols), BF16, False),
+            ((4, out_rows, quarter), BF16, False),
+            ((8, rows, ff2), BF16, False),
+            ((8, width), F32, True),
         ],
-        in_specs=[vmem, vmem, vmem, vmem, hbm, vmem, vmem],
-        out_specs=[vmem, hbm, hbm, hbm, vmem],
-        scratch_shapes=[
-            pltpu.VMEM((2, 4, 4 * rows, cols), BF16),
-            pltpu.VMEM((8, tokens, width), BF16),
-            *[pltpu.VMEM((4, tokens, width), BF16)] * 3,
-            *[pltpu.VMEM((2, 4, rows, cols), BF16)] * 2,
-            *[pltpu.VMEM((4, rows, cols), BF16)] * 2,
-            *[pltpu.VMEM((2, 2, out_rows, quarter), BF16)] * 2,
-            *[pltpu.VMEM((2, out_rows, quarter), BF16)] * 2,
-            pltpu.VMEM((7, 8, width), F32),
-            pltpu.SemaphoreType.DMA((N_SEMS,)),
-            pltpu.SemaphoreType.DMA((N_SEMS,)),
+        [
+            ((2, 4, 4 * rows, cols), BF16),
+            ((8, tokens, width), BF16),
+            *[((4, tokens, width), BF16)] * 3,
+            *[((2, 4, rows, cols), BF16)] * 2,
+            *[((4, rows, cols), BF16)] * 2,
+            *[((2, 2, out_rows, quarter), BF16)] * 2,
+            *[((2, out_rows, quarter), BF16)] * 2,
+            ((7, 8, width), F32),
         ],
-        name="last",
-        compiler_params=pltpu.CompilerParams(
-            collective_id=2, has_side_effects=True, vmem_limit_bytes=62 << 20
-        ),
-    )(grad_cat, w_all, scaled, gout, gffn, inputs, term)
+        2,
+    )
 
 
 def local(

time: 524 us -> 479 us (0.914); the launches traced: 515 us -> 476 us
  Pallas kernels: 494 us -> 466 us
  local copies, waits for them, and re-layouts: 16.5 us -> 3.78 us
    pallas_call x6, Pallas kernels: 494 us -> 466 us  [staged_call(): pl.pallas_call(body, out_shape=[jax.ShapeDtypeStruct(shape, kind) for sha...]
    unnamed x39 -> x7, local copies, waits for them, and re-layouts: 14.3 us -> 0.94 us
where the time goes in v5:
time: 479 us; the launch traced here: 476 us
  Pallas kernels  466 us (97%)
  other arithmetic  4.82 us (1%)
    pallas_call x6, Pallas kernels, staged_call(): pl.pallas_call(body, out_shape=[jax.ShapeDtypeStruct(shape, kind) for sha...  466 us

profile of v5, /device:TPU:9, one launch (start us, length us, event | category | flops | bytes accessed | tf_op | source)
XLA Modules:
  0.0 475.6 jit_solution(484409136149139231)
XLA Ops:
  0.6 0.7 pad_maximum_fusion
  1.3 0.1 copy.27
  1.4 0.6 pad.4.refs_7_
  2.1 4.0 pack.1
  6.1 213.0 %forward.1 = (bf16[2048,1408]{1,0:T(8,128)(2,1)}, bf16[8,128,2048]{2,1,0:T(8,128)(2,1)}, bf16[432,2048]{1,0:T(8,128)(2,1)}, bf16[2,512,256]{2,1,0:T(8,128)(2,1)}...) custom-call(bf16[128,2048]{1,0:T(8,128)(2,1)} %bitcast.19, ...), custom_call_target="tpu_custom_call" | custom-call | tf_op jit(solution)/shard_map/forward/pallas_call | solution.py:607
  219.1 50.7 %feed_forward.1 = (f32[128,2048]{1,0:T(8,128)}, bf16[128,2048]{1,0:T(8,128)(2,1)}, f32[1,2048]{1,0:T(1,128)}, f32[108,2048]{1,0:T(8,128)}, bf16[8,128,2048]{2,1,...) custom-call(bf16[8,128,2048]{2,1,0:T(8,128)(2,1)} %get-tuple-element.63.refs_0_, ...), custom_call_target="tpu_custom_call" | custom-call | tf_op jit(solution)/shard_map/feed_forward/pallas_call | solution.py:607
  269.8 81.9 %attention_back.1 = (bf16[1024,1376]{1,0:T(8,128)(2,1)}, f32[128,2048]{1,0:T(8,128)}, bf16[4,108,2048]{2,1,0:T(8,128)(2,1)}, bf16[2,4,64,864]{3,2,1,0:T(8,128)(2,1)}) custom-call(bf16[128,2048]{1,0:T(8,128)(2,1)} %get-tuple-element.68.refs_0_, bf16[8,128,2048]{2,1,0:T(8,128)(2,1)} %get-tuple-element.69.refs_1_, bf16[2,4,4,64,864]{4,3,2,1,0:T(8,128)(2,1)} %bitcast.21, ...), custom_call_target="tpu_custom_call" | custom-call | tf_op jit(solution)/shard_map/attention_back/pallas_call | solution.py:607
  351.7 111.2 %last.1 = (f32[128,2048]{1,0:T(8,128)}, bf16[8,64,1376]{2,1,0:T(8,128)(2,1)}, bf16[4,108,512]{2,1,0:T(8,128)(2,1)}, bf16[8,64,864]{2,1,0:T(8,128)(2,1)}, f32[8,2048]{1,0:T(8,128)}) custom-call(bf16[1024,1376]{1,0:T(8,128)(2,1)} %get-tuple-element.87.refs_0_, bf16[2048,1408]{1,0:T(8,128)(2,1)} %get-tuple-element.88.refs_1_, ...), custom_call_target="tpu_custom_call" | custom-call | tf_op jit(solution)/shard_map/last/pallas_call | solution.py:607
  463.0 0.0 copy-start
  463.0 0.0 copy-start.1
  463.0 4.9 %unpack.1 = (f32[64,2048]{1,0:T(8,128)}, f32[64,2048]{1,0:T(8,128)}, f32[64,3456]{1,0:T(8,128)}, f32[64,3456]{1,0:T(8,128)}, f32[108,2048]{1,0:T(8,128)}, /*index=5*/f32[64,3456]{1,0:T(8,128)}, f32[64,3456]{1,0:T(8,128)}) custom-call(bf16[8,64,1376]{2,1,0:T(8,128)(2,1)} %get-tuple-element.94.refs_0_, bf16[4,108,512]{2,1,0:T(8,128)(2,1)} %get-tuple-element.95.refs_1_, ...), custom_call_target="tpu_custom_call" | custom-call | tf_op jit(solution)/shard_map/unpack/pallas_call | solution.py:607
  467.9 0.8 slice.9
  468.8 0.0 copy-done
  468.8 0.2 fusion.7
  469.0 0.0 copy-done.1
  469.0 0.3 fusion.2
  469.3 0.0 copy-start.2
  469.3 3.6 fusion.6
  472.9 0.7 constant_dynamic-slice_fusion
  473.7 0.5 slice_bitcast_fusion
  474.2 0.0 copy-done.2
  474.2 0.9 copy.29
  (2 shorter events, 0.0 us)
Async XLA Ops:
  463.0 5.8 %copy-start = (bf16[1,128,2048]{2,1,0:T(8,128)(2,1)S(1)}, bf16[1,128,2048]{2,1,0:T(8,128)(2,1)}, u32[]{:S(2)}) copy-start(bf16[1,128,2048]{2,1,0:T(8,128)(2,1)} %param.13) | copy-start | bytes 1572868
  463.0 6.0 %copy-start.1 = (f32[128,2048]{1,0:T(8,128)S(1)}, f32[128,2048]{1,0:T(8,128)}, u32[]{:S(2)}) copy-start(f32[128,2048]{1,0:T(8,128)} %get-tuple-element.93) | copy-start | bytes 3145732
  469.3 4.9 %copy-start.2 = (f32[108,2048]{1,0:T(8,128)S(1)}, f32[108,2048]{1,0:T(8,128)}, u32[]{:S(2)}) copy-start(f32[108,2048]{1,0:T(8,128)} %get-tuple-element.131) | copy-start | bytes 2654212

commit v6 on v5

--- a/solution.py
+++ b/solution.py
@@ -355,10 +355,12 @@
             copy.wait_send()
 
 
-def greet(devices):
+def greet(devices, meanwhile=None):
     barrier = pltpu.get_barrier_semaphore()
     for device in devices:
         pl.semaphore_signal(barrier, inc=1, device_id=device, device_id_type=MESH)
+    if meanwhile is not None:
+        meanwhile()
     pl.semaphore_wait(barrier, len(devices))
 
 
@@ -562,10 +564,10 @@
 
 
 class Stage:
-    def __init__(self, loads, stores):
+    def __init__(self, loads, stores, first):
         self.loads, self.stores, self.started = loads, stores, []
-        for copy in loads.values():
-            copy.start()
+        for i in (*first, *(i for i in loads if i not in first)):
+            loads[i].start()
 
     def need(self, *which):
         for i in which:
@@ -584,7 +586,7 @@
             copy.wait()
 
 
-def staged_call(kernel, name, ins, outs, scratch, remote=None):
+def staged_call(kernel, name, ins, outs, scratch, remote=None, first=()):
     in_held = [i for i, (_, held) in enumerate(ins) if held]
     out_held = [i for i, (_, _, held) in enumerate(outs) if held]
 
@@ -599,7 +601,7 @@
         for j, i in enumerate(out_held, len(in_held)):
             stores[i] = pltpu.make_async_copy(held[j], results[i], sems.at[j])
             results[i] = held[j]
-        stage = Stage(loads, stores)
+        stage = Stage(loads, stores, first)
         kernel(stage, *given, *results, *own)
         stage.end()
 
@@ -652,46 +654,33 @@
     return view if part is None else view.at[part]
 
 
-def pack(w_query, w_key, w_value, w_swish, w_output, w_gate, w_up, gains):
-    rows, (out_rows, width) = w_query.shape[0], w_output.shape
-    key, val, ff, quarter = KEY_DIM, VALUE_DIM, w_gate.shape[1] // 8, width // 4
-    cols = 2 * key + 2 * val + 32
-
-    def kernel(stage, q, k, v, s, o, g, u, n, packed, outw, gu):
-        stage.need(*range(8))
-        for d in range(2):
-            for z in range(4):
-                h, i = 2 * z + d, 4 * d + z
-                at = 0
-                for ref, w in ((q, key), (k, key), (v, val), (s, val)):
-                    packed[i, :, at : at + w] = ref[:, h * w : (h + 1) * w]
-                    at += w
-                packed[i, :, at : at + 32] = n[...]
-        for i in range(8):
-            gu[i, :, :ff] = g[:, i * ff : (i + 1) * ff]
-            gu[i, :, ff:] = u[:, i * ff : (i + 1) * ff]
-        for j in range(4):
-            outw[j] = o[:, j * quarter : (j + 1) * quarter]
-
-    weights = (w_query, w_key, w_value, w_swish, w_output, w_gate, w_up, gains)
-    return staged_call(
-        kernel,
-        "pack",
-        [(w, True) for w in weights],
-        [
-            ((8, rows, cols), BF16, True),
-            ((4, out_rows, quarter), BF16, True),
-            ((8, rows, 2 * ff), BF16, True),
-        ],
-        [],
-    )
-
-
-def unpack(heads, outg, slices):
+def finish(heads, outg, slices, residual, layer_part, grad, grad_scaled, hidden, gains, terms, down):
     rows, (_, out_rows, quarter) = heads.shape[1], outg.shape
+    tokens, width = hidden.shape
     key, val, ff = KEY_DIM, VALUE_DIM, slices.shape[2] // 2
 
-    def kernel(stage, hs, og, sl, q, k, v, s, o, g, u):
+    def kernel(
+        stage, hs, og, sl, res, part, gr, gs, hid, gain, term, down_in, q, k, v, s, o, g, u, y, x, down_out, n1, n2
+    ):
+        stage.need(3, 4, 5, 6, 7, 8, 9)
+        me = lax.axis_index(DP) * 16 + lax.axis_index(CTX) * 4 + lax.axis_index(ULY)
+        pair = pl.ds(pl.multiple_of(lax.div(me, 2) * 2 * rows, 2 * rows), 2 * rows)
+        own = jnp.where(lax.rem(me, 2) == 0, term[:, pair][:, :rows], term[:, pair][:, rows:])
+        n1[...] = own[0:1]
+        n2[...] = own[1:2]
+
+        def body(i, carry):
+            at = pl.ds(pl.multiple_of(i * 16, 16), 16)
+            y[at, :] = res[at, :] + part[at, :]
+            normed, inverse = normalize(hid[at, :].astype(F32))
+            x[at, :] = gr[at, :] + norm_back(gs[at, :] * gain[0:1, :], normed, inverse)
+            return carry
+
+        lax.fori_loop(0, tokens // 16, body, 0)
+        stage.put(7, 8)
+        stage.need(10)
+        down_out[...] = down_in[...]
+        stage.put(9)
         stage.need(0, 1, 2)
         for d in range(2):
             for z in range(4):
@@ -700,19 +689,23 @@
                 for ref, w in ((q, key), (k, key), (v, val), (s, val)):
                     ref[:, h * w : (h + 1) * w] = hs[i, :, at : at + w].astype(F32)
                     at += w
+        stage.put(0, 1, 2, 3)
         for i in range(8):
             g[:, i * ff : (i + 1) * ff] = sl[i, :, :ff].astype(F32)
             u[:, i * ff : (i + 1) * ff] = sl[i, :, ff:].astype(F32)
+        stage.put(5, 6)
         for j in range(4):
             o[:, j * quarter : (j + 1) * quarter] = og[j].astype(F32)
 
     widths = (8 * key, 8 * key, 8 * val, 8 * val, 4 * quarter, 8 * ff, 8 * ff)
     heights = (rows, rows, rows, rows, out_rows, rows, rows)
+    arrays = (heads, outg, slices, residual, layer_part, grad, grad_scaled, hidden, gains, terms, down)
+    shapes = [*zip(heights, widths), (tokens, width), (tokens, width), down.shape, (1, rows), (1, rows)]
     return staged_call(
         kernel,
-        "unpack",
-        [(heads, True), (outg, True), (slices, True)],
-        [(shape, F32, True) for shape in zip(heights, widths)],
+        "finish",
+        [(array, True) for array in arrays],
+        [(shape, F32, True) for shape in shapes],
         [],
     )
 
@@ -749,12 +742,13 @@
     return found
 
 
-def forward(hidden, cot, decay, packed, outw, gu, w_down):
+def forward(hidden, cot, decay, w_down, w_query, w_key, w_value, w_swish, w_output, w_gate, w_up, gains):
     tokens, width = hidden.shape
-    rows, cols = packed.shape[1:]
-    out_rows, quarter = outw.shape[1:]
-    ff2 = gu.shape[2]
     key, val = KEY_DIM, VALUE_DIM
+    rows, cols = w_query.shape[0], 2 * key + 2 * val + gains.shape[1]
+    out_rows, quarter = w_output.shape[0], width // 4
+    ff = w_gate.shape[1] // 8
+    ff2 = 2 * ff
     block, both = 4 * tokens, 8 * tokens
     half = block // 2
     scale = 1.0 / math.sqrt(key)
@@ -903,15 +897,32 @@
         m.arrive("o1", quarter_of(oall, pl.ds(2, 2), p.dg))
 
     def kernel(
-        stage, hid_ref, cot_ref, dec_ref, pk_ref, ow_ref, gu_ref, wd_ref,
+        stage, hid_ref, cot_ref, dec_ref, wd_ref, wq_ref, wk_ref, wv_ref, ws_ref, wo_ref, wg_ref, wu_ref, n_ref,
         w_all, s1_all, w2d, q_ref, k_ref, v_ref, sw_ref, w_ref, mask_ref, st_ref, reach_ref, tail_ref, cum_ref,
         gain_ref, hn_ref, hi_ref, ga_ref, res_ref, s2_all, top_all, gu_all, wd_all,
-        wall, s1, oall, dall, gall, dec8, cols8, upd, upds, ret, part, sib, right, left, s2, send, recv,
+        pk_ref, ow_ref, gu_ref, wall, s1, oall, dall, gall, dec8, cols8, upd, upds, ret, part, sib, right, left, s2, send, recv,
     ):
         uly = lax.axis_index(ULY)
         names = {}
         place = Place(uly)
-        greet(everyone(place))
+
+        def pack():
+            stage.need(*range(4, 12))
+            for d in range(2):
+                for z in range(4):
+                    h, i = 2 * z + d, 4 * d + z
+                    at = 0
+                    for ref, w in ((wq_ref, key), (wk_ref, key), (wv_ref, val), (ws_ref, val)):
+                        pk_ref[i, :, at : at + w] = ref[:, h * w : (h + 1) * w]
+                        at += w
+                    pk_ref[i, :, at:] = n_ref[...]
+            for i in range(8):
+                gu_ref[i, :, :ff] = wg_ref[:, i * ff : (i + 1) * ff]
+                gu_ref[i, :, ff:] = wu_ref[:, i * ff : (i + 1) * ff]
+            for j in range(4):
+                ow_ref[j] = wo_ref[:, j * quarter : (j + 1) * quarter]
+
+        greet(everyone(place), pack)
         stage.need(0)
         common = Mover(place, names, send, recv)
         ctx = place.ctx
@@ -996,7 +1007,6 @@
             v_ref[s] = rest[:, :val].astype(BF16)
             sw_ref[pl.ds(s * block, block), :] = rest[:, val : 2 * val]
         out_relay(common, oall)
-        for_each(spread_on)
         for s in range(2):
             k_tail = (k_ref[s].astype(F32) * tail_ref[s]).astype(BF16)
             upd[s] = dot_t(k_tail, v_ref[s]).astype(BF16)
@@ -1022,6 +1032,7 @@
             return carry
 
         lax.fori_loop(0, 2, intra, 0)
+        for_each(spread_on)
         next(states)
         lax.fori_loop(2, 4, intra, 0)
         out_end(common, oall)
@@ -1109,7 +1120,8 @@
         kernel,
         "forward",
         [
-            (hidden, True), (cot, False), (decay, False), (packed, False), (outw, False), (gu, False), (w_down, False)
+            (hidden, True), (cot, False), (decay, False), (w_down, False), (w_query, True), (w_key, True),
+            (w_value, True), (w_swish, True), (w_output, True), (w_gate, True), (w_up, True), (gains, True),
         ],
         [
             ((width, cols), BF16, False),
@@ -1136,6 +1148,9 @@
             ((4, out_rows, width), BF16, False),
         ],
         [
+            ((8, rows, cols), BF16),
+            ((4, out_rows, quarter), BF16),
+            ((8, rows, ff2), BF16),
             ((width, cols), BF16),
             ((8, tokens, width), BF16),
             ((4, out_rows, width), BF16),
@@ -1185,9 +1200,7 @@
             for u in range(4):
                 pl.when(uly == u)(functools.partial(body, u))
 
-        stage.need(0, 1, 2, 3)
-        for i in range(4):
-            w_d[i * out_rows : (i + 1) * out_rows, :] = wd_ref[i]
+        stage.need(0, 2)
 
         def weights():
             return gu_ref[...].reshape(32 * rows, ff2)
@@ -1197,6 +1210,10 @@
             lhs = s2_ref[pl.ds(4 * s, 4)].reshape(block, width)
             pre = matmul(lhs, weights())
             gate_pre, up_pre = pre[:, :ff], pre[:, ff:]
+            if 1 in stage.loads:
+                stage.need(1, 3)
+                for i in range(4):
+                    w_d[i * out_rows : (i + 1) * out_rows, :] = wd_ref[i]
             grad_product = dot_nt(top_ref[pl.ds(4 * s, 4)].reshape(block, width), w_d[...])
             sigma = jax.nn.sigmoid(gate_pre)
             act = gate_pre * sigma
@@ -1208,14 +1225,8 @@
         def tokens_back(s):
             here = pl.ds(pl.multiple_of(s * block, block), block)
 
-            def back(n, carry):
-                at = pl.ds(pl.multiple_of(n * 512, 512), 512)
-                right_side = gu_ref[pl.ds(2 * n, 2)].reshape(512, ff2)
-                value = dot_nt(grad_gu[here, :], right_side).astype(BF16)
-                part[pl.ds(4 * s, 4), :, at] = value.reshape(4, tokens, 512)
-                return carry
-
-            lax.fori_loop(0, width // 512, back, 0)
+            value = dot_nt(grad_gu[here, :], weights()).astype(BF16)
+            part[pl.ds(4 * s, 4)] = value.reshape(4, tokens, width)
 
         reduced = plane_reduce(common, "s", part, total, sib, sums, got, got2)
         tokens_of(p.other)
@@ -1308,6 +1319,7 @@
             ((4, out_rows, width), BF16),
         ],
         3,
+        (0, 2),
     )
 
 
@@ -1702,13 +1714,10 @@
             at = pl.ds(pl.multiple_of((dp * 4 + c) * 4 * rows, 4 * rows), 4 * rows)
             grads[dp, c] = dot_t(s1_ref[:, :, at].reshape(both, 4 * rows), cat_ref[...]).astype(BF16)
 
-        def token_grad(i, carry):
-            s = jnp.where(i < 4, p.other, p.dp)
-            n = pl.ds(pl.multiple_of(lax.rem(i, 4) * quarter, quarter), quarter)
+        def token_grad(s):
             rows_s = pl.ds(pl.multiple_of(s * block, block), block)
-            value = dot_nt(cat_ref[rows_s, :], wa_ref[n, :cols]).astype(BF16)
-            part[pl.ds(4 * s, 4), :, n] = value.reshape(4, tokens, quarter)
-            return carry
+            value = dot_nt(cat_ref[rows_s, :], wa_ref[:, :cols]).astype(BF16)
+            part[pl.ds(4 * s, 4)] = value.reshape(4, tokens, width)
 
         def to_x(i, c):
             weight_grad(0, c)
@@ -1723,7 +1732,8 @@
         to_x(1, p.dg)
         to_y(1, p.dg)
         stage.need(1)
-        lax.fori_loop(0, 8, token_grad, 0)
+        token_grad(p.other)
+        token_grad(p.dp)
         movers = [
             Mover(
                 Place(u), names, send, recv, lambda: halves_of_rows(sib.at[0], 0), lambda: sib.at[0]
@@ -1780,6 +1790,7 @@
             ((7, 8, width), F32),
         ],
         2,
+        (0, 2),
     )
 
 
@@ -1807,17 +1818,17 @@
     key, val, ff = KEY_DIM, VALUE_DIM, w_gate.shape[1] // 8
 
     gains = jnp.pad(jnp.stack([gain_attn, gain_ffn], axis=1), ((0, 0), (0, 30)))
-    packed, outw, gate_up = pack(w_query, w_key, w_value, w_swish, w_output, w_gate, w_up, gains)
     block = 4 * tokens
     (
         w_all, scaled_one, w_out, q, k, v, swish_pre, weights, mask, state_in, reach, tail, cum,
         gains, head_normed, head_inverse, gated, residual, scaled_two, top_all, w_gu, w_dn,
-    ) = forward(hidden_in[0], cotangent[0], log_decay[0], packed, outw, gate_up, w_down)
-    gain_one = gains[0]
+    ) = forward(
+        hidden_in[0], cotangent[0], log_decay[0], w_down,
+        w_query, w_key, w_value, w_swish, w_output, w_gate, w_up, gains,
+    )
     grad_residual, grad_y, gain_two_term, grad_down, layer_part, ggu = feed_forward(
         scaled_two, top_all, w_gu, w_dn, residual, cotangent[0], gains
     )
-    inputs = hidden_in[0].astype(f32)
     grad_cat, out_part, g_out, ggu = attention_back(
         grad_y,
         layer_part,
@@ -1837,7 +1848,6 @@
         tail,
         cum,
     )
-    layer_out = residual + out_part
     gs1, gcat, g_out, ggu, gain_terms = last_exchange(
         grad_cat,
         w_all,
@@ -1847,14 +1857,12 @@
         hidden_in[0],
         gain_two_term,
     )
-    normed_one, inverse_one = normalize(inputs)
-    grad_input = grad_residual + norm_back(gs1 * gain_one, normed_one, inverse_one)
-
-    grad_query, grad_key, grad_value, grad_swish, grad_output, grad_gate, grad_up = unpack(
-        gcat, g_out, ggu
-    )
-    me = dp * 16 + ctx * 4 + lax.axis_index(ULY)
-    gain_terms = lax.dynamic_slice_in_dim(gain_terms, me * rows, rows, axis=1)
+    (
+        grad_query, grad_key, grad_value, grad_swish, grad_output, grad_gate, grad_up,
+        layer_out, grad_input, grad_down, gain_one_term, gain_two_term,
+    ) = finish(
+        gcat, g_out, ggu, residual, out_part, grad_residual, gs1, hidden_in[0], gains, gain_terms, grad_down
+    )
     return (
         layer_out[None],
         grad_input[None],
@@ -1866,8 +1874,8 @@
         grad_gate,
         grad_up,
         grad_down,
-        gain_terms[0],
-        gain_terms[1],
+        gain_one_term[0],
+        gain_two_term[0],
     )
 
 

time: 479 us -> 459 us (0.958)
  Pallas kernels: 466 us -> 454 us
    pallas_call x6 -> x5, Pallas kernels: 466 us -> 454 us  [staged_call(): pl.pallas_call(body, out_shape=[jax.ShapeDtypeStruct(shape, kind) for sha...]
where the time goes in v6:
time: 459 us; the launch traced here: 456 us
  Pallas kernels  454 us (99%)
    pallas_call x5, Pallas kernels, staged_call(): pl.pallas_call(body, out_shape=[jax.ShapeDtypeStruct(shape, kind) for sha...  454 us

profile of v6, /device:TPU:9, one launch (start us, length us, event | category | flops | bytes accessed | tf_op | source)
XLA Modules:
  0.0 455.9 jit_solution(741449693372922588)
XLA Ops:
  0.6 0.7 pad_maximum_fusion
  1.3 0.1 copy.27
  1.4 0.6 pad.4.refs_11_
  2.1 205.0 %forward.1 = (bf16[2048,1408]{1,0:T(8,128)(2,1)}, bf16[8,128,2048]{2,1,0:T(8,128)(2,1)}, bf16[432,2048]{1,0:T(8,128)(2,1)}, bf16[2,512,256]{2,1,0:T(8,128)(2,1)}...) custom-call(bf16[128,2048]{1,0:T(8,128)(2,1)} %bitcast.11, ...), custom_call_target="tpu_custom_call" | custom-call | tf_op jit(solution)/shard_map/forward/pallas_call | solution.py:609
  207.0 50.1 %feed_forward.1 = (f32[128,2048]{1,0:T(8,128)}, bf16[128,2048]{1,0:T(8,128)(2,1)}, f32[1,2048]{1,0:T(1,128)}, f32[108,2048]{1,0:T(8,128)}, bf16[8,128,2048]{2,1,...) custom-call(bf16[8,128,2048]{2,1,0:T(8,128)(2,1)} %get-tuple-element.61.refs_0_, ...), custom_call_target="tpu_custom_call" | custom-call | tf_op jit(solution)/shard_map/feed_forward/pallas_call | solution.py:609
  257.1 80.3 %attention_back.1 = (bf16[1024,1376]{1,0:T(8,128)(2,1)}, f32[128,2048]{1,0:T(8,128)}, bf16[4,108,2048]{2,1,0:T(8,128)(2,1)}, bf16[2,4,64,864]{3,2,1,0:T(8,128)(2,1)}) custom-call(bf16[128,2048]{1,0:T(8,128)(2,1)} %get-tuple-element.67.refs_0_, bf16[8,128,2048]{2,1,0:T(8,128)(2,1)} %get-tuple-element.68.refs_1_, bf16[2,4,4,64,864]{4,3,2,1,0:T(8,128)(2,1)} %bitcast.14, ...), custom_call_target="tpu_custom_call" | custom-call | tf_op jit(solution)/shard_map/attention_back/pallas_call | solution.py:609
  337.4 109.8 %last.1 = (f32[128,2048]{1,0:T(8,128)}, bf16[8,64,1376]{2,1,0:T(8,128)(2,1)}, bf16[4,108,512]{2,1,0:T(8,128)(2,1)}, bf16[8,64,864]{2,1,0:T(8,128)(2,1)}, f32[8,2048]{1,0:T(8,128)}) custom-call(bf16[1024,1376]{1,0:T(8,128)(2,1)} %get-tuple-element.84.refs_0_, bf16[2048,1408]{1,0:T(8,128)(2,1)} %get-tuple-element.85.refs_1_, ...), custom_call_target="tpu_custom_call" | custom-call | tf_op jit(solution)/shard_map/last/pallas_call | solution.py:609
  447.2 8.4 %finish.1 = (f32[64,2048]{1,0:T(8,128)}, f32[64,2048]{1,0:T(8,128)}, f32[64,3456]{1,0:T(8,128)}, f32[64,3456]{1,0:T(8,128)}, f32[108,2048]{1,0:T(8,128)}, /*inde...) custom-call(bf16[8,64,1376]{2,1,0:T(8,128)(2,1)} %get-tuple-element., ...), custom_call_target="tpu_custom_call" | custom-call | tf_op jit(solution)/shard_map/finish/pallas_call | solution.py:609

commit v7 on v6

--- a/solution.py
+++ b/solution.py
@@ -1336,8 +1336,8 @@
 
     def kernel(
         stage, own_ref, lo_ref, g_ref, wo_ref, ga_ref, hn_ref, hi_ref, sw_ref, q_ref, k_ref, v_ref, w_ref, mask_ref, st_ref,
-        reach_ref, tail_ref, cum_ref, cat_ref, total, gout, gsum,
-        gy, gr, gs, gq, gk, gv, gst, gsts, sib, chip, got, got2, right, left, send, recv,
+        reach_ref, tail_ref, cum_ref, cat_ref, total, osum, gsum,
+        gout, oxs, oys, ox2, oy2, gy, gr, gs, gq, gk, gv, gst, gsts, sib, chip, got, got2, right, left, send, recv,
     ):
         uly = lax.axis_index(ULY)
         names = {}
@@ -1425,11 +1425,6 @@
             at = pl.ds(s * block, block)
             gq[at, :] = jnp.dot(gs[at, :], k_ref[s], preferred_element_type=F32)
             gk[at, :] = dot_t(gs[at, :], q_ref[s])
-        next(states)
-        for s in range(2):
-            at = pl.ds(s * block, block)
-            gv[at, :] = dot_t(w_ref[s], gr[at, :])
-
         def out_grad(n, carry):
             at = pl.ds(pl.multiple_of(n * 512, 512), 512)
             grad = gy[:, :, at].reshape(both, 512)
@@ -1439,7 +1434,19 @@
             return carry
 
         lax.fori_loop(0, width // 512, out_grad, 0)
-        stage.put(2)
+        next(states)
+
+        quarter = width // 4
+
+        def column(part, c):
+            return gout.at[part, :, pl.ds(pl.multiple_of(c * quarter, quarter), quarter)]
+
+        for i, (cx, cy) in ((1, (place.dg, place.dg)), (0, (place.xn, place.yn))):
+            common.send(("ox", i), column(pl.ds(0, 2), cx), oxs.at[i], place.at(ctx=place.xn))
+            common.send(("oy", i), column(pl.ds(2, 2), cy), oys.at[i], place.at(ctx=place.yn))
+        for s in range(2):
+            at = pl.ds(s * block, block)
+            gv[at, :] = dot_t(w_ref[s], gr[at, :])
         for _ in states:
             pass
         for s in range(2):
@@ -1455,6 +1462,14 @@
             cat_ref[at, at_v:at_s] = (
                 gv[at, :] + tail_ref[s] * jnp.dot(k_ref[s], update, preferred_element_type=F32)
             ).astype(BF16)
+        stage.put(0)
+        common.arrive(("ox", 1), oxs.at[1])
+        common.arrive(("oy", 1), oys.at[1])
+        for t in range(2):
+            add_up(oxs.at[1, t], [column(t, place.yn), oxs.at[1, t]])
+            add_up(oys.at[1, t], [column(2 + t, place.xn), oys.at[1, t]])
+        common.send("oy2", oxs.at[1], oy2, place.at(ctx=place.yn))
+        common.send("ox2", oys.at[1], ox2, place.at(ctx=place.xn))
 
         def last(u):
             for _ in ways[u]:
@@ -1462,6 +1477,11 @@
             movers[u].finish()
 
         for_each(last)
+        for name, ref in ((("ox", 0), oxs.at[0]), (("oy", 0), oys.at[0]), ("oy2", oy2), ("ox2", ox2)):
+            common.arrive(name, ref)
+        for us in range(4):
+            got, got2 = (oxs, oy2) if us < 2 else (oys, ox2)
+            add_up(osum.at[us], [column(us, place.ctx), got.at[0, us % 2], got2.at[us % 2]])
         common.finish()
         assert len(names) <= N_SEMS
 
@@ -1473,10 +1493,13 @@
         [
             ((both, 2 * key + 2 * val), BF16, True),
             ((tokens, width), F32, True),
-            ((4, piece, width), BF16, True),
+            ((4, piece, width // 4), BF16, True),
             ((2, 4, rows, cols), BF16, True),
         ],
         [
+            ((4, piece, width), BF16),
+            *[((2, 2, piece, width // 4), BF16)] * 2,
+            *[((2, piece, width // 4), BF16)] * 2,
             ((8, tokens, width), BF16),
             ((both, val), BF16),
             ((both, block), BF16),
@@ -1500,13 +1523,11 @@
     tokens, width = inputs.shape
     both, cols = grad_cat.shape
     block = both // 2
-    out_rows = gout.shape[1]
-    quarter = width // 4
+    out_rows, quarter = gout.shape[1:]
     rows, ff2 = gffn.shape[1:]
 
     def streams(
-        m, line, tile, o_ref, f_ref, in_ref, t_ref, out, gall, oall, fall, gains,
-        gotx, goty, gotx2, goty2, oxs, oys, ox2, oy2, away,
+        m, line, tile, f_ref, in_ref, t_ref, out, gall, fall, gains, gotx, goty, gotx2, goty2, away,
     ):
         p = m.place
         u = p.uly
@@ -1571,68 +1592,6 @@
                     m.arrive(("g", 0, us), gall.at[p.dp * 4 + us])
                     m.arrive(("g", 1, us), gall.at[p.other * 4 + us])
 
-        def out_proj():
-            def column(ref, part, c):
-                return ref.at[part, :, pl.ds(pl.multiple_of(c * quarter, quarter), quarter)]
-
-            low, high = pl.ds(0, 2), pl.ds(2, 2)
-            for i, (cx, cy) in ((1, (p.dg, p.dg)), (0, (p.xn, p.yn))):
-                m.send(("ox", i), column(o_ref, low, cx), oxs.at[i], p.at(ctx=p.xn))
-                m.send(("oy", i), column(o_ref, high, cy), oys.at[i], p.at(ctx=p.yn))
-            yield
-            m.arrive(("ox", 1), oxs.at[1])
-            for t in range(2):
-                add_up(oxs.at[1, t], [column(o_ref, t, p.yn), oxs.at[1, t]])
-            m.send("oy2", oxs.at[1], oy2, p.at(ctx=p.yn))
-            m.arrive(("oy", 1), oys.at[1])
-            for t in range(2):
-                add_up(oys.at[1, t], [column(o_ref, 2 + t, p.xn), oys.at[1, t]])
-            m.send("ox2", oys.at[1], ox2, p.at(ctx=p.xn))
-            yield
-            m.arrive(("ox", 0), oxs.at[0])
-            m.arrive(("oy", 0), oys.at[0])
-            m.arrive("oy2", oy2)
-            m.arrive("ox2", ox2)
-            home_dp, home_ctx = u // 2, 2 * (u % 2) + p.dp
-            here_all = []
-            for us in range(4):
-                got, got2 = (oxs, oy2) if us < 2 else (oys, ox2)
-                t = us % 2
-                add_up(got.at[0, t], [column(o_ref, us, p.ctx), got.at[0, t], got2.at[t]])
-                own = (home_dp == p.dp) & (home_ctx == p.ctx) & (us == u)
-                there = oall.at[p.ctx]
-                here = pltpu.make_async_copy(
-                    got.at[0, t], there, m.send_sems.at[m.number("O")]
-                )
-
-                @pl.when(own)
-                def _(here=here):
-                    here.start()
-                    here.wait()
-
-                for j in range(4):
-                    copy = pltpu.make_async_remote_copy(
-                        src_ref=got.at[0, t],
-                        dst_ref=there,
-                        send_sem=m.send_sems.at[m.number(("os", us))],
-                        recv_sem=m.recv_sems.at[m.number(("o", j))],
-                        device_id=(home_dp, home_ctx, us),
-                        device_id_type=MESH,
-                    )
-                    pl.when(jnp.logical_not(own) & (p.ctx == j))(copy.start)
-                here_all.append((own, copy))
-            yield
-            head_dp, head_u = lax.rem(p.ctx, 2), p.dp * 2 + lax.div(p.ctx, 2)
-            for j in range(4):
-                mine = (head_dp == p.dp) & (p.ctx == j) & (head_u == u)
-
-                @pl.when(jnp.logical_not(mine))
-                def _(j=j):
-                    m.arrive(("o", j), oall.at[j])
-
-            for own, copy in here_all:
-                pl.when(jnp.logical_not(own))(copy.wait_send)
-
         def feed():
             mine = fall.at[p.dp * 4 + p.ctx]
             copy = m.local("F", f_ref.at[p.dp * 4 + p.ctx], mine)
@@ -1688,13 +1647,12 @@
         return [
             attn(),
             tokens_stream(),
-            later(out_proj(), 1),
-            later(feed(), 5),
+            later(feed(), 3),
         ]
 
     def kernel(
         stage, cat_ref, wa_ref, s1_ref, o_ref, f_ref, in_ref, t_ref, out, gall, oall, fall, gains,
-        grads, part, sib, right, left, gotx, goty, gotx2, goty2, oxs, oys, ox2, oy2, away, send, recv,
+        grads, part, sib, right, left, gotx, goty, gotx2, goty2, away, send, recv,
     ):
         uly = lax.axis_index(ULY)
         names = {}
@@ -1729,6 +1687,56 @@
             for t in range(4):
                 common.send(("gy", i, t), tile(1, c, t), goty.at[i, t], p.at(ctx=p.yn))
 
+        def out_copies(m, senders):
+            at = m.place
+            home_dp, home_ctx = at.uly // 2, 2 * (at.uly % 2) + at.dp
+            found = []
+            for us in range(4):
+                own = (home_dp == at.dp) & (home_ctx == at.ctx) & (us == at.uly)
+                copies = [
+                    pltpu.make_async_remote_copy(
+                        src_ref=o_ref.at[us],
+                        dst_ref=oall.at[at.ctx],
+                        send_sem=m.send_sems.at[m.number(("os", us))],
+                        recv_sem=m.recv_sems.at[m.number(("o", j))],
+                        device_id=(home_dp, home_ctx, us),
+                        device_id_type=MESH,
+                    )
+                    for j in senders
+                ]
+                found.append((us, own, copies))
+            return found
+
+        def out_start(u):
+            m = Mover(Place(u), names, send, recv)
+            for us, own, copies in out_copies(m, range(4)):
+
+                @pl.when(own)
+                def _(us=us):
+                    here = pltpu.make_async_copy(
+                        o_ref.at[us], oall.at[p.ctx], send.at[m.number("O")]
+                    )
+                    here.start()
+                    here.wait()
+
+                for j, copy in enumerate(copies):
+                    pl.when(jnp.logical_not(own) & (p.ctx == j))(copy.start)
+
+        def out_end(u):
+            m = Mover(Place(u), names, send, recv)
+            head_dp, head_u = lax.rem(p.ctx, 2), p.dp * 2 + lax.div(p.ctx, 2)
+            for j in range(4):
+                mine = (head_dp == p.dp) & (p.ctx == j) & (head_u == u)
+
+                @pl.when(jnp.logical_not(mine))
+                def _(j=j):
+                    m.arrive(("o", j), oall.at[j])
+
+            for _, own, copies in out_copies(m, range(1)):
+                pl.when(jnp.logical_not(own))(copies[0].wait_send)
+
+        stage.need(3)
+        for_each(out_start)
         to_x(1, p.dg)
         to_y(1, p.dg)
         stage.need(1)
@@ -1750,18 +1758,19 @@
         weight_grad(1, p.xn)
         weight_grad(0, p.ctx)
         weight_grad(1, p.ctx)
-        stage.need(3, 5, 6)
+        stage.need(5, 6)
 
         def rest(u):
             m = Mover(Place(u), names, send, recv)
             together(
                 streams(
-                    m, lines[u], tile, o_ref, f_ref, in_ref, t_ref, out, gall, oall, fall, gains,
-                    gotx, goty, gotx2, goty2, oxs, oys, ox2, oy2, away,
+                    m, lines[u], tile, f_ref, in_ref, t_ref, out, gall, fall, gains,
+                    gotx, goty, gotx2, goty2, away,
                 )
             )
             m.finish()
             movers[u].finish()
+            out_end(u)
 
         for_each(rest)
         common.finish()
@@ -1785,12 +1794,10 @@
             *[((4, tokens, width), BF16)] * 3,
             *[((2, 4, rows, cols), BF16)] * 2,
             *[((4, rows, cols), BF16)] * 2,
-            *[((2, 2, out_rows, quarter), BF16)] * 2,
-            *[((2, out_rows, quarter), BF16)] * 2,
             ((7, 8, width), F32),
         ],
         2,
-        (0, 2),
+        (3, 0, 2),
     )
 
 

time: 459 us -> 451 us (0.983)
  Pallas kernels: 454 us -> 444 us
    pallas_call x5, Pallas kernels: 454 us -> 444 us  [staged_call(): pl.pallas_call(body, out_shape=[jax.ShapeDtypeStruct(shape, kind) for sha...]
where the time goes in v7:
time: 451 us; the launch traced here: 447 us
  Pallas kernels  444 us (98%)
    pallas_call x5, Pallas kernels, staged_call(): pl.pallas_call(body, out_shape=[jax.ShapeDtypeStruct(shape, kind) for sha...  444 us

profile of v7, /device:TPU:9, one launch (start us, length us, event | category | flops | bytes accessed | tf_op | source)
XLA Modules:
  0.0 446.7 jit_solution(1186520041595434208)
XLA Ops:
  0.6 0.7 pad_maximum_fusion
  1.3 0.1 copy.27
  1.4 0.6 pad.4.refs_11_
  2.1 205.0 %forward.1 = (bf16[2048,1408]{1,0:T(8,128)(2,1)}, bf16[8,128,2048]{2,1,0:T(8,128)(2,1)}, bf16[432,2048]{1,0:T(8,128)(2,1)}, bf16[2,512,256]{2,1,0:T(8,128)(2,1)}...) custom-call(bf16[128,2048]{1,0:T(8,128)(2,1)} %bitcast.11, ...), custom_call_target="tpu_custom_call" | custom-call | tf_op jit(solution)/shard_map/forward/pallas_call | solution.py:609
  207.0 50.1 %feed_forward.1 = (f32[128,2048]{1,0:T(8,128)}, bf16[128,2048]{1,0:T(8,128)(2,1)}, f32[1,2048]{1,0:T(1,128)}, f32[108,2048]{1,0:T(8,128)}, bf16[8,128,2048]{2,1,...) custom-call(bf16[8,128,2048]{2,1,0:T(8,128)(2,1)} %get-tuple-element.61.refs_0_, ...), custom_call_target="tpu_custom_call" | custom-call | tf_op jit(solution)/shard_map/feed_forward/pallas_call | solution.py:609
  257.1 85.8 %attention_back.1 = (bf16[1024,1376]{1,0:T(8,128)(2,1)}, f32[128,2048]{1,0:T(8,128)}, bf16[4,108,512]{2,1,0:T(8,128)(2,1)}, bf16[2,4,64,864]{3,2,1,0:T(8,128)(2,1)}) custom-call(bf16[128,2048]{1,0:T(8,128)(2,1)} %get-tuple-element.67.refs_0_, bf16[8,128,2048]{2,1,0:T(8,128)(2,1)} %get-tuple-element.68.refs_1_, bf16[2,4,4,64,864]{4,3,2,1,0:T(8,128)(2,1)} %bitcast.14, ...), custom_call_target="tpu_custom_call" | custom-call | tf_op jit(solution)/shard_map/attention_back/pallas_call | solution.py:609
  342.9 95.1 %last.1 = (f32[128,2048]{1,0:T(8,128)}, bf16[8,64,1376]{2,1,0:T(8,128)(2,1)}, bf16[4,108,512]{2,1,0:T(8,128)(2,1)}, bf16[8,64,864]{2,1,0:T(8,128)(2,1)}, f32[8,2048]{1,0:T(8,128)}) custom-call(bf16[1024,1376]{1,0:T(8,128)(2,1)} %get-tuple-element.84.refs_0_, bf16[2048,1408]{1,0:T(8,128)(2,1)} %get-tuple-element.85.refs_1_, ...), custom_call_target="tpu_custom_call" | custom-call | tf_op jit(solution)/shard_map/last/pallas_call | solution.py:609
  438.0 8.4 %finish.1 = (f32[64,2048]{1,0:T(8,128)}, f32[64,2048]{1,0:T(8,128)}, f32[64,3456]{1,0:T(8,128)}, f32[64,3456]{1,0:T(8,128)}, f32[108,2048]{1,0:T(8,128)}, /*inde...) custom-call(bf16[8,64,1376]{2,1,0:T(8,128)(2,1)} %get-tuple-element., ...), custom_call_target="tpu_custom_call" | custom-call | tf_op jit(solution)/shard_map/finish/pallas_call | solution.py:609

commit v8 on v7

--- a/solution.py
+++ b/solution.py
@@ -662,25 +662,6 @@
     def kernel(
         stage, hs, og, sl, res, part, gr, gs, hid, gain, term, down_in, q, k, v, s, o, g, u, y, x, down_out, n1, n2
     ):
-        stage.need(3, 4, 5, 6, 7, 8, 9)
-        me = lax.axis_index(DP) * 16 + lax.axis_index(CTX) * 4 + lax.axis_index(ULY)
-        pair = pl.ds(pl.multiple_of(lax.div(me, 2) * 2 * rows, 2 * rows), 2 * rows)
-        own = jnp.where(lax.rem(me, 2) == 0, term[:, pair][:, :rows], term[:, pair][:, rows:])
-        n1[...] = own[0:1]
-        n2[...] = own[1:2]
-
-        def body(i, carry):
-            at = pl.ds(pl.multiple_of(i * 16, 16), 16)
-            y[at, :] = res[at, :] + part[at, :]
-            normed, inverse = normalize(hid[at, :].astype(F32))
-            x[at, :] = gr[at, :] + norm_back(gs[at, :] * gain[0:1, :], normed, inverse)
-            return carry
-
-        lax.fori_loop(0, tokens // 16, body, 0)
-        stage.put(7, 8)
-        stage.need(10)
-        down_out[...] = down_in[...]
-        stage.put(9)
         stage.need(0, 1, 2)
         for d in range(2):
             for z in range(4):
@@ -696,6 +677,26 @@
         stage.put(5, 6)
         for j in range(4):
             o[:, j * quarter : (j + 1) * quarter] = og[j].astype(F32)
+        stage.put(4)
+        stage.need(3, 4, 5, 6, 7, 8, 9)
+        me = lax.axis_index(DP) * 16 + lax.axis_index(CTX) * 4 + lax.axis_index(ULY)
+        pair = pl.ds(pl.multiple_of(lax.div(me, 2) * 2 * rows, 2 * rows), 2 * rows)
+        own = jnp.where(lax.rem(me, 2) == 0, term[:, pair][:, :rows], term[:, pair][:, rows:])
+        n1[...] = own[0:1]
+        n2[...] = own[1:2]
+
+        def body(i, carry):
+            at = pl.ds(pl.multiple_of(i * 16, 16), 16)
+            y[at, :] = res[at, :] + part[at, :]
+            normed, inverse = normalize(hid[at, :].astype(F32))
+            x[at, :] = gr[at, :] + norm_back(gs[at, :] * gain[0:1, :], normed, inverse)
+            return carry
+
+        lax.fori_loop(0, tokens // 16, body, 0)
+        stage.put(7, 8)
+        stage.need(10)
+        down_out[...] = down_in[...]
+        stage.put(9)
 
     widths = (8 * key, 8 * key, 8 * val, 8 * val, 4 * quarter, 8 * ff, 8 * ff)
     heights = (rows, rows, rows, rows, out_rows, rows, rows)
@@ -707,6 +708,7 @@
         [(array, True) for array in arrays],
         [(shape, F32, True) for shape in shapes],
         [],
+        first=(0, 2, 1),
     )
 
 

time: 451 us -> 449 us (level)
  no operation moved by 1% of the time
where the time goes in v8:
time: 449 us; the launch traced here: 445 us
  Pallas kernels  443 us (99%)
    pallas_call x5, Pallas kernels, staged_call(): pl.pallas_call(body, out_shape=[jax.ShapeDtypeStruct(shape, kind) for sha...  443 us

profile of v8, /device:TPU:9, one launch (start us, length us, event | category | flops | bytes accessed | tf_op | source)
XLA Modules:
  0.0 444.9 jit_solution(12769900208756659064)
XLA Ops:
  0.6 0.7 pad_maximum_fusion
  1.3 0.1 copy.27
  1.4 0.6 pad.4.refs_11_
  2.1 205.0 %forward.1 = (bf16[2048,1408]{1,0:T(8,128)(2,1)}, bf16[8,128,2048]{2,1,0:T(8,128)(2,1)}, bf16[432,2048]{1,0:T(8,128)(2,1)}, bf16[2,512,256]{2,1,0:T(8,128)(2,1)}...) custom-call(bf16[128,2048]{1,0:T(8,128)(2,1)} %bitcast.11, ...), custom_call_target="tpu_custom_call" | custom-call | tf_op jit(solution)/shard_map/forward/pallas_call | solution.py:609
  207.0 50.1 %feed_forward.1 = (f32[128,2048]{1,0:T(8,128)}, bf16[128,2048]{1,0:T(8,128)(2,1)}, f32[1,2048]{1,0:T(1,128)}, f32[108,2048]{1,0:T(8,128)}, bf16[8,128,2048]{2,1,...) custom-call(bf16[8,128,2048]{2,1,0:T(8,128)(2,1)} %get-tuple-element.61.refs_0_, ...), custom_call_target="tpu_custom_call" | custom-call | tf_op jit(solution)/shard_map/feed_forward/pallas_call | solution.py:609
  257.1 85.8 %attention_back.1 = (bf16[1024,1376]{1,0:T(8,128)(2,1)}, f32[128,2048]{1,0:T(8,128)}, bf16[4,108,512]{2,1,0:T(8,128)(2,1)}, bf16[2,4,64,864]{3,2,1,0:T(8,128)(2,1)}) custom-call(bf16[128,2048]{1,0:T(8,128)(2,1)} %get-tuple-element.67.refs_0_, bf16[8,128,2048]{2,1,0:T(8,128)(2,1)} %get-tuple-element.68.refs_1_, bf16[2,4,4,64,864]{4,3,2,1,0:T(8,128)(2,1)} %bitcast.14, ...), custom_call_target="tpu_custom_call" | custom-call | tf_op jit(solution)/shard_map/attention_back/pallas_call | solution.py:609
  342.9 95.1 %last.1 = (f32[128,2048]{1,0:T(8,128)}, bf16[8,64,1376]{2,1,0:T(8,128)(2,1)}, bf16[4,108,512]{2,1,0:T(8,128)(2,1)}, bf16[8,64,864]{2,1,0:T(8,128)(2,1)}, f32[8,2048]{1,0:T(8,128)}) custom-call(bf16[1024,1376]{1,0:T(8,128)(2,1)} %get-tuple-element.84.refs_0_, bf16[2048,1408]{1,0:T(8,128)(2,1)} %get-tuple-element.85.refs_1_, ...), custom_call_target="tpu_custom_call" | custom-call | tf_op jit(solution)/shard_map/last/pallas_call | solution.py:609
  438.0 6.7 %finish.1 = (f32[64,2048]{1,0:T(8,128)}, f32[64,2048]{1,0:T(8,128)}, f32[64,3456]{1,0:T(8,128)}, f32[64,3456]{1,0:T(8,128)}, f32[108,2048]{1,0:T(8,128)}, /*inde...) custom-call(bf16[8,64,1376]{2,1,0:T(8,128)(2,1)} %get-tuple-element., ...), custom_call_target="tpu_custom_call" | custom-call | tf_op jit(solution)/shard_map/finish/pallas_call | solution.py:609

commit v9 on v8

--- a/solution.py
+++ b/solution.py
@@ -1478,12 +1478,13 @@
                 pass
             movers[u].finish()
 
-        for_each(last)
         for name, ref in ((("ox", 0), oxs.at[0]), (("oy", 0), oys.at[0]), ("oy2", oy2), ("ox2", ox2)):
             common.arrive(name, ref)
         for us in range(4):
             got, got2 = (oxs, oy2) if us < 2 else (oys, ox2)
             add_up(osum.at[us], [column(us, place.ctx), got.at[0, us % 2], got2.at[us % 2]])
+        stage.put(2)
+        for_each(last)
         common.finish()
         assert len(names) <= N_SEMS
 

time: 449 us -> 449 us (level)
  no operation moved by 1% of the time
where the time goes in v9:
time: 449 us; the launch traced here: 445 us
  Pallas kernels  443 us (99%)
    pallas_call x5, Pallas kernels, staged_call(): pl.pallas_call(body, out_shape=[jax.ShapeDtypeStruct(shape, kind) for sha...  443 us

profile of v9, /device:TPU:9, one launch (start us, length us, event | category | flops | bytes accessed | tf_op | source)
XLA Modules:
  0.0 445.0 jit_solution(9840102378241730952)
XLA Ops:
  0.6 0.7 pad_maximum_fusion
  1.3 0.1 copy.27
  1.4 0.6 pad.4.refs_11_
  2.1 205.0 %forward.1 = (bf16[2048,1408]{1,0:T(8,128)(2,1)}, bf16[8,128,2048]{2,1,0:T(8,128)(2,1)}, bf16[432,2048]{1,0:T(8,128)(2,1)}, bf16[2,512,256]{2,1,0:T(8,128)(2,1)}...) custom-call(bf16[128,2048]{1,0:T(8,128)(2,1)} %bitcast.11, ...), custom_call_target="tpu_custom_call" | custom-call | tf_op jit(solution)/shard_map/forward/pallas_call | solution.py:609
  207.0 50.1 %feed_forward.1 = (f32[128,2048]{1,0:T(8,128)}, bf16[128,2048]{1,0:T(8,128)(2,1)}, f32[1,2048]{1,0:T(1,128)}, f32[108,2048]{1,0:T(8,128)}, bf16[8,128,2048]{2,1,...) custom-call(bf16[8,128,2048]{2,1,0:T(8,128)(2,1)} %get-tuple-element.61.refs_0_, ...), custom_call_target="tpu_custom_call" | custom-call | tf_op jit(solution)/shard_map/feed_forward/pallas_call | solution.py:609
  257.1 86.0 %attention_back.1 = (bf16[1024,1376]{1,0:T(8,128)(2,1)}, f32[128,2048]{1,0:T(8,128)}, bf16[4,108,512]{2,1,0:T(8,128)(2,1)}, bf16[2,4,64,864]{3,2,1,0:T(8,128)(2,1)}) custom-call(bf16[128,2048]{1,0:T(8,128)(2,1)} %get-tuple-element.67.refs_0_, bf16[8,128,2048]{2,1,0:T(8,128)(2,1)} %get-tuple-element.68.refs_1_, bf16[2,4,4,64,864]{4,3,2,1,0:T(8,128)(2,1)} %bitcast.14, ...), custom_call_target="tpu_custom_call" | custom-call | tf_op jit(solution)/shard_map/attention_back/pallas_call | solution.py:609
  343.2 95.0 %last.1 = (f32[128,2048]{1,0:T(8,128)}, bf16[8,64,1376]{2,1,0:T(8,128)(2,1)}, bf16[4,108,512]{2,1,0:T(8,128)(2,1)}, bf16[8,64,864]{2,1,0:T(8,128)(2,1)}, f32[8,2048]{1,0:T(8,128)}) custom-call(bf16[1024,1376]{1,0:T(8,128)(2,1)} %get-tuple-element.84.refs_0_, bf16[2048,1408]{1,0:T(8,128)(2,1)} %get-tuple-element.85.refs_1_, ...), custom_call_target="tpu_custom_call" | custom-call | tf_op jit(solution)/shard_map/last/pallas_call | solution.py:609
  438.1 6.7 %finish.1 = (f32[64,2048]{1,0:T(8,128)}, f32[64,2048]{1,0:T(8,128)}, f32[64,3456]{1,0:T(8,128)}, f32[64,3456]{1,0:T(8,128)}, f32[108,2048]{1,0:T(8,128)}, /*inde...) custom-call(bf16[8,64,1376]{2,1,0:T(8,128)(2,1)} %get-tuple-element., ...), custom_call_target="tpu_custom_call" | custom-call | tf_op jit(solution)/shard_map/finish/pallas_call | solution.py:609
